TPU v7x, 32 devices: a whole 2x2x4 slice. The times are simulated.
32 devices in a mesh: dp: 8 (over z, y), head: 4 (over x, core).
Axes of the slice: x: 2, y: 2, z: 4, core: 2. Of those that a mesh axis runs over, the one named last changes fastest.
Arguments:
- node_rows: bfloat16 [4096, 768], P(('dp', 'head')), may hold values from -6 to 6
- output_grad: bfloat16 [4096, 768], P(('dp', 'head')), may hold values from -6 to 6
- weight_in: float32 [4, 768, 768], P(None, 'dp', 'head'), may hold values from -0.21875 to 0.21875
- first_in: float32 [4, 768, 768], P(None, 'dp', 'head'), may hold values from -0.0008544922 to 0.0008544922
- second_in: float32 [4, 768, 768], P(None, 'dp', 'head'), may hold values from 2.6260505e-10 to 1.0504202e-09
- weight_out: float32 [768, 768], P('head', 'dp'), may hold values from -0.875 to 0.875
- first_out: float32 [768, 768], P('head', 'dp'), may hold values from -0.0008544922 to 0.0008544922
- second_out: float32 [768, 768], P('head', 'dp'), may hold values from 2.6260505e-10 to 1.0504202e-09
- weight_down: float32 [768, 768], P('head', 'dp'), may hold values from -0.21875 to 0.21875
- first_down: float32 [768, 768], P('head', 'dp'), may hold values from -0.0008544922 to 0.0008544922
- second_down: float32 [768, 768], P('head', 'dp'), may hold values from 2.6260505e-10 to 1.0504202e-09
- vectors: float32 [9, 768], P(None, ('dp', 'head')), may hold values from -0.9 to 1.9
- first_vectors: float32 [9, 768], P(None, ('dp', 'head')), may hold values from -0.0008544922 to 0.0008544922
- second_vectors: float32 [9, 768], P(None, ('dp', 'head')), may hold values from 2.6260505e-10 to 1.0504202e-09
- bias_table: float32 [8192, 32], P('dp', 'head'), may hold values from -3 to 3
- first_table: float32 [8192, 32], P('dp', 'head'), may hold values from -0.0008544922 to 0.0008544922
- second_table: float32 [8192, 32], P('dp', 'head'), may hold values from 2.6260505e-10 to 1.0504202e-09
- big_counts: int32 [8], P('dp'), may hold values from 1 to 256, 1536 in all
- small_counts: int32 [8, 4], P('dp'), may hold values from 1 to 64, 160 in all within a row
- big_distance: int32 [8, 256, 256], P('dp'), may hold values from 0 to 511
- small_distance: int32 [32, 64, 64], P('dp'), may hold values from 0 to 511
- big_paths: int32 [5, 8, 256, 256], P(None, 'dp'), may hold values from 0 to 1535
- small_paths: int32 [5, 32, 64, 64], P(None, 'dp'), may hold values from 0 to 1535
- big_lengths: int32 [8, 256, 256], P('dp'), may hold values from 1 to 5
- small_lengths: int32 [32, 64, 64], P('dp'), may hold values from 1 to 5
Outputs:
- layer_out: bfloat16 [4096, 768], P(('dp', 'head'))
- input_grad: bfloat16 [4096, 768], P(('dp', 'head'))
- grad_norm: float32 [], replicated
- weight_in_new: float32 [4, 768, 768], P(None, 'dp', 'head')
- first_in_new: float32 [4, 768, 768], P(None, 'dp', 'head')
- second_in_new: float32 [4, 768, 768], P(None, 'dp', 'head')
- weight_out_new: float32 [768, 768], P('head', 'dp')
- first_out_new: float32 [768, 768], P('head', 'dp')
- second_out_new: float32 [768, 768], P('head', 'dp')
- weight_down_new: float32 [768, 768], P('head', 'dp')
- first_down_new: float32 [768, 768], P('head', 'dp')
- second_down_new: float32 [768, 768], P('head', 'dp')
- vectors_new: float32 [9, 768], P(None, ('dp', 'head'))
- first_vectors_new: float32 [9, 768], P(None, ('dp', 'head'))
- second_vectors_new: float32 [9, 768], P(None, ('dp', 'head'))
- bias_table_new: float32 [8192, 32], P('dp', 'head')
- first_table_new: float32 [8192, 32], P('dp', 'head')
- second_table_new: float32 [8192, 32], P('dp', 'head')
Inputs may be any that keep to these rules, and one draw needn't show every extreme that they name: `big_counts`: at least one large bucket in all is full; all counts sum to 3/4 of all large slots. `small_counts`: one small bucket of each index of dp is full.
All inputs are finite; a program needn't handle non-finite values. No bound on the sum of `big_counts` on one device may be relied on, other than what follows from the above.
Results may differ from a plain program's by a relative error of at most 0.015.
Values may be sent and summed in bfloat16 or wider, within the bound.
No kernel may reach another device: no remote copies, remote signals or barrier semaphores. Data moves between devices by JAX's collectives and lax.ppermute only.
A program may use at most 576 MiB of HBM per device.

v0:
```python
import jax
import jax.numpy as jnp
from jax import lax
from jax.sharding import PartitionSpec as P

HEAD_DIM = 24
NDIST = 512
NTYPE = 1536
STEPS = 5
ADAM_STEP = 10
BIGB = 1


NORM_EPSILON = 1e-05
NEGATIVE_FILL = -1e30
BETA_FIRST = 0.9
BETA_SECOND = 0.95
ADAM_EPSILON = 1e-08
RATE_MATRIX = 0.02
RATE_OUTPUT = 0.05
RATE_VECTOR = 0.15
WEIGHT_DECAY = 0.01
CLIP_NORM = 1.0


def cut_along(value, dim, peers):
    before, after = (value.shape[:dim], value.shape[dim + 1 :])
    return jnp.moveaxis(value.reshape(*before, peers, -1, *after), dim, 0)


def sum_at_owner(value, axis, dim):
    tiles = cut_along(value, dim, lax.axis_size(axis))
    arrived = lax.all_to_all(tiles, axis, split_axis=0, concat_axis=0, tiled=True)
    return arrived.astype(jnp.float32).sum(axis=0)


def in_one_piece(arrays, axis, dim, along):
    ends, at = ([], 0)
    for a in arrays[:-1]:
        at += a.shape[along]
        ends.append(at)
    both = jnp.concatenate(arrays, axis=along)
    return tuple(jnp.split(sum_at_owner(both, axis, dim), ends, axis=along))


def norm_rows(values, norm_gain, norm_shift):
    center = values - jnp.mean(values, axis=-1, keepdims=True)
    spread = jnp.mean(center * center, axis=-1, keepdims=True)
    return center * lax.rsqrt(spread + NORM_EPSILON) * norm_gain + norm_shift


def exact_gelu(values):
    return jax.nn.gelu(values, approximate=False)


def hop_index(hop_step, path_block):
    return NDIST + hop_step * NTYPE + path_block[hop_step]


def pair_bias(table_rows, dist_block, path_block, length_block):
    bias_total = jnp.take(table_rows, dist_block, axis=0)
    edge_bias = jnp.zeros_like(bias_total)
    for hop_step in range(STEPS):
        looked = jnp.take(table_rows, hop_index(hop_step, path_block), axis=0)
        edge_bias = edge_bias + jnp.where((length_block > hop_step)[..., None], looked, 0.0)
    bias_total = bias_total + edge_bias / length_block[..., None].astype(jnp.float32)
    return jnp.transpose(bias_total, (0, 3, 1, 2))


def table_grads(score_parts, index_parts, row_total):
    all_ids = []
    all_data = []
    for score_rows, (distance, paths, lengths) in zip(score_parts, index_parts):
        grad_rows = score_rows.astype(jnp.float32)
        flat_lengths = lengths.reshape(-1, 1)
        shared = grad_rows / flat_lengths.astype(jnp.float32)
        all_ids.append(distance.reshape(-1))
        all_data.append(grad_rows)
        for hop_step in range(STEPS):
            all_ids.append(hop_index(hop_step, paths).reshape(-1))
            all_data.append(jnp.where(flat_lengths > hop_step, shared, 0.0))
    return jax.ops.segment_sum(
        jnp.concatenate(all_data, axis=0), jnp.concatenate(all_ids, axis=0), num_segments=row_total
    )


def block_scores(query_block, key_block, count_block, bias_block):
    raw_scores = jnp.einsum(
        "bqhd,bkhd->bhqk", query_block, key_block, preferred_element_type=jnp.float32
    ) * HEAD_DIM ** (-0.5)
    raw_scores = raw_scores + bias_block
    bucket_width = key_block.shape[1]
    key_valid = (
        lax.broadcasted_iota(jnp.int32, (count_block.shape[0], bucket_width), 1)
        < count_block[:, None]
    )
    return jnp.where(key_valid[:, None, None, :], raw_scores, NEGATIVE_FILL)


def forward_block(query_block, key_block, value_block, count_block, bias_block):
    score_block = block_scores(query_block, key_block, count_block, bias_block)
    row_max = jnp.max(score_block, axis=-1, keepdims=True)
    logsum = row_max + jnp.log(jnp.sum(jnp.exp(score_block - row_max), axis=-1, keepdims=True))
    prob_low = jnp.exp(score_block - logsum).astype(jnp.bfloat16)
    mixed_out = jnp.einsum(
        "bhqk,bkhd->bqhd", prob_low, value_block, preferred_element_type=jnp.float32
    )
    return (mixed_out.astype(jnp.bfloat16), logsum[..., 0])


def backward_block(
    query_block, key_block, value_block, grad_block, logsum_block, count_block, bias_block
):
    score_block = block_scores(query_block, key_block, count_block, bias_block)
    prob_block = jnp.exp(score_block - logsum_block[..., None])
    prob_low = prob_block.astype(jnp.bfloat16)
    grad_values = jnp.einsum(
        "bhqk,bqhd->bkhd", prob_low, grad_block, preferred_element_type=jnp.float32
    )
    grad_probs = jnp.einsum(
        "bqhd,bkhd->bhqk", grad_block, value_block, preferred_element_type=jnp.float32
    )
    inner_sum = jnp.sum(prob_block * grad_probs, axis=-1, keepdims=True)
    grad_scores = (prob_block * (grad_probs - inner_sum)).astype(jnp.bfloat16)
    grad_queries = jnp.einsum(
        "bhqk,bkhd->bqhd", grad_scores, key_block, preferred_element_type=jnp.float32
    ) * HEAD_DIM ** (-0.5)
    grad_keys = jnp.einsum(
        "bhqk,bqhd->bkhd", grad_scores, query_block, preferred_element_type=jnp.float32
    ) * HEAD_DIM ** (-0.5)
    return (
        grad_queries.astype(jnp.bfloat16),
        grad_keys.astype(jnp.bfloat16),
        grad_values.astype(jnp.bfloat16),
        jnp.transpose(grad_scores, (0, 2, 3, 1)),
    )


def block_layout(counts, bias_part, per_block):
    count_blocks = counts.reshape(-1, per_block)
    bias_blocks = bias_part.reshape((count_blocks.shape[0], per_block) + bias_part.shape[1:])
    return (count_blocks, bias_blocks)


def head_blocks(tensor, per_block, bucket_width):
    return tensor.reshape(-1, per_block, bucket_width, tensor.shape[1] // HEAD_DIM, HEAD_DIM)


def attend_part(queries, keys, values, layout, per_block):
    bucket_width = layout[1].shape[-1]

    def one_block(block_items):
        return forward_block(*block_items)

    block_items = (
        head_blocks(queries, per_block, bucket_width),
        head_blocks(keys, per_block, bucket_width),
        head_blocks(values, per_block, bucket_width),
    ) + layout
    mixed_out, logsums = lax.map(one_block, block_items)
    return (mixed_out.reshape(queries.shape), logsums)


def attend_back_part(queries, keys, values, grad_heads, logsums, layout, per_block):
    bucket_width = layout[1].shape[-1]
    head_count = layout[1].shape[2]

    def one_block(block_items):
        return backward_block(*block_items)

    block_items = (
        head_blocks(queries, per_block, bucket_width),
        head_blocks(keys, per_block, bucket_width),
        head_blocks(values, per_block, bucket_width),
        head_blocks(grad_heads, per_block, bucket_width),
        logsums,
    ) + layout
    grad_parts = lax.map(one_block, block_items)
    return (
        (
            grad_parts[0].reshape(queries.shape),
            grad_parts[1].reshape(queries.shape),
            grad_parts[2].reshape(queries.shape),
        ),
        grad_parts[3].reshape(-1, head_count),
    )


def place_columns(values, head_index, total_width):
    return lax.dynamic_update_slice_in_dim(
        jnp.zeros((total_width,), jnp.float32), values, head_index * values.shape[0], 0
    )


def adamw_update(weight, first_moment, second_moment, gradient, learn_rate):
    first_new = BETA_FIRST * first_moment + (1.0 - BETA_FIRST) * gradient
    second_new = BETA_SECOND * second_moment + (1.0 - BETA_SECOND) * gradient * gradient
    first_hat = first_new / (1.0 - BETA_FIRST**ADAM_STEP)
    second_hat = second_new / (1.0 - BETA_SECOND**ADAM_STEP)
    weight_new = weight - learn_rate * (
        first_hat / (jnp.sqrt(second_hat) + ADAM_EPSILON) + WEIGHT_DECAY * weight
    )
    return (weight_new, first_new, second_new)


def on_device(
    node_rows,
    output_grad,
    weight_in,
    first_in,
    second_in,
    weight_out,
    first_out,
    second_out,
    weight_down,
    first_down,
    second_down,
    vectors,
    first_vectors,
    second_vectors,
    bias_table,
    first_table,
    second_table,
    big_counts,
    small_counts,
    big_distance,
    small_distance,
    big_paths,
    small_paths,
    big_lengths,
    small_lengths,
):
    proj_in, proj_out, proj_down, table_local = (
        lax.all_gather(weight_in.astype(jnp.bfloat16), "dp", axis=1, tiled=True),
        lax.all_gather(weight_out.astype(jnp.bfloat16), "dp", axis=1, tiled=True),
        lax.all_gather(weight_down.astype(jnp.bfloat16), "dp", axis=1, tiled=True),
        lax.all_gather(bias_table.astype(jnp.bfloat16), "dp", axis=0, tiled=True),
    )
    all_vectors = lax.all_gather(vectors, ("dp", "head"), axis=1, tiled=True)
    head_index = lax.axis_index("head")
    head_width = proj_in.shape[2]
    model_width = proj_in.shape[1]
    bias_query = lax.dynamic_slice_in_dim(all_vectors[4], head_index * head_width, head_width)
    bias_value = lax.dynamic_slice_in_dim(all_vectors[5], head_index * head_width, head_width)
    bias_hidden = lax.dynamic_slice_in_dim(all_vectors[7], head_index * head_width, head_width)
    table_rows = table_local.astype(jnp.float32)
    big_bias = pair_bias(table_rows, big_distance, big_paths, big_lengths)
    small_bias = pair_bias(table_rows, small_distance, small_paths, small_lengths)
    big_layout = block_layout(big_counts, big_bias, BIGB)
    small_layout = block_layout(small_counts.reshape(-1), small_bias, 4)
    big_rows = big_distance.shape[0] * big_distance.shape[1]
    inputs = node_rows.astype(jnp.float32)
    normed_one, pull_one = jax.vjp(norm_rows, inputs, all_vectors[0], all_vectors[1])
    gathered_one = lax.all_gather(normed_one.astype(jnp.bfloat16), "head", axis=0, tiled=True)
    projected = jnp.einsum(
        "rd,kdc->krc", gathered_one, proj_in[:3], preferred_element_type=jnp.float32
    )
    queries = (projected[0] + bias_query).astype(jnp.bfloat16)
    keys_all = projected[1].astype(jnp.bfloat16)
    values_all = (projected[2] + bias_value).astype(jnp.bfloat16)
    big_out, big_logsum = attend_part(
        queries[:big_rows], keys_all[:big_rows], values_all[:big_rows], big_layout, BIGB
    )
    small_out, small_logsum = attend_part(
        queries[big_rows:], keys_all[big_rows:], values_all[big_rows:], small_layout, 4
    )
    attn_heads = jnp.concatenate([big_out, small_out], axis=0)
    attn_share = lax.psum_scatter(
        jnp.dot(attn_heads, proj_out, preferred_element_type=jnp.float32).astype(jnp.bfloat16),
        "head",
        scatter_dimension=0,
        tiled=True,
    ).astype(jnp.float32)
    hidden = inputs + attn_share + all_vectors[6]
    normed_two, pull_two = jax.vjp(norm_rows, hidden, all_vectors[2], all_vectors[3])
    normed_low = normed_two.astype(jnp.bfloat16)
    grad_final = output_grad.astype(jnp.float32)
    gathered_two = lax.all_gather(normed_low, "head", axis=0, tiled=True)
    pre_act = jnp.dot(gathered_two, proj_in[3], preferred_element_type=jnp.float32) + bias_hidden
    activation, pull_gelu = jax.vjp(exact_gelu, pre_act)
    activ_low = activation.astype(jnp.bfloat16)
    ffn_share = lax.psum_scatter(
        jnp.dot(activ_low, proj_down, preferred_element_type=jnp.float32).astype(jnp.bfloat16),
        "head",
        scatter_dimension=0,
        tiled=True,
    ).astype(jnp.float32)
    layer_out = (hidden + ffn_share + all_vectors[8]).astype(jnp.bfloat16)
    gathered_grad = lax.all_gather(output_grad, "head", axis=0, tiled=True)
    grad_activ = jnp.einsum(
        "rd,cd->rc", gathered_grad, proj_down, preferred_element_type=jnp.float32
    )
    grad_pre = pull_gelu(grad_activ)[0].astype(jnp.bfloat16)
    grad_ffn_in = jnp.einsum(
        "rd,rc->dc", gathered_two, grad_pre, preferred_element_type=jnp.float32
    )
    grad_down = jnp.einsum(
        "rc,rd->cd", activ_low, gathered_grad, preferred_element_type=jnp.float32
    )
    grad_hidden_bias = place_columns(
        jnp.sum(grad_pre.astype(jnp.float32), axis=0), head_index, model_width
    )
    grad_normed_two = lax.psum_scatter(
        jnp.einsum("rc,dc->rd", grad_pre, proj_in[3], preferred_element_type=jnp.float32).astype(
            jnp.bfloat16
        ),
        "head",
        scatter_dimension=0,
        tiled=True,
    ).astype(jnp.float32)
    grad_hidden_norm, grad_gain_two, grad_shift_two = pull_two(grad_normed_two)
    grad_hidden = grad_final + grad_hidden_norm
    grad_hidden_low = grad_hidden.astype(jnp.bfloat16)
    gathered_hidden = lax.all_gather(grad_hidden_low, "head", axis=0, tiled=True)
    grad_heads = jnp.einsum(
        "rd,cd->rc", gathered_hidden, proj_out, preferred_element_type=jnp.float32
    ).astype(jnp.bfloat16)
    grad_proj_out = jnp.einsum(
        "rc,rd->cd", attn_heads, gathered_hidden, preferred_element_type=jnp.float32
    )
    big_grads, big_score_rows = attend_back_part(
        queries[:big_rows],
        keys_all[:big_rows],
        values_all[:big_rows],
        grad_heads[:big_rows],
        big_logsum,
        big_layout,
        BIGB,
    )
    small_grads, small_score_rows = attend_back_part(
        queries[big_rows:],
        keys_all[big_rows:],
        values_all[big_rows:],
        grad_heads[big_rows:],
        small_logsum,
        small_layout,
        4,
    )
    table_grad = table_grads(
        (big_score_rows, small_score_rows),
        ((big_distance, big_paths, big_lengths), (small_distance, small_paths, small_lengths)),
        table_rows.shape[0],
    )
    stacked = jnp.stack(
        [
            jnp.concatenate([big_grads[0], small_grads[0]], axis=0),
            jnp.concatenate([big_grads[1], small_grads[1]], axis=0),
            jnp.concatenate([big_grads[2], small_grads[2]], axis=0),
        ]
    )
    grad_proj_qkv = jnp.einsum(
        "rd,krc->kdc", gathered_one, stacked, preferred_element_type=jnp.float32
    )
    grad_normed_one = lax.psum_scatter(
        jnp.einsum("krc,kdc->rd", stacked, proj_in[:3], preferred_element_type=jnp.float32).astype(
            jnp.bfloat16
        ),
        "head",
        scatter_dimension=0,
        tiled=True,
    ).astype(jnp.float32)
    grad_inputs_norm, grad_gain_one, grad_shift_one = pull_one(grad_normed_one)
    input_grad = (grad_hidden + grad_inputs_norm).astype(jnp.bfloat16)
    grad_proj_in = jnp.concatenate([grad_proj_qkv, grad_ffn_in[None]], axis=0)
    shard_in, shard_out, shard_down, shard_table = (
        sum_at_owner(grad_proj_in.astype(jnp.bfloat16), "dp", 1),
        *in_one_piece(
            (grad_proj_out.astype(jnp.bfloat16), grad_down.astype(jnp.bfloat16)), "dp", 1, 0
        ),
        sum_at_owner(table_grad.astype(jnp.bfloat16), "dp", 0),
    )
    column_sums = jnp.sum(stacked.astype(jnp.float32), axis=1)
    vector_terms = jnp.stack(
        [
            grad_gain_one,
            grad_shift_one,
            grad_gain_two,
            grad_shift_two,
            place_columns(column_sums[0], head_index, model_width),
            place_columns(column_sums[2], head_index, model_width),
            jnp.sum(grad_hidden, axis=0),
            grad_hidden_bias,
            jnp.sum(grad_final, axis=0),
        ]
    )
    square_part = (
        jnp.sum(shard_in * shard_in)
        + jnp.sum(shard_out * shard_out)
        + jnp.sum(shard_down * shard_down)
        + jnp.sum(shard_table * shard_table)
    )
    vector_sum, square_sum = lax.psum((vector_terms, square_part), ("dp", "head"))
    grad_norm = jnp.sqrt(square_sum + jnp.sum(vector_sum * vector_sum))
    clip_factor = CLIP_NORM / jnp.maximum(grad_norm, CLIP_NORM)
    shard_width = vectors.shape[1]
    flat_index = lax.axis_index("dp") * lax.axis_size("head") + head_index
    shard_vectors = lax.dynamic_slice_in_dim(vector_sum, flat_index * shard_width, shard_width, 1)
    new_in = adamw_update(weight_in, first_in, second_in, shard_in * clip_factor, RATE_MATRIX)
    new_out = adamw_update(weight_out, first_out, second_out, shard_out * clip_factor, RATE_OUTPUT)
    new_down = adamw_update(
        weight_down, first_down, second_down, shard_down * clip_factor, RATE_MATRIX
    )
    new_vectors = adamw_update(
        vectors, first_vectors, second_vectors, shard_vectors * clip_factor, RATE_VECTOR
    )
    new_table = adamw_update(
        bias_table, first_table, second_table, shard_table * clip_factor, RATE_VECTOR
    )
    return (
        layer_out,
        input_grad,
        grad_norm,
        new_in[0],
        new_in[1],
        new_in[2],
        new_out[0],
        new_out[1],
        new_out[2],
        new_down[0],
        new_down[1],
        new_down[2],
        new_vectors[0],
        new_vectors[1],
        new_vectors[2],
        new_table[0],
        new_table[1],
        new_table[2],
    )


def solution(mesh):
    return jax.shard_map(
        on_device,
        mesh=mesh,
        in_specs=(
            P(("dp", "head"), None),
            P(("dp", "head"), None),
            P(None, "dp", "head"),
            P(None, "dp", "head"),
            P(None, "dp", "head"),
            P("head", "dp"),
            P("head", "dp"),
            P("head", "dp"),
            P("head", "dp"),
            P("head", "dp"),
            P("head", "dp"),
            P(None, ("dp", "head")),
            P(None, ("dp", "head")),
            P(None, ("dp", "head")),
            P("dp", "head"),
            P("dp", "head"),
            P("dp", "head"),
            P("dp"),
            P("dp", None),
            P("dp", None, None),
            P("dp", None, None),
            P(None, "dp", None, None),
            P(None, "dp", None, None),
            P("dp", None, None),
            P("dp", None, None),
        ),
        out_specs=(
            P(("dp", "head"), None),
            P(("dp", "head"), None),
            P(),
            P(None, "dp", "head"),
            P(None, "dp", "head"),
            P(None, "dp", "head"),
            P("head", "dp"),
            P("head", "dp"),
            P("head", "dp"),
            P("head", "dp"),
            P("head", "dp"),
            P("head", "dp"),
            P(None, ("dp", "head")),
            P(None, ("dp", "head")),
            P(None, ("dp", "head")),
            P("dp", "head"),
            P("dp", "head"),
            P("dp", "head"),
        ),
        check_vma=False,
    )
```

profile of v0, /device:TPU:0, one launch (start us, length us, event | category | flops | bytes accessed | tf_op | source)
XLA Modules:
  0.0 5054.3 jit_solution(6134245099639764305)
XLA Ops:
  21.2 44.5 all-gather
  67.6 33.2 all_gather.31
  126.9 33.2 all_gather.33
  163.0 31.0 all_gather.30
  196.4 56.9 %gather_fusion.11 = f32[16384,8]{1,0:T(8,128)} fusion(f32[8192,8]{1,0:T(8,128)} %copy.473, s32[16384]{0:T(1024)S(1)} %broadcast_clamp_fusion.6), kind=kCustom, calls=%fused_computation.11.clone | custom fusion | bytes 1114112 | tf_op jit(solution)/shard_map/jit(_take)/gather | solution.py:64
  262.2 56.9 %gather_fusion.10 = f32[16384,8]{1,0:T(8,128)} fusion(f32[8192,8]{1,0:T(8,128)} %copy.473, s32[16384]{0:T(1024)S(1)} %broadcast_clamp_fusion.7), kind=kCustom, calls=%fused_computation.10.clone | custom fusion | bytes 1114112 | tf_op jit(solution)/shard_map/jit(_take)/gather | solution.py:64
  328.1 56.9 %gather_fusion.9 = f32[16384,8]{1,0:T(8,128)} fusion(f32[8192,8]{1,0:T(8,128)} %copy.473, s32[16384]{0:T(1024)S(1)} %broadcast_clamp_fusion.8), kind=kCustom, calls=%fused_computation.9.clone | custom fusion | bytes 1114112 | tf_op jit(solution)/shard_map/jit(_take)/gather | solution.py:64
  393.9 56.9 %gather_fusion.8 = f32[16384,8]{1,0:T(8,128)} fusion(f32[8192,8]{1,0:T(8,128)} %copy.473, s32[16384]{0:T(1024)S(1)} %broadcast_clamp_fusion.9), kind=kCustom, calls=%fused_computation.8.clone | custom fusion | bytes 1114112 | tf_op jit(solution)/shard_map/jit(_take)/gather | solution.py:64
  459.8 56.9 %gather_fusion.7 = f32[16384,8]{1,0:T(8,128)} fusion(f32[8192,8]{1,0:T(8,128)} %copy.473, s32[16384]{0:T(1024)S(1)} %broadcast_clamp_fusion.10), kind=kCustom, calls=%fused_computation.7.clone | custom fusion | bytes 1114112 | tf_op jit(solution)/shard_map/jit(_take)/gather | solution.py:64
  525.6 56.9 %gather_fusion.6 = f32[16384,8]{1,0:T(8,128)} fusion(f32[8192,8]{1,0:T(8,128)} %copy.473, s32[16384]{0:T(1024)S(1)} %broadcast_clamp_fusion.11), kind=kCustom, calls=%fused_computation.1.clone | custom fusion | bytes 1114112 | tf_op jit(solution)/shard_map/jit(_take)/gather | solution.py:61
  591.5 219.3 %gather_fusion.5 = f32[65536,8]{1,0:T(8,128)} fusion(f32[8192,8]{1,0:T(8,128)} %copy.473, s32[65536]{0:T(1024)S(1)} %broadcast_clamp_fusion), kind=kCustom, calls=%fused_computation.6.clone | custom fusion | bytes 4456448 | tf_op jit(solution)/shard_map/jit(_take)/gather | solution.py:64
  810.8 19.6 copy.500
  832.0 219.3 %gather_fusion.4 = f32[65536,8]{1,0:T(8,128)} fusion(f32[8192,8]{1,0:T(8,128)} %copy.473, s32[65536]{0:T(1024)S(1)} %copy-done.52), kind=kCustom, calls=%fused_computation.5.clone | custom fusion | bytes 4456448 | tf_op jit(solution)/shard_map/jit(_take)/gather | solution.py:64
  1051.3 19.6 copy.495
  1072.4 219.3 %gather_fusion.3 = f32[65536,8]{1,0:T(8,128)} fusion(f32[8192,8]{1,0:T(8,128)} %copy.473, s32[65536]{0:T(1024)S(1)} %copy-done.51), kind=kCustom, calls=%fused_computation.4.clone | custom fusion | bytes 4456448 | tf_op jit(solution)/shard_map/jit(_take)/gather | solution.py:64
  1291.7 19.8 copy.490
  1313.1 219.3 %gather_fusion.2 = f32[65536,8]{1,0:T(8,128)} fusion(f32[8192,8]{1,0:T(8,128)} %copy.473, s32[65536]{0:T(1024)S(1)} %copy-done.50), kind=kCustom, calls=%fused_computation.3.clone | custom fusion | bytes 4456448 | tf_op jit(solution)/shard_map/jit(_take)/gather | solution.py:64
  1532.3 19.6 copy.485
  1553.5 219.3 %gather_fusion.1 = f32[65536,8]{1,0:T(8,128)} fusion(f32[8192,8]{1,0:T(8,128)} %copy.473, s32[65536]{0:T(1024)S(1)} %copy-done.49), kind=kCustom, calls=%fused_computation.2.clone | custom fusion | bytes 4456448 | tf_op jit(solution)/shard_map/jit(_take)/gather | solution.py:64
  1793.9 219.3 %gather_fusion = f32[65536,8]{1,0:T(8,128)} fusion(f32[8192,8]{1,0:T(8,128)} %copy.473, s32[65536]{0:T(1024)S(1)} %copy-done.48), kind=kCustom, calls=%fused_computation.clone | custom fusion | bytes 4456448 | tf_op jit(solution)/shard_map/jit(_take)/gather | solution.py:61
  2013.2 19.7 copy.475
  2205.0 107.5 %copy.561 = f32[491520,8]{1,0:T(8,128)} copy(f32[491520,8]{0,1:T(8,128)} %select_dynamic-update-slice_fusion.5) | data formatting | bytes 31457280 | tf_op jit(solution)/shard_map/concatenate | solution.py:83
  2312.5 2600.8 %scatter_custom_fusion = f32[8192,8]{1,0:T(8,128)} fusion(s32[491520]{0:T(1024)} %constant_dynamic-update-slice_fusion.3, f32[491520,8]{1,0:T(8,128)} %copy.561, f32[]{:T(128)} %constant.93.clone.1), kind=kCustom, calls=%fused_computation.33 | custom fusion | flops 3932160 | bytes 262656 | tf_op jit(solution)/shard_map/scatter-add | solution.py:82
  4996.4 37.6 all-reduce
  (622 shorter events, 389.5 us)
Async XLA Ops:
  7.2 2030.0 %all-gather.3.cloned.1.call-start = ((), (), s32[]{:S(2)}) async-start(), calls=%async_computation.7 | async-start | bytes 1769472 | tf_op jit(solution)/shard_map/all_gather | solution.py:234
  9.4 2068.5 %reduce-scatter.5.cloned.1.call-start = ((), (), s32[]{:S(2)}) async-start(), calls=%async_computation.8 | async-start | bytes 983040 | tf_op jit(solution)/shard_map/reduce_scatter | solution.py:268
  12.3 96.8 %copy-start.35 = (f32[4,64,64]{2,1,0:T(8,128)}, f32[4,64,64]{2,1,0:T(8,128)S(1)}, u32[]{:S(2)}) copy-start(f32[4,64,64]{2,1,0:T(8,128)S(1)} %convert_element_type.261) | copy-start | bytes 196612
  19.5 81.3 %copy-start = (bf16[128,768]{1,0:T(8,128)(2,1)S(1)}, bf16[128,768]{1,0:T(8,128)(2,1)}, u32[]{:S(2)}) copy-start(bf16[128,768]{1,0:T(8,128)(2,1)} %param.29) | copy-start | bytes 589828
  20.5 89.4 %copy-start.118 = (f32[1024,8]{0,1:T(8,128)S(1)}, f32[1024,8]{0,1:T(8,128)}, u32[]{:S(2)}) copy-start(f32[1024,8]{0,1:T(8,128)} %param.43) | copy-start | bytes 98308
  20.5 89.4 %copy-start.84 = (s32[4,64,64]{2,1,0:T(8,128)S(1)}, s32[4,64,64]{2,1,0:T(8,128)}, u32[]{:S(2)}) copy-start(s32[4,64,64]{2,1,0:T(8,128)} %get-tuple-element.265) | copy-start | bytes 196612
  21.2 88.8 %copy-start.83 = (s32[4,64,64]{2,1,0:T(8,128)S(1)}, s32[4,64,64]{2,1,0:T(8,128)}, u32[]{:S(2)}) copy-start(s32[4,64,64]{2,1,0:T(8,128)} %get-tuple-element.266) | copy-start | bytes 196612
  65.7 44.4 copy-start.82
  65.8 44.5 copy-start.81
  66.5 43.3 copy-start.126
  67.5 42.9 copy-start.55
  126.8 69.6 %copy-start.57 = (f32[192,96]{0,1:T(8,128)}, f32[192,96]{0,1:T(8,128)S(1)}, u32[]{:S(2)}) copy-start(f32[192,96]{0,1:T(8,128)S(1)} %copy.540) | copy-start | bytes 221188
  2057.1 85.2 %reduce-scatter.9.cloned.1.call-start = ((), (), s32[]{:S(2)}) async-start(), calls=%async_computation.10 | async-start | bytes 983040 | tf_op jit(solution)/shard_map/reduce_scatter | solution.py:303
  2063.7 26.9 copy-start.157
  2095.6 51.9 %reduce-scatter.7.cloned.1.call-start = ((), (), s32[]{:S(2)}) async-start(), calls=%async_computation.9 | async-start | bytes 983040 | tf_op jit(solution)/shard_map/reduce_scatter | solution.py:282
  4919.6 13.3 all-to-all-start.2
  4932.8 18.6 all-to-all-start.1
  4936.4 34.2 reduce-scatter.11.cloned.1.call-start
  4951.4 40.4 all-to-all-start
  4969.8 25.6 copy-start.18
  4969.8 25.6 copy-start.127
  4969.8 25.6 copy-start.147
  4969.8 25.7 copy-start.155
  4970.6 24.9 copy-start.27
  (151 other events, 1268.0 us)
Sparse Core Ops, SparseCore 0:
  10.8 47.0 all-gather.2
  2057.2 20.6 reduce-scatter.4
  2095.8 23.6 reduce-scatter.8
  2121.8 23.2 reduce-scatter.6
  4939.6 23.9 reduce-scatter.10
where the time goes:
time: 5070 us; the launch traced here: 5050 us
  other arithmetic  2670 us (53%)
  local copies, waits for them, and re-layouts  2060 us (41%)
  blocking collectives  214 us (4%)
    scatter-add x1, other arithmetic, table_grads(): jax.ops.segment_sum(jnp.concatenate(all_data, axis=0), jnp.concatenate(al...  2600 us
    gather x20, local copies, waits for them, and re-layouts, pair_bias(): looked = jnp.take(table_rows, hop_index(hop_step, path_block), axis=0)  1520 us
    gather x4, local copies, waits for them, and re-layouts, pair_bias(): bias_total = jnp.take(table_rows, dist_block, axis=0)  303 us
    concatenate x1, local copies, waits for them, and re-layouts, table_grads(): jnp.concatenate(all_data, axis=0)  108 us
  transfers between devices with their start and end apart: 8, of which 4 were waited for; matrix products, arithmetic and copies ran while one was open for 39% of the time, Pallas kernels for 0%

commit v1 on v0

v1 whole, which is shorter than its diff:
```python
import jax
import jax.numpy as jnp
from jax import lax
from jax.experimental import pallas as pl
from jax.experimental.pallas import tpu as pltpu
from jax.sharding import PartitionSpec as P

HEAD_DIM = 24
NDIST = 512
NTYPE = 1536
STEPS = 5
ADAM_STEP = 10

NORM_EPSILON = 1e-05
NEGATIVE_FILL = -1e30
BETA_FIRST = 0.9
BETA_SECOND = 0.95
ADAM_EPSILON = 1e-08
RATE_MATRIX = 0.02
RATE_OUTPUT = 0.05
RATE_VECTOR = 0.15
WEIGHT_DECAY = 0.01
CLIP_NORM = 1.0

LANES = 128
SUB = 8
FIRST = [0] + [(NDIST + n * NTYPE) // LANES for n in range(STEPS)]
CHUNKS = [NDIST // LANES] + [NTYPE // LANES] * STEPS
LOOKUPS = STEPS + 1
SCALE = HEAD_DIM**-0.5
BF = jnp.bfloat16
F32 = jnp.float32
VMEM_BYTES = 48 << 20

NN = (((1,), (0,)), ((), ()))
NT = (((1,), (1,)), ((), ()))
TN = (((0,), (0,)), ((), ()))


def dot(left, right, dims):
    return lax.dot_general(left, right, dims, preferred_element_type=F32)


def kernel_call(body, outs, name, flops, nbytes, n_in=0, in_specs=None):
    return pl.pallas_call(
        body,
        out_shape=outs,
        in_specs=in_specs or [pl.BlockSpec(memory_space=pltpu.VMEM)] * n_in,
        name=name,
        compiler_params=pltpu.CompilerParams(vmem_limit_bytes=VMEM_BYTES),
        cost_estimate=pl.CostEstimate(flops=flops, bytes_accessed=nbytes, transcendentals=0),
    )


def pair_block(big, small, block, half, is_small):
    distance, paths, lengths = small if is_small else big
    rows = pl.ds(SUB * block, SUB)
    if is_small:

        def two(ref, *lead):
            return jnp.concatenate([ref[(*lead, 2 * half, rows)], ref[(*lead, 2 * half + 1, rows)]], axis=1)

        index = [two(distance)] + [two(paths, n) for n in range(STEPS)]
        return index, two(lengths)
    lanes = slice(LANES * half, LANES * half + LANES)
    index = [distance[0, rows, lanes]] + [paths[n, 0, rows, lanes] for n in range(STEPS)]
    return index, lengths[0, rows, lanes]


def each_block(big, small, step):
    width, narrow = big[0].shape[1], small[0].shape[1]
    halves, pairs = width // LANES, small[0].shape[0] // 2

    def big_step(block, carry):
        for half in range(halves):
            index, lengths = pair_block(big, small, block, half, False)
            step(index, lengths, (half * width + SUB * block) * SUB)
        return carry

    lax.fori_loop(0, width // SUB, big_step, 0)

    def small_step(block, carry):
        for pair in range(pairs):
            index, lengths = pair_block(big, small, block, pair, True)
            step(index, lengths, (halves * width + pair * narrow + SUB * block) * SUB)
        return carry

    lax.fori_loop(0, narrow // SUB, small_step, 0)


def hop_weights(lengths):
    inverse = 1.0 / lengths.astype(F32)
    return [None] + [jnp.where(lengths > n, inverse, 0.0) for n in range(STEPS)]


def pick(items, high):
    bit = 1
    while len(items) > 1:
        odd = (high & bit) != 0
        items = [
            jnp.where(odd, items[k + 1], items[k]) if k + 1 < len(items) else items[k]
            for k in range(0, len(items), 2)
        ]
        bit *= 2
    return items[0]


def bias_body(table, bd, bp, bl, sd, sp, sl, out):
    def step(index, lengths, base):
        weights = hop_weights(lengths)
        total = [None] * SUB
        for t in range(LOOKUPS):
            chunks = [table[SUB * (FIRST[t] + k) : SUB * (FIRST[t] + k + 1), :] for k in range(CHUNKS[t])]
            low, high = index[t] & (LANES - 1), index[t] >> 7
            for s in range(SUB):
                low_row = jnp.broadcast_to(low[s : s + 1], (SUB, LANES))
                high_row = jnp.broadcast_to(high[s : s + 1], (SUB, LANES))
                found = [
                    jnp.take_along_axis(c, low_row, axis=1, mode="promise_in_bounds") for c in chunks
                ]
                value = pick(found, high_row)
                if t > 0:
                    value = value * jnp.broadcast_to(weights[t][s : s + 1], (SUB, LANES))
                total[s] = value if total[s] is None else total[s] + value
        for s in range(SUB):
            out[pl.ds(base + SUB * s, SUB), :] = total[s]

    each_block((bd, bp, bl), (sd, sp, sl), step)


def scatter_body(grads, bd, bp, bl, sd, sp, sl, out):
    out[...] = jnp.zeros_like(out)
    sub = lax.broadcasted_iota(jnp.int32, (2 * SUB, LANES), 0)
    low_pattern = [(sub + 2 * SUB * k).astype(F32).astype(BF) for k in range(LANES // (2 * SUB))]
    upper = (sub >= SUB).astype(jnp.int32)
    high_pattern = [(2 * k + upper).astype(F32).astype(BF) for k in range(max(CHUNKS) // 2)]
    zero = jnp.zeros((2 * SUB, LANES), BF)

    def wide(row):
        return jnp.broadcast_to(row, (2 * SUB, LANES)).astype(BF)

    def step(index, lengths, base):
        weights = hop_weights(lengths)
        twice = []
        for s in range(SUB):
            g = grads[pl.ds(base + SUB * s, SUB), :]
            twice.append(jnp.concatenate([g, g], axis=0).astype(BF))
        for t in range(LOOKUPS):
            low, high = (index[t] & (LANES - 1)).astype(F32), (index[t] >> 7).astype(F32)
            left, right = [], []
            for s in range(SUB):
                low_row, high_row = wide(low[s : s + 1]), wide(high[s : s + 1])
                one = wide(weights[t][s : s + 1]) if t > 0 else jnp.ones((2 * SUB, LANES), BF)
                right.append(jnp.concatenate([jnp.where(low_row == p, one, zero) for p in low_pattern], axis=0))
                left.append(
                    jnp.concatenate(
                        [jnp.where(high_row == p, twice[s], zero) for p in high_pattern[: CHUNKS[t] // 2]],
                        axis=0,
                    )
                )
            part = dot(jnp.concatenate(left, axis=1), jnp.concatenate(right, axis=1), NT)
            out[SUB * FIRST[t] : SUB * (FIRST[t] + CHUNKS[t]), :] += part

    each_block((bd, bp, bl), (sd, sp, sl), step)


def norm_parts(values):
    center = values - jnp.mean(values, axis=-1, keepdims=True)
    spread = lax.rsqrt(jnp.mean(center * center, axis=-1, keepdims=True) + NORM_EPSILON)
    return center * spread, spread


def norm_back(scaled, xhat, spread):
    return spread * (
        scaled
        - jnp.mean(scaled, axis=-1, keepdims=True)
        - xhat * jnp.mean(scaled * xhat, axis=-1, keepdims=True)
    )


def head_lanes(head, width):
    lane = lax.broadcasted_iota(jnp.int32, (1, width), 1)
    return (lane >= head * HEAD_DIM) & (lane < (head + 1) * HEAD_DIM)


def forward_body(
    rows, gains, biases, weights, bias, big_counts, small_counts, normed, q, k, v, mixed, big_probs, small_probs
):
    width = big_probs.shape[1]
    narrow = (rows.shape[0] - width) // small_counts.shape[1]
    wide = 2 * narrow
    pairs = small_counts.shape[1] // 2
    columns = q.shape[1]
    heads = columns // HEAD_DIM
    halves = width // LANES
    xhat, _ = norm_parts(rows[...].astype(F32))
    normed[...] = (xhat * gains[0:1, :] + gains[1:2, :]).astype(BF)
    q[...] = (dot(normed[...], weights[0], NN) + biases[0:1, :]).astype(BF)
    k[...] = dot(normed[...], weights[1], NN).astype(BF)
    v[...] = (dot(normed[...], weights[2], NN) + biases[1:2, :]).astype(BF)
    mixed[...] = jnp.zeros_like(mixed)
    key = lax.broadcasted_iota(jnp.int32, (1, width), 1)
    big_live = key < big_counts[0]
    small_live = []
    for pair in range(pairs):
        row = lax.broadcasted_iota(jnp.int32, (wide, wide), 0)
        lane = lax.broadcasted_iota(jnp.int32, (wide, wide), 1)
        first = (row < narrow) & (lane < small_counts[0, 2 * pair])
        second = (row >= narrow) & (lane >= narrow) & (lane < narrow + small_counts[0, 2 * pair + 1])
        small_live.append(first | second)

    def attend(span, scores, live, mine):
        scores = jnp.where(live, scores, NEGATIVE_FILL)
        power = jnp.exp(scores - jnp.max(scores, axis=-1, keepdims=True))
        probs = power * (1.0 / jnp.sum(power, axis=-1, keepdims=True))
        out = dot(probs.astype(BF), v[span, :], NN)
        mixed[span, :] = jnp.where(mine, out.astype(BF), mixed[span, :])
        return probs

    def one_head(head, carry):
        mine = head_lanes(head, columns)
        span = slice(0, width)
        query = jnp.where(mine, q[span, :], 0.0)
        extra = jnp.concatenate(
            [bias[pl.ds(half * width * SUB + head, width, stride=SUB), :] for half in range(halves)], axis=1
        )
        scores = dot(query, k[span, :], NT) * SCALE + extra
        big_probs[head] = attend(span, scores, big_live, mine)
        for pair in range(pairs):
            span = slice(width + pair * wide, width + (pair + 1) * wide)
            query = jnp.where(mine, q[span, :], 0.0)
            at = (halves * width + pair * narrow) * SUB
            extra = bias[pl.ds(at + head, narrow, stride=SUB), :]
            scores = dot(query, k[span, :], NT) * SCALE + jnp.concatenate([extra, extra], axis=0)
            small_probs[head, pair] = attend(span, scores, small_live[pair], mine)
        return carry

    lax.fori_loop(0, heads, one_head, 0)


def backward_body(grad_heads, q, k, v, big_probs, small_probs, dq, dk, dv, score_rows):
    heads, width = big_probs.shape[:2]
    pairs, wide = small_probs.shape[1:3]
    narrow = wide // 2
    columns = q.shape[1]
    halves = width // LANES
    for ref in (dq, dk, dv):
        ref[...] = jnp.zeros_like(ref)

    def attend(span, probs, mine):
        upper = jnp.where(mine, grad_heads[span, :], 0.0)
        grad_probs = dot(upper, v[span, :], NT)
        inner = jnp.sum(probs * grad_probs, axis=-1, keepdims=True)
        grad_scores = (probs * (grad_probs - inner)).astype(BF)
        dv[span, :] = jnp.where(mine, dot(probs.astype(BF), upper, TN).astype(BF), dv[span, :])
        dq[span, :] = jnp.where(mine, (dot(grad_scores, k[span, :], NN) * SCALE).astype(BF), dq[span, :])
        dk[span, :] = jnp.where(mine, (dot(grad_scores, q[span, :], TN) * SCALE).astype(BF), dk[span, :])
        return grad_scores.astype(F32)

    def one_head(head, carry):
        mine = head_lanes(head, columns)
        span = slice(0, width)
        grad_scores = attend(span, big_probs[head], mine)
        for half in range(halves):
            score_rows[pl.ds(half * width * SUB + head, width, stride=SUB), :] = grad_scores[
                :, LANES * half : LANES * (half + 1)
            ]
        for pair in range(pairs):
            span = slice(width + pair * wide, width + (pair + 1) * wide)
            grad_scores = attend(span, small_probs[head, pair], mine)
            at = (halves * width + pair * narrow) * SUB
            score_rows[pl.ds(at + head, narrow, stride=SUB), :] = grad_scores[:narrow] + grad_scores[narrow:]
        return carry

    lax.fori_loop(0, heads, one_head, 0)


def middle_body(
    heads_in, rows, upper, gains, weights, layer_out, grad_hidden, grad_low, normed_low, grad_heads, act, grad_pre, sums, pre_sums
):
    parts, _, columns = heads_in.shape
    hidden = rows[...].astype(F32) + gains[2:3, :]
    for j in range(parts):
        hidden = hidden + dot(heads_in[j], weights[0, j], NT)
    xhat, spread = norm_parts(hidden)
    low = (xhat * gains[0:1, :] + gains[1:2, :]).astype(BF)
    normed_low[...] = low
    cotangent = upper[...]
    final = hidden + gains[4:5, :]
    grad_normed = jnp.zeros_like(hidden)
    for j in range(parts):
        pre = dot(low, weights[1, j], NN) + gains[3:4, j * columns : (j + 1) * columns]
        phi = 0.5 * (1.0 + lax.erf(pre * (0.5**0.5)))
        active = (pre * phi).astype(BF)
        act[j] = active
        final = final + dot(active, weights[2, j], NT)
        slope = phi + pre * jnp.exp(-0.5 * pre * pre) * (0.5 / jnp.pi) ** 0.5
        grad_j = dot(cotangent, weights[2, j], NN) * slope
        low_j = grad_j.astype(BF)
        grad_pre[j] = low_j
        pre_sums[j : j + 1, :] = jnp.sum(low_j.astype(F32), axis=0, keepdims=True)
        grad_normed = grad_normed + dot(low_j, weights[1, j], NT)
    layer_out[...] = final.astype(BF)
    wide = cotangent.astype(F32)
    grad = wide + norm_back(grad_normed * gains[0:1, :], xhat, spread)
    grad_hidden[...] = grad
    grad_small = grad.astype(BF)
    grad_low[...] = grad_small
    for j in range(parts):
        grad_heads[j] = dot(grad_small, weights[0, j], NN).astype(BF)
    sums[0:1, :] = jnp.sum(grad_normed * xhat, axis=0, keepdims=True)
    sums[1:2, :] = jnp.sum(grad_normed, axis=0, keepdims=True)
    sums[2:3, :] = jnp.sum(grad, axis=0, keepdims=True)
    sums[3:4, :] = jnp.sum(wide, axis=0, keepdims=True)


def adamw_update(weight, first_moment, second_moment, gradient, learn_rate):
    first_new = BETA_FIRST * first_moment + (1.0 - BETA_FIRST) * gradient
    second_new = BETA_SECOND * second_moment + (1.0 - BETA_SECOND) * gradient * gradient
    first_hat = first_new / (1.0 - BETA_FIRST**ADAM_STEP)
    second_hat = second_new / (1.0 - BETA_SECOND**ADAM_STEP)
    weight_new = weight - learn_rate * (
        first_hat / (jnp.sqrt(second_hat) + ADAM_EPSILON) + WEIGHT_DECAY * weight
    )
    return (weight_new, first_new, second_new)


def exchange(value, axis):
    return lax.all_to_all(value, axis, split_axis=0, concat_axis=0, tiled=True)


def spread_all(value, axis):
    size = lax.axis_size(axis)
    return exchange(jnp.broadcast_to(value[None], (size, *value.shape)), axis)


def struct(shape, dtype):
    return jax.ShapeDtypeStruct(shape, dtype)


def on_device(
    node_rows,
    output_grad,
    weight_in,
    first_in,
    second_in,
    weight_out,
    first_out,
    second_out,
    weight_down,
    first_down,
    second_down,
    vectors,
    first_vectors,
    second_vectors,
    bias_table,
    first_table,
    second_table,
    big_counts,
    small_counts,
    big_distance,
    small_distance,
    big_paths,
    small_paths,
    big_lengths,
    small_lengths,
):
    everyone = ("dp", "head")
    n_dp, n_head = lax.axis_size("dp"), lax.axis_size("head")
    head_index = lax.axis_index("head")
    shard_rows, columns = weight_in.shape[1], weight_in.shape[2]
    model = shard_rows * n_dp
    my_rows = node_rows.shape[0]
    group_rows = my_rows * n_head
    heads = columns // HEAD_DIM
    width, narrow = big_distance.shape[1], small_distance.shape[1]
    pairs = small_distance.shape[0] // 2
    pair_rows = width // LANES * width + pairs * narrow
    pair_count = pair_rows * LANES
    table_rows = bias_table.shape[0]
    ints = (big_distance, big_paths, big_lengths, small_distance, small_paths, small_lengths)

    def chunked(table):
        return table.T.reshape(heads, table_rows // LANES, LANES).transpose(1, 0, 2)

    def unchunked(value):
        return value.transpose(1, 0, 2).reshape(heads, table_rows).T

    with jax.named_scope("table_all"):
        table_all = spread_all(chunked(bias_table.astype(BF)), "dp")
    table_all = table_all.reshape(-1, LANES).astype(F32)
    with jax.named_scope("vectors_all"):
        all_vectors = spread_all(vectors, everyone).transpose(1, 0, 2).reshape(vectors.shape[0], -1)
    with jax.named_scope("rows_all"):
        rows_all = spread_all(node_rows, "head").reshape(group_rows, model)
    with jax.named_scope("weights_qkv"):
        weights_qkv = lax.all_gather(weight_in[:3].astype(BF), "dp", axis=1, tiled=True)
    local_rest = jnp.stack([weight_out.astype(BF).T, weight_in[3].astype(BF), weight_down.astype(BF).T])
    with jax.named_scope("weights_rest"):
        weights_rest = lax.all_gather(local_rest, everyone)
    weights_rest = (
        weights_rest.reshape(n_dp, n_head, 3, shard_rows, columns)
        .transpose(2, 1, 0, 3, 4)
        .reshape(3, n_head, model, columns)
    )
    with jax.named_scope("upper_all"):
        upper_all = spread_all(output_grad, "head").reshape(group_rows, model)

    bias = kernel_call(
        bias_body,
        struct((pair_rows * SUB, LANES), F32),
        "pair_bias",
        pair_count * 8 * 60 * 100,
        pair_count * 8 * 8,
        7,
    )(table_all, *ints)

    my_bias = lax.dynamic_slice_in_dim(all_vectors, head_index * columns, columns, 1)
    vmem, smem = pl.BlockSpec(memory_space=pltpu.VMEM), pl.BlockSpec(memory_space=pltpu.SMEM)
    low_half = struct((group_rows, columns), BF)
    normed_one, q, k, v, mixed, big_probs, small_probs = kernel_call(
        forward_body,
        (
            struct((group_rows, model), BF),
            low_half,
            low_half,
            low_half,
            low_half,
            struct((heads, width, width), F32),
            struct((heads, pairs, 2 * narrow, 2 * narrow), F32),
        ),
        "attend_forward",
        6 * group_rows * model * columns,
        10 << 20,
        in_specs=[vmem] * 5 + [smem] * 2,
    )(
        rows_all,
        all_vectors[:2],
        my_bias[4:6],
        weights_qkv,
        bias,
        big_counts,
        small_counts,
    )
    with jax.named_scope("mixed_rows"):
        mixed_rows = exchange(mixed.reshape(n_head, my_rows, columns), "head")

    mine = struct((my_rows, model), BF)
    split = struct((n_head, my_rows, columns), BF)
    gains = jnp.concatenate([all_vectors[2:4], all_vectors[6:9]], axis=0)
    layer_out, grad_hidden, grad_low, normed_two, grad_heads, act, grad_pre, sums, pre_sums = kernel_call(
        middle_body,
        (
            mine,
            struct((my_rows, model), F32),
            mine,
            mine,
            split,
            split,
            split,
            struct((4, model), F32),
            struct((n_head, columns), F32),
        ),
        "feed_forward",
        14 * my_rows * model * model,
        8 << 20,
        5,
    )(mixed_rows, node_rows, output_grad, gains, weights_rest)

    with jax.named_scope("grad_heads"):
        grad_heads = exchange(grad_heads, "head").reshape(group_rows, columns)
    with jax.named_scope("act_pre"):
        act_pre = exchange(jnp.stack([act, grad_pre], axis=1), "head")
    act_all = act_pre[:, 0].reshape(group_rows, columns)
    pre_all = act_pre[:, 1].reshape(group_rows, columns)
    with jax.named_scope("rows_two"):
        rows_two = spread_all(jnp.stack([normed_two, grad_low]), "head")
    normed_all = rows_two[:, 0].reshape(group_rows, model)
    low_all = rows_two[:, 1].reshape(group_rows, model)

    dq, dk, dv, score_rows = kernel_call(
        backward_body,
        (low_half, low_half, low_half, struct((pair_rows * SUB, LANES), F32)),
        "attend_backward",
        heads * pair_count * columns * 8,
        10 << 20,
        6,
    )(grad_heads, q, k, v, big_probs, small_probs)

    def outer(left, right):
        return dot(left, right, TN).astype(BF).reshape(n_dp, shard_rows, columns)

    with jax.named_scope("rest_grads"):
        rest_shards = exchange(
            jnp.stack([outer(low_all, mixed), outer(normed_all, pre_all), outer(upper_all, act_all)], axis=1), "dp"
        )
    with jax.named_scope("qkv_grads"):
        qkv_shards = exchange(
            jnp.stack([outer(normed_one, dq), outer(normed_one, dk), outer(normed_one, dv)], axis=1), "dp"
        )
    partial = (dot(dq, weights_qkv[0], NT) + dot(dk, weights_qkv[1], NT) + dot(dv, weights_qkv[2], NT)).astype(BF)
    with jax.named_scope("grad_normed_one"):
        grad_normed_one = exchange(partial.reshape(n_head, my_rows, model), "head")
    grad_normed_one = jnp.sum(grad_normed_one.astype(F32), axis=0)
    xhat, spread = norm_parts(node_rows.astype(F32))
    input_grad = (grad_hidden + norm_back(grad_normed_one * all_vectors[0], xhat, spread)).astype(BF)

    table_grad = kernel_call(
        scatter_body,
        struct((n_dp * table_rows // LANES * heads, LANES), F32),
        "table_scatter",
        pair_count * 8 * 60 * 100,
        pair_count * 8 * 8,
        7,
    )(score_rows, *ints)
    with jax.named_scope("table_grad"):
        table_shards = exchange(
            table_grad.astype(BF).reshape(n_dp, table_rows // LANES, heads, LANES), "dp"
        )

    def my_columns(values):
        return lax.dynamic_update_slice_in_dim(
            jnp.zeros((1, model), F32), values[None], head_index * columns, 1
        )

    vector_terms = jnp.concatenate(
        [
            jnp.sum(grad_normed_one * xhat, axis=0)[None],
            jnp.sum(grad_normed_one, axis=0)[None],
            sums[0:2],
            my_columns(jnp.sum(dq.astype(F32), axis=0)),
            my_columns(jnp.sum(dv.astype(F32), axis=0)),
            sums[2:3],
            pre_sums.reshape(1, model),
            sums[3:4],
        ]
    )
    with jax.named_scope("vector_grads"):
        vector_shards = exchange(
            vector_terms.reshape(vectors.shape[0], n_dp * n_head, -1).transpose(1, 0, 2), everyone
        )
    shard_vectors = jnp.sum(vector_shards, axis=0)
    shard_rest = jnp.sum(rest_shards.astype(F32), axis=0)
    shard_qkv = jnp.sum(qkv_shards.astype(F32), axis=0)
    shard_table = jnp.sum(table_shards.astype(F32), axis=0)
    square_part = (
        jnp.sum(shard_rest * shard_rest)
        + jnp.sum(shard_qkv * shard_qkv)
        + jnp.sum(shard_vectors * shard_vectors)
        + jnp.sum(shard_table * shard_table)
    )
    with jax.named_scope("squares"):
        squares = spread_all(jnp.broadcast_to(square_part, (LANES,)), everyone)
    grad_norm = jnp.sqrt(jnp.sum(squares[:, 0]))
    clip_factor = CLIP_NORM / jnp.maximum(grad_norm, CLIP_NORM)
    shard_in = jnp.concatenate([shard_qkv, shard_rest[1:2]], axis=0)
    new_in = adamw_update(weight_in, first_in, second_in, shard_in * clip_factor, RATE_MATRIX)
    new_out = adamw_update(weight_out, first_out, second_out, shard_rest[0].T * clip_factor, RATE_OUTPUT)
    new_down = adamw_update(weight_down, first_down, second_down, shard_rest[2].T * clip_factor, RATE_MATRIX)
    new_vectors = adamw_update(
        vectors, first_vectors, second_vectors, shard_vectors * clip_factor, RATE_VECTOR
    )
    new_table = adamw_update(
        bias_table, first_table, second_table, unchunked(shard_table) * clip_factor, RATE_VECTOR
    )
    return (layer_out, input_grad, grad_norm, *new_in, *new_out, *new_down, *new_vectors, *new_table)


def solution(mesh):
    rows = P(("dp", "head"), None)
    square = P(None, "dp", "head")
    across = P("head", "dp")
    thin = P(None, ("dp", "head"))
    table = P("dp", "head")
    return jax.shard_map(
        on_device,
        mesh=mesh,
        in_specs=(rows, rows)
        + (square,) * 3
        + (across,) * 6
        + (thin,) * 3
        + (table,) * 3
        + (P("dp"), P("dp", None))
        + (P("dp", None, None),) * 2
        + (P(None, "dp", None, None),) * 2
        + (P("dp", None, None),) * 2,
        out_specs=(rows, rows, P()) + (square,) * 3 + (across,) * 6 + (thin,) * 3 + (table,) * 3,
        check_vma=False,
    )
```

time: 5070 us -> 432 us (0.09)
  other arithmetic: 2670 us -> 19.4 us
  local copies, waits for them, and re-layouts: 2060 us -> 67.3 us
  blocking collectives: 214 us -> 34.9 us
  Pallas kernels: 0 us -> 129 us
  waiting for transfers between devices: 41.6 us -> 95.5 us
    scatter-add x1 -> x0, other arithmetic: 2600 us -> none  [table_grads(): jax.ops.segment_sum(jnp.concatenate(all_data, axis=0), jnp.concatenate(al...]
    gather x24 -> x0, local copies, waits for them, and re-layouts: 1820 us -> none  [the longest x20 1520 us: pair_bias(): looked = jnp.take(table_rows, hop_index(hop_step, path_block), axis=0)]
    all_gather x8 -> x1, blocking collectives: 176 us -> 34.9 us  [on_device(): lax.all_gather(weight_in[:3].astype(BF), 'dp', axis=1, tiled=True)]
    pallas_call x0 -> x5, Pallas kernels: none -> 129 us  [the longest x1 59.6 us: on_device(): kernel_call(bias_body, struct((pair_rows * SUB, LANES), F32), 'pair_bias'...]
    concatenate x7 -> x9, local copies, waits for them, and re-layouts: 117 us -> 3.69 us  [on_device(): jnp.concatenate([jnp.sum(grad_normed_one * xhat, axis=0)[None], jnp.sum(g...]
    all_to_all x3 -> x14, waiting for transfers between devices: 30.3 us -> 95.5 us  [exchange(): return lax.all_to_all(value, axis, split_axis=0, concat_axis=0, tiled=True)]
  transfers between devices with their start and end apart: 8 -> 15, of which waited for: 4 -> 11; matrix products, arithmetic and copies ran while one was open for 39% -> 11% of each run, Pallas kernels for 0% -> 27%
where the time goes in v1:
time: 432 us; the launch traced here: 430 us
  Pallas kernels  129 us (30%)
  waiting for transfers between devices  95.5 us (22%)
  local copies, waits for them, and re-layouts  67.3 us (16%)
  starting transfers between devices  56.7 us (13%)
  blocking collectives  34.9 us (8%)
  between operations  20.2 us (5%)
  other arithmetic  19.4 us (4%)
  matrix products  6.24 us (1%)
    all_to_all x14, waiting for transfers between devices, exchange(): return lax.all_to_all(value, axis, split_axis=0, concat_axis=0, tiled=True)  95.5 us
    pallas_call x1, Pallas kernels, on_device(): kernel_call(bias_body, struct((pair_rows * SUB, LANES), F32), 'pair_bias'...  59.6 us
    all_to_all x14, starting transfers between devices, exchange(): return lax.all_to_all(value, axis, split_axis=0, concat_axis=0, tiled=True)  56.7 us
    pallas_call x1, Pallas kernels, on_device(): kernel_call(scatter_body, struct((n_dp * table_rows // LANES * heads, LAN...  43.2 us
    unnamed x159, local copies, waits for them, and re-layouts  37.2 us
    all_gather x1, blocking collectives, on_device(): lax.all_gather(weight_in[:3].astype(BF), 'dp', axis=1, tiled=True)  34.9 us
    pallas_call x1, Pallas kernels, on_device(): kernel_call(forward_body, (struct((group_rows, model), BF), low_half, low...  11.3 us
    pallas_call x1, Pallas kernels, on_device(): kernel_call(backward_body, (low_half, low_half, low_half, struct((pair_ro...  9.53 us
  transfers between devices with their start and end apart: 15, of which 11 were waited for; matrix products, arithmetic and copies ran while one was open for 11% of the time, Pallas kernels for 27%

profile of v1, /device:TPU:0, one launch (start us, length us, event | category | flops | bytes accessed | tf_op | source)
XLA Modules:
  0.0 429.7 jit_solution(8524622306609531815)
XLA Ops:
  11.9 7.3 %all-to-all-start.1 = ((f32[32,1,216]{2,1,0:T(1,128)}), f32[32,1,216]{2,1,0:T(1,128)S(1)}, u32[]{:S(2)}, u32[]{:S(2)}) async-start(f32[32,1,216]{2,1,0:T(1,128)} %reshape.178), calls=%async_computation.1 | async-start | bytes 65536 | tf_op jit(solution)/shard_map/vectors_all/all_to_all | solution.py:329
  19.3 34.9 %all_gather.9.weights = bf16[3,768,192]{2,1,0:T(8,128)(2,1)S(1)} all-gather(bf16[3,96,192]{2,1,0:T(8,128)(2,1)S(1)} %slice.100), channel_id=1, replica_groups=mesh['dp'=8,'head'=4] {'dp'}, dimensions={1}, use_global_device_ids=true | all-gather | bytes 995328 | tf_op jit(solution)/shard_map/weights_qkv/all_gather | solution.py:397
  55.6 5.1 %all-to-all-start.2 = ((bf16[8,8,8,128]{3,2,1,0:T(8,128)(2,1)}), bf16[8,8,8,128]{3,2,1,0:T(8,128)(2,1)S(1)}, u32[]{:S(2)}, u32[]{:S(2)}) async-start(bf16[8,8,8,128]{3,2,1,0:T(8,128)(2,1)} %broadcast_in_dim.18), calls=%async_computation.2 | async-start | bytes 262144 | tf_op jit(solution)/shard_map/table_all/all_to_all | solution.py:329
  63.0 5.1 %all-to-all-done.2 = bf16[8,8,8,128]{3,2,1,0:T(8,128)(2,1)S(1)} async-done(((bf16[8,8,8,128]{3,2,1,0:T(8,128)(2,1)}), bf16[8,8,8,128]{3,2,1,0:T(8,128)(2,1)S(1)}, u32[]{:S(2)}, u32[]{:S(2)}) %all-to-all-start.2) | async-done | bytes 131104 | tf_op jit(solution)/shard_map/table_all/all_to_all | solution.py:329
  69.8 3.6 all-to-all-start
  76.7 59.6 %pair_bias.1.bias = f32[5120,128]{1,0:T(8,128)S(1)} custom-call(f32[512,128]{1,0:T(8,128)S(1)} %bitcast_convert_fusion.table, s32[1,256,256]{2,1,0:T(8,128)S(1)} %copy-done.29, s32[5,1,256,256]{3,2,1,0:T(8,128)S(1)} %copy-done.25, s32[1,256,256]{2,1,0:T(8,128)S(1)} %copy-done.31, s32[4,64,64]{2,1,0:T(8,128)S(1)} %copy-done.33, ...), custom_call_target="tpu_custom_call" | custom-call | flops 3932160000 | bytes 5242880 | tf_op jit(solution)/shard_map/pair_bias/pallas_call | solution.py:409
  137.8 11.3 %attend_forward.1 = (bf16[512,768]{1,0:T(8,128)(2,1)S(1)}, bf16[512,192]{1,0:T(8,128)(2,1)S(1)}, bf16[512,192]{1,0:T(8,128)(2,1)S(1)}, bf16[512,192]{1,0:T(8,128...) custom-call(bf16[512,768]{1,0:T(8,128)(2,1)S(1)} %bitcast.126, ...), custom_call_target="tpu_custom_call" | custom-call | flops 452984832 | bytes 10485760 | tf_op jit(solution)/shard_map/attend_forward/pallas_call | solution.py:421
  157.2 3.9 all-to-all-done.3
  161.3 5.0 %copy.149 = bf16[8,4,3,96,192]{4,3,0,1,2:T(8,128)(2,1)} copy(bf16[8,4,3,96,192]{4,3,2,1,0:T(8,128)(2,1)} %bitcast.134) | data formatting | bytes 7077888 | tf_op jit(solution)/shard_map/reshape | solution.py:402
  166.3 5.7 %feed_forward.1 = (bf16[128,768]{1,0:T(8,128)(2,1)}, f32[128,768]{1,0:T(8,128)S(1)}, bf16[128,768]{1,0:T(8,128)(2,1)S(1)}, bf16[128,768]{1,0:T(8,128)(2,1)S(1)},...) custom-call(bf16[4,128,192]{2,1,0:T(8,128)(2,1)S(1)} %copy.150.heads, ...), custom_call_target="tpu_custom_call" | custom-call | flops 1056964608 | bytes 8388608 | tf_op jit(solution)/shard_map/feed_forward/pallas_call | solution.py:451
  189.4 9.5 %attend_backward.1 = (bf16[512,192]{1,0:T(8,128)(2,1)S(1)}, bf16[512,192]{1,0:T(8,128)(2,1)S(1)}, bf16[512,192]{1,0:T(8,128)(2,1)S(1)}, f32[5120,128]{1,0:T(8,128)}) custom-call(bf16[512,192]{1,0:T(8,128)(2,1)S(1)} %bitcast.127, bf16[512,192]{1,0:T(8,128)(2,1)S(1)} %copy-done.10, bf16[512,192]{1,0:T(8,128)(2,1)S(1)} %copy-done.12, ...), custom_call_target="tpu_custom_call" | custom-call | flops 1006632960 | bytes 10485760 | tf_op jit(solution)/shard_map/attend_backward/pallas_call | solution.py:481
  201.1 4.5 %all-to-all-start.5 = ((bf16[4,128,768]{2,1,0:T(8,128)(2,1)}), bf16[4,128,768]{2,1,0:T(8,128)(2,1)}, u32[]{:S(2)}, u32[]{:S(2)}) async-start(bf16[4,128,768]{2,1,0:T(8,128)(2,1)} %bitcast.135), calls=%async_computation.5 | async-start | bytes 1572864 | tf_op jit(solution)/shard_map/grad_normed_one/all_to_all | solution.py:329
  216.5 43.2 %table_scatter.1 = f32[512,128]{1,0:T(8,128)S(1)} custom-call(f32[5120,128]{1,0:T(8,128)S(1)} %copy-done.24, s32[1,256,256]{2,1,0:T(8,128)S(1)} %copy-done.30, s32[5,1,256,256]{3,2,1,0:T(8,128)S(1)} %copy-done.26, s32[1,256,256]{2,1,0:T(8,128)S(1)} %copy-done.32, s32[4,64,64]{2,1,0:T(8,128)S(1)} %copy-done.34, s32[5,4,64,64]{3,2,1,0:T(8,128)S(1)} %copy-done.28, ...), custom_call_target="tpu_custom_call" | custom-call | flops 3932160000 | bytes 5242880 | tf_op jit(solution)/shard_map/table_scatter/pallas_call | solution.py:508
  269.9 5.9 %all-to-all-done.8 = bf16[4,128,768]{2,1,0:T(8,128)(2,1)S(1)} async-done(((bf16[4,128,768]{2,1,0:T(8,128)(2,1)}), bf16[4,128,768]{2,1,0:T(8,128)(2,1)S(1)}, u32[]{:S(2)}, u32[]{:S(2)}) %all-to-all-start.8) | async-done | bytes 786464 | tf_op jit(solution)/shard_map/upper_all/all_to_all | solution.py:329
  275.7 4.1 all-to-all-start.7
  281.7 5.7 %all-to-all-done.7 = bf16[4,2,128,192]{2,3,1,0:T(8,128)(2,1)} async-done(((bf16[4,2,128,192]{2,3,1,0:T(8,128)(2,1)}), bf16[4,2,128,192]{2,3,1,0:T(8,128)(2,1)}, u32[]{:S(2)}, u32[]{:S(2)}) %all-to-all-start.7) | async-done | bytes 393248 | tf_op jit(solution)/shard_map/act_pre/all_to_all | solution.py:329
  287.4 4.6 %all-to-all-start.12 = ((bf16[8,8,8,128]{3,2,1,0:T(8,128)(2,1)}), bf16[8,8,8,128]{3,2,1,0:T(8,128)(2,1)S(1)}, u32[]{:S(2)}, u32[]{:S(2)}) async-start(bf16[8,8,8,128]{3,2,1,0:T(8,128)(2,1)} %bitcast.32), calls=%async_computation.12 | async-start | bytes 262144 | tf_op jit(solution)/shard_map/table_grad/all_to_all | solution.py:329
  303.1 6.4 %all-to-all-done.11 = f32[32,1,216]{2,1,0:T(1,128)S(1)} async-done(((f32[32,1,216]{2,1,0:T(1,128)}), f32[32,1,216]{2,1,0:T(1,128)S(1)}, u32[]{:S(2)}, u32[]{:S(2)}) %all-to-all-start.11) | async-done | bytes 27680 | tf_op jit(solution)/shard_map/vector_grads/all_to_all | solution.py:329
  311.8 4.4 %all-to-all-start.6 = ((bf16[4,2,128,768]{3,2,1,0:T(8,128)(2,1)}), bf16[4,2,128,768]{3,2,1,0:T(8,128)(2,1)}, u32[]{:S(2)}, u32[]{:S(2)}) async-start(bf16[4,2,128,768]{3,2,1,0:T(8,128)(2,1)} %broadcast_in_dim.19), calls=%async_computation.6 | async-start | bytes 3145728 | tf_op jit(solution)/shard_map/rows_two/all_to_all | solution.py:329
  320.1 16.2 %all-to-all-done.6 = bf16[4,2,128,768]{3,2,1,0:T(8,128)(2,1)} async-done(((bf16[4,2,128,768]{3,2,1,0:T(8,128)(2,1)}), bf16[4,2,128,768]{3,2,1,0:T(8,128)(2,1)}, u32[]{:S(2)}, u32[]{:S(2)}) %all-to-all-start.6) | async-done | bytes 1572896 | tf_op jit(solution)/shard_map/rows_two/all_to_all | solution.py:329
  349.0 19.5 %all-to-all-done.10 = bf16[8,3,96,192]{2,3,1,0:T(8,128)(2,1)S(1)} async-done(((bf16[8,3,96,192]{2,3,1,0:T(8,128)(2,1)}), bf16[8,3,96,192]{2,3,1,0:T(8,128)(2,1)S(1)}, u32[]{:S(2)}, u32[]{:S(2)}) %all-to-all-start.10) | async-done | bytes 884768 | tf_op jit(solution)/shard_map/qkv_grads/all_to_all | solution.py:329
  368.4 3.6 all-to-all-start.9
  379.3 21.5 %all-to-all-done.9 = bf16[8,3,96,192]{2,3,1,0:T(8,128)(2,1)S(1)} async-done(((bf16[8,3,96,192]{2,3,1,0:T(8,128)(2,1)}), bf16[8,3,96,192]{2,3,1,0:T(8,128)(2,1)S(1)}, u32[]{:S(2)}, u32[]{:S(2)}) %all-to-all-start.9) | async-done | bytes 884768 | tf_op jit(solution)/shard_map/rest_grads/all_to_all | solution.py:329
  408.7 6.2 %all-to-all-done.13 = f32[32,1,128]{2,1,0:T(1,128)S(1)} async-done(((f32[32,1,128]{2,1,0:T(1,128)}), f32[32,1,128]{2,1,0:T(1,128)S(1)}, u32[]{:S(2)}, u32[]{:S(2)}) %all-to-all-start.13) | async-done | bytes 16416 | tf_op jit(solution)/shard_map/squares/all_to_all | solution.py:329
  (277 shorter events, 112.8 us)
Async XLA Ops:
  7.2 154.0 %all-gather.3.cloned.1.call-start = ((), (), s32[]{:S(2)}) async-start(), calls=%async_computation.14 | async-start | bytes 4866048 | tf_op jit(solution)/shard_map/weights_rest/all_gather | solution.py:400
  11.9 43.0 %all-to-all-start.1 = ((f32[32,1,216]{2,1,0:T(1,128)}), f32[32,1,216]{2,1,0:T(1,128)S(1)}, u32[]{:S(2)}, u32[]{:S(2)}) async-start(f32[32,1,216]{2,1,0:T(1,128)} %reshape.178), calls=%async_computation.1 | async-start | bytes 65536 | tf_op jit(solution)/shard_map/vectors_all/all_to_all | solution.py:329
  55.6 12.6 %all-to-all-start.2 = ((bf16[8,8,8,128]{3,2,1,0:T(8,128)(2,1)}), bf16[8,8,8,128]{3,2,1,0:T(8,128)(2,1)S(1)}, u32[]{:S(2)}, u32[]{:S(2)}) async-start(bf16[8,8,8,128]{3,2,1,0:T(8,128)(2,1)} %broadcast_in_dim.18), calls=%async_computation.2 | async-start | bytes 262144 | tf_op jit(solution)/shard_map/table_all/all_to_all | solution.py:329
  69.8 68.0 %all-to-all-start = ((bf16[4,128,768]{2,1,0:T(8,128)(2,1)}), bf16[4,128,768]{2,1,0:T(8,128)(2,1)S(1)}, u32[]{:S(2)}, u32[]{:S(2)}) async-start(bf16[4,128,768]{2,1,0:T(8,128)(2,1)} %broadcast_in_dim.16), calls=%async_computation | async-start | bytes 1572864 | tf_op jit(solution)/shard_map/rows_all/all_to_all | solution.py:329
  76.7 61.1 %copy-start.23 = (s32[1,4]{1,0:T(1,128)S(1)}, s32[1,4]{1,0:T(1,128)}, u32[]{:S(2)}) copy-start(s32[1,4]{1,0:T(1,128)} %small_counts.1) | copy-start | bytes 52
  152.4 8.7 %all-to-all-start.3 = ((bf16[4,128,192]{1,2,0:T(8,128)(2,1)}), bf16[4,128,192]{1,2,0:T(8,128)(2,1)S(1)}, u32[]{:S(2)}, u32[]{:S(2)}) async-start(bf16[4,128,192]{1,2,0:T(8,128)(2,1)} %copy.144), calls=%async_computation.3 | async-start | bytes 393216 | tf_op jit(solution)/shard_map/mixed_rows/all_to_all | solution.py:329
  174.9 8.7 %all-to-all-start.4 = ((bf16[4,128,192]{1,2,0:T(8,128)(2,1)}), bf16[4,128,192]{1,2,0:T(8,128)(2,1)S(1)}, u32[]{:S(2)}, u32[]{:S(2)}) async-start(bf16[4,128,192]{1,2,0:T(8,128)(2,1)} %copy.151), calls=%async_computation.4 | async-start | bytes 393216 | tf_op jit(solution)/shard_map/grad_heads/all_to_all | solution.py:329
  201.1 58.5 %all-to-all-start.5 = ((bf16[4,128,768]{2,1,0:T(8,128)(2,1)}), bf16[4,128,768]{2,1,0:T(8,128)(2,1)}, u32[]{:S(2)}, u32[]{:S(2)}) async-start(bf16[4,128,768]{2,1,0:T(8,128)(2,1)} %bitcast.135), calls=%async_computation.5 | async-start | bytes 1572864 | tf_op jit(solution)/shard_map/grad_normed_one/all_to_all | solution.py:329
  216.5 43.2 %copy-start.6 = (bf16[128,768]{1,0:T(8,128)(2,1)S(1)}, bf16[128,768]{1,0:T(8,128)(2,1)}, u32[]{:S(2)}) copy-start(bf16[128,768]{1,0:T(8,128)(2,1)} %upper.1) | copy-start | bytes 589828
  260.6 15.1 %all-to-all-start.8 = ((bf16[4,128,768]{2,1,0:T(8,128)(2,1)}), bf16[4,128,768]{2,1,0:T(8,128)(2,1)S(1)}, u32[]{:S(2)}, u32[]{:S(2)}) async-start(bf16[4,128,768]{2,1,0:T(8,128)(2,1)} %broadcast_in_dim.20), calls=%async_computation.8 | async-start | bytes 1572864 | tf_op jit(solution)/shard_map/upper_all/all_to_all | solution.py:329
  267.0 26.1 %copy-start.58 = (f32[1,32,24]{2,1,0:T(8,128)S(1)}, f32[1,32,24]{2,1,0:T(8,128)}, u32[]{:S(2)}) copy-start(f32[1,32,24]{2,1,0:T(8,128)} %concatenate.34) | copy-start | bytes 9220
  268.5 33.8 %copy-start.20 = (bf16[128,768]{1,0:T(8,128)(2,1)S(1)}, bf16[128,768]{1,0:T(8,128)(2,1)}, u32[]{:S(2)}) copy-start(bf16[128,768]{1,0:T(8,128)(2,1)} %copy-done.19) | copy-start | bytes 589828
  268.5 33.8 %copy-start.22 = (bf16[128,768]{1,0:T(8,128)(2,1)S(1)}, bf16[128,768]{1,0:T(8,128)(2,1)}, u32[]{:S(2)}) copy-start(bf16[128,768]{1,0:T(8,128)(2,1)} %copy-done.21) | copy-start | bytes 589828
  275.7 27.3 %copy-start.39 = (bf16[4,128,768]{2,1,0:T(8,128)(2,1)}, bf16[4,128,768]{2,1,0:T(8,128)(2,1)S(1)}, u32[]{:S(2)}) copy-start(bf16[4,128,768]{2,1,0:T(8,128)(2,1)S(1)} %all-to-all-done.8) | copy-start | bytes 2359300
  275.7 11.6 %all-to-all-start.7 = ((bf16[4,2,128,192]{2,3,1,0:T(8,128)(2,1)}), bf16[4,2,128,192]{2,3,1,0:T(8,128)(2,1)}, u32[]{:S(2)}, u32[]{:S(2)}) async-start(bf16[4,2,128,192]{2,3,1,0:T(8,128)(2,1)} %copy.154), calls=%async_computation.7 | async-start | bytes 786432 | tf_op jit(solution)/shard_map/act_pre/all_to_all | solution.py:329
  287.4 11.9 %all-to-all-start.12 = ((bf16[8,8,8,128]{3,2,1,0:T(8,128)(2,1)}), bf16[8,8,8,128]{3,2,1,0:T(8,128)(2,1)S(1)}, u32[]{:S(2)}, u32[]{:S(2)}) async-start(bf16[8,8,8,128]{3,2,1,0:T(8,128)(2,1)} %bitcast.32), calls=%async_computation.12 | async-start | bytes 262144 | tf_op jit(solution)/shard_map/table_grad/all_to_all | solution.py:329
  299.3 10.3 %all-to-all-start.11 = ((f32[32,1,216]{2,1,0:T(1,128)}), f32[32,1,216]{2,1,0:T(1,128)S(1)}, u32[]{:S(2)}, u32[]{:S(2)}) async-start(f32[32,1,216]{2,1,0:T(1,128)} %reshape.180), calls=%async_computation.11 | async-start | bytes 65536 | tf_op jit(solution)/shard_map/vector_grads/all_to_all | solution.py:329
  311.8 24.5 %all-to-all-start.6 = ((bf16[4,2,128,768]{3,2,1,0:T(8,128)(2,1)}), bf16[4,2,128,768]{3,2,1,0:T(8,128)(2,1)}, u32[]{:S(2)}, u32[]{:S(2)}) async-start(bf16[4,2,128,768]{3,2,1,0:T(8,128)(2,1)} %broadcast_in_dim.19), calls=%async_computation.6 | async-start | bytes 3145728 | tf_op jit(solution)/shard_map/rows_two/all_to_all | solution.py:329
  336.3 32.1 %all-to-all-start.10 = ((bf16[8,3,96,192]{2,3,1,0:T(8,128)(2,1)}), bf16[8,3,96,192]{2,3,1,0:T(8,128)(2,1)S(1)}, u32[]{:S(2)}, u32[]{:S(2)}) async-start(bf16[8,3,96,192]{2,3,1,0:T(8,128)(2,1)} %pad_maximum_fusion.1), calls=%async_computation.10 | async-start | bytes 2359296 | tf_op jit(solution)/shard_map/qkv_grads/all_to_all | solution.py:329
  368.4 32.4 %all-to-all-start.9 = ((bf16[8,3,96,192]{2,3,1,0:T(8,128)(2,1)}), bf16[8,3,96,192]{2,3,1,0:T(8,128)(2,1)S(1)}, u32[]{:S(2)}, u32[]{:S(2)}) async-start(bf16[8,3,96,192]{2,3,1,0:T(8,128)(2,1)} %pad_maximum_fusion), calls=%async_computation.9 | async-start | bytes 2359296 | tf_op jit(solution)/shard_map/rest_grads/all_to_all | solution.py:329
  378.6 29.2 %copy-start.8 = (f32[128,768]{1,0:T(8,128)S(1)}, f32[128,768]{1,0:T(8,128)}, u32[]{:S(2)}) copy-start(f32[128,768]{1,0:T(8,128)} %copy-done.7) | copy-start | bytes 1179652
  378.6 29.2 %copy-start.38 = (f32[128,768]{1,0:T(8,128)S(1)}, f32[128,768]{1,0:T(8,128)}, u32[]{:S(2)}) copy-start(f32[128,768]{1,0:T(8,128)} %copy-done.37) | copy-start | bytes 1179652
  378.6 29.2 %copy-start.67 = (f32[128]{0:T(128)S(1)}, f32[128]{0:T(128)}, u32[]{:S(2)}) copy-start(f32[128]{0:T(128)} %add_rsqrt_fusion) | copy-start | bytes 1540
  405.0 9.9 %all-to-all-start.13 = ((f32[32,1,128]{2,1,0:T(1,128)}), f32[32,1,128]{2,1,0:T(1,128)S(1)}, u32[]{:S(2)}, u32[]{:S(2)}) async-start(f32[32,1,128]{2,1,0:T(1,128)} %broadcast_in_dim.23), calls=%async_computation.13 | async-start | bytes 32768 | tf_op jit(solution)/shard_map/squares/all_to_all | solution.py:329
  (61 other events, 348.5 us)
Sparse Core Ops, SparseCore 0:
  11.5 72.2 all-gather.2

commit v2 on v1

v2 whole, which is shorter than its diff:
```python
import jax
import jax.numpy as jnp
from jax import lax
from jax.experimental import pallas as pl
from jax.experimental.pallas import tpu as pltpu
from jax.sharding import PartitionSpec as P

HEAD_DIM = 24
NDIST = 512
NTYPE = 1536
STEPS = 5
ADAM_STEP = 10

NORM_EPSILON = 1e-05
NEGATIVE_FILL = -1e30
BETA_FIRST = 0.9
BETA_SECOND = 0.95
ADAM_EPSILON = 1e-08
RATE_MATRIX = 0.02
RATE_OUTPUT = 0.05
RATE_VECTOR = 0.15
WEIGHT_DECAY = 0.01
CLIP_NORM = 1.0

LANES = 128
SUB = 8
FIRST = [0] + [(NDIST + n * NTYPE) // LANES for n in range(STEPS)]
CHUNKS = [NDIST // LANES] + [NTYPE // LANES] * STEPS
LOOKUPS = STEPS + 1
VECTOR_ROWS = 16
BIG_QUARTERS = (1, 3)
BIG_PARTS = len(BIG_QUARTERS)
FIXED = 8192.0
NOWHERE = 4095
SCALE = HEAD_DIM**-0.5
BF = jnp.bfloat16
F32 = jnp.float32
VMEM_BYTES = 56 << 20

NN = (((1,), (0,)), ((), ()))
NT = (((1,), (1,)), ((), ()))
TN = (((0,), (0,)), ((), ()))


def dot(left, right, dims):
    return lax.dot_general(left, right, dims, preferred_element_type=F32)


def inner_of(size):
    return 1 << ((size.bit_length() - 1) // 2)


def xor_order(size):
    inner = inner_of(size)
    return [a * inner + b for b in range(inner) for a in range(size // inner)]


def kernel_call(body, outs, name, micros, args, scratch=(), smem_in=(), placed=(), us_at=None, ready=(), limit=VMEM_BYTES):
    n_in, n_out = len(args), len(outs)
    moved = [i for i in range(n_in) if i not in smem_in and i not in ready]
    blocks = [out[0] if isinstance(out, tuple) else 0 for out in outs]
    shapes = [out[1] if isinstance(out, tuple) else out for out in outs]
    flat = [(i, k) for i in range(n_out) for k in range(max(blocks[i], 1))]
    n_sems = sum(args[i].shape[0] if i in placed else 1 for i in moved)

    def wrapped(*refs):
        given, results = refs[:n_in], refs[n_in : n_in + len(flat)]
        refs = refs[n_in + len(flat) :]
        held = dict(zip(moved, refs))
        made, refs = refs[len(moved) : len(moved) + n_out], refs[len(moved) + n_out :]
        rest, (in_sems, out_sems) = refs[:-2], refs[-2:]
        arriving, sem = {}, 0
        for i in moved:
            pieces = [(given[i], held[i])]
            if i in placed:
                size = args[i].shape[0]
                pieces = [
                    (given[i].at[k], held[i].at[given[us_at][1] ^ other]) for k, other in enumerate(xor_order(size))
                ]
            arriving[i] = [pltpu.make_async_copy(a, b, in_sems.at[sem + n]) for n, (a, b) in enumerate(pieces)]
            sem += len(pieces)
        leaving = [
            pltpu.make_async_copy(made[i].at[k] if blocks[i] else made[i], results[at], out_sems.at[at])
            for at, (i, k) in enumerate(flat)
        ]
        for i in moved:
            for copy in arriving[i]:
                copy.start()
        waiting, unsent = list(moved), list(range(n_out))

        def need(*which):
            for i in which:
                if i in waiting:
                    waiting.remove(i)
                    for copy in arriving[i]:
                        copy.wait()

        def done(*which):
            for i in which:
                if i in unsent:
                    unsent.remove(i)
                    for at, (j, _) in enumerate(flat):
                        if i == j:
                            leaving[at].start()

        body(need, done, *[held.get(i, given[i]) for i in range(n_in)], *made, *rest)
        need(*moved)
        done(*range(n_out))
        for copy in leaving:
            copy.wait()

    anywhere, smem = pl.BlockSpec(memory_space=pl.ANY), pl.BlockSpec(memory_space=pltpu.SMEM)
    vmem = pl.BlockSpec(memory_space=pltpu.VMEM)
    return pl.pallas_call(
        wrapped,
        out_shape=tuple(shapes[i] for i, _ in flat),
        in_specs=[smem if i in smem_in else vmem if i in ready else anywhere for i in range(n_in)],
        out_specs=tuple([anywhere] * len(flat)),
        scratch_shapes=[pltpu.VMEM(args[i].shape, args[i].dtype) for i in moved]
        + [pltpu.VMEM((n, *o.shape) if n else o.shape, o.dtype) for n, o in zip(blocks, shapes)]
        + list(scratch)
        + [pltpu.SemaphoreType.DMA((n_sems,)), pltpu.SemaphoreType.DMA((len(flat),))],
        name=name,
        compiler_params=pltpu.CompilerParams(vmem_limit_bytes=limit),
        cost_estimate=pl.CostEstimate(flops=int(micros * 1e9), bytes_accessed=1 << 20, transcendentals=0),
    )(*args)


def big_block(refs, block, half):
    distance, paths, lengths = refs
    rows, lanes = pl.ds(SUB * block, SUB), slice(LANES * half, LANES * half + LANES)
    return [distance[0, rows, lanes]] + [paths[n, 0, rows, lanes] for n in range(STEPS)], lengths[0, rows, lanes]


def small_block(refs, block, pair):
    distance, paths, lengths = refs
    rows = pl.ds(SUB * block, SUB)

    def two(ref, *lead):
        return jnp.concatenate([ref[(*lead, 2 * pair, rows)], ref[(*lead, 2 * pair + 1, rows)]], axis=1)

    return [two(distance)] + [two(paths, n) for n in range(STEPS)], two(lengths)


def each_block(load, refs, first, count, sides, group, step):
    def some(at, carry):
        blocks = [first + at * group + u for u in range(group)]
        step([(*load(refs, block, side), block, side) for block in blocks for side in range(sides)])
        return carry

    lax.fori_loop(0, count // group, some, 0)


def bias_body(part, need, done, table, *refs):
    small, refs = (refs[:3], refs[3:]) if part == 0 else (None, refs)
    big, outs, words = refs[:3], refs[3:-1], refs[-1]
    need(0)
    heads, count = words.shape[:2]
    for k in range(count):
        low = jnp.round(table[SUB * 2 * k : SUB * (2 * k + 1), :].astype(F32) * FIXED).astype(jnp.int32)
        high = jnp.round(table[SUB * (2 * k + 1) : SUB * (2 * k + 2), :].astype(F32) * FIXED).astype(jnp.int32)
        word = (high << 16) | (low & 0xFFFF)
        for h in range(heads):
            words[h, k] = jnp.broadcast_to(word[h : h + 1], (SUB, LANES))

    def step(store):
        def run(parts):
            for index, lengths, block, side in parts:
                share = (1.0 / FIXED) / lengths.astype(F32)
                first, edges = [None] * heads, [None] * heads
                for t in range(LOOKUPS):
                    code = index[t]
                    lane = code & (LANES - 1)
                    odd = [(code & bit) != 0 for bit in (256, 512, 1024)]
                    shift = ((code >> 3) & 16) ^ 16
                    live = lengths > t - 1
                    for h in range(heads):
                        found = [
                            jnp.take_along_axis(words[h, FIRST[t] // 2 + k], lane, axis=1, mode="promise_in_bounds")
                            for k in range(CHUNKS[t] // 2)
                        ]
                        level = 0
                        while len(found) > 1:
                            found = [
                                jnp.where(odd[level], found[k + 1], found[k]) if k + 1 < len(found) else found[k]
                                for k in range(0, len(found), 2)
                            ]
                            level += 1
                        value = (found[0] << shift) >> 16
                        if t == 0:
                            first[h] = value
                        else:
                            value = jnp.where(live, value, 0)
                            edges[h] = value if edges[h] is None else edges[h] + value
                for h in range(heads):
                    value = first[h].astype(F32) * (1.0 / FIXED) + edges[h].astype(F32) * share
                    store(h, side, block, value)

        return run

    if small:

        def store_small(h, side, block, value):
            outs[0][h, side, pl.ds(SUB * block, SUB), :] = value

        need(1, 2, 3)
        each_block(small_block, small, 0, small[0].shape[1] // SUB, small[0].shape[0] // 2, 1, step(store_small))
        done(0)
    need(*range(1, 7 if small else 4))
    out = outs[-1]
    count = out.shape[2] // SUB
    first_block = big[0].shape[1] // SUB // sum(BIG_QUARTERS) * sum(BIG_QUARTERS[:part])

    def store_big(h, side, block, value):
        out[h, side, pl.ds(SUB * (block - first_block), SUB), :] = value

    each_block(big_block, big, first_block, count, big[0].shape[2] // LANES, 1, step(store_big))


def scatter_body(need, done, small_grads, sd, sp, sl, big_grads, bd, bp, bl, out, total):
    total[...] = jnp.zeros_like(total)
    sub = lax.broadcasted_iota(jnp.int32, (2 * SUB, LANES), 0)
    low_pattern = [(sub + 2 * SUB * k).astype(F32).astype(BF) for k in range(LANES // (2 * SUB))]
    upper = (sub >= SUB).astype(jnp.int32)
    high_pattern = [(2 * k + upper).astype(F32).astype(BF) for k in range(max(CHUNKS) // 2)]
    zero, one = jnp.zeros((2 * SUB, LANES), BF), jnp.ones((2 * SUB, LANES), BF)

    def twice(value):
        return jnp.concatenate([value, value], axis=0).astype(BF)

    def step(grads, side_rows):
        def run(parts):
            whole, shared = [], []
            for index, lengths, block, side in parts:
                inverse = 1.0 / lengths.astype(F32)
                for s in range(SUB):
                    g = grads[pl.ds((side * side_rows + SUB * block + s) * SUB, SUB), :]
                    whole.append(twice(g))
                    shared.append(twice(g * jnp.broadcast_to(inverse[s : s + 1], (SUB, LANES))))
            for t in range(LOOKUPS):
                left, right = [], []
                for part, (index, lengths, _, _) in enumerate(parts):
                    code = index[t] if t == 0 else jnp.where(lengths > t - 1, index[t], NOWHERE)
                    for s in range(SUB):
                        spread = jnp.broadcast_to(code[s : s + 1], (SUB, LANES))
                        low = twice((spread & (LANES - 1)).astype(F32))
                        high = twice((spread >> 7).astype(F32))
                        source = (whole if t == 0 else shared)[SUB * part + s]
                        left.append(jnp.concatenate([jnp.where(low == p, one, zero) for p in low_pattern], axis=0))
                        right.append(
                            jnp.concatenate(
                                [jnp.where(high == p, source, zero) for p in high_pattern[: CHUNKS[t] // 2]], axis=0
                            )
                        )
                span = slice(SUB * FIRST[t], SUB * (FIRST[t] + CHUNKS[t]))
                total[:, span] += dot(jnp.concatenate(left, axis=1), jnp.concatenate(right, axis=1), NT)

        return run

    need(0, 1, 2, 3)
    narrow, width = sd.shape[1], bd.shape[1]
    each_block(small_block, (sd, sp, sl), 0, narrow // SUB, sd.shape[0] // 2, 2, step(small_grads, narrow))
    need(4, 5, 6, 7)
    each_block(big_block, (bd, bp, bl), 0, width // SUB, width // LANES, 2, step(big_grads, width))
    out[...] = total[...].T.astype(BF)


def whole_matrix(ref, k):
    if len(ref.shape) == 3:
        return ref[k]
    value = ref[:, k]
    return value.reshape(value.shape[0] * value.shape[1], value.shape[2])


def norm_parts(values):
    center = values - jnp.mean(values, axis=-1, keepdims=True)
    spread = lax.rsqrt(jnp.mean(center * center, axis=-1, keepdims=True) + NORM_EPSILON)
    return center * spread, spread


def norm_back(scaled, xhat, spread):
    return spread * (
        scaled
        - jnp.mean(scaled, axis=-1, keepdims=True)
        - xhat * jnp.mean(scaled * xhat, axis=-1, keepdims=True)
    )


def head_lanes(head, width):
    lane = lax.broadcasted_iota(jnp.int32, (1, width), 1)
    return (lane >= head * HEAD_DIM) & (lane < (head + 1) * HEAD_DIM)


def peer_block(me, r, rows):
    return pl.ds(pl.multiple_of((me[0] ^ r) * rows, rows), rows)


def forward_body(n_head, need, done, *refs):
    rows_in, refs = refs[:n_head], refs[n_head:]
    me, big_counts, small_counts, pieces, weights, small_bias = refs[:6]
    big_bias, refs = refs[6 : 6 + BIG_PARTS], refs[6 + BIG_PARTS :]
    normed, qkv, big_probs, small_probs, vectors, hidden_bias = refs[:6]
    mixed_out, mixed = refs[6 : 6 + n_head], refs[6 + n_head]
    block = rows_in[0].shape[1]
    need(*range(n_head), n_head + 3)
    n_vectors, size = vectors.shape[0], vectors.shape[1] // pieces.shape[0]
    for piece in range(pieces.shape[0]):
        vectors[:, piece * size : (piece + 1) * size] = pieces[piece, :n_vectors, :size]
    heads, width = big_probs.shape[:2]
    pairs, wide = small_probs.shape[1:3]
    narrow = wide // 2
    columns = qkv.shape[2]
    halves = width // LANES
    biases = [None] * 2
    for j in range(n_head):
        span = slice(j * columns, (j + 1) * columns)
        hidden_bias[j : j + 1, :] = vectors[7:8, span]
        for i in range(2):
            value = jnp.where(me[0] == j, vectors[4 + i : 5 + i, span], 0.0)
            biases[i] = value if j == 0 else biases[i] + value
    for r in range(n_head):
        xhat, _ = norm_parts(rows_in[r][0].astype(F32))
        normed[peer_block(me, r, block), :] = (xhat * vectors[0:1, :] + vectors[1:2, :]).astype(BF)
    done(0, 4, 5)
    need(n_head + 4)
    for k in range(3):
        value = dot(normed[...], whole_matrix(weights, k), NN)
        if k != 1:
            value = value + biases[k // 2]
        qkv[k] = value.astype(BF)
    done(1)
    need(*range(n_head + 5, n_head + 6 + BIG_PARTS))
    mixed[...] = jnp.zeros_like(mixed)
    big_live = lax.broadcasted_iota(jnp.int32, (1, width), 1) < big_counts[0]
    small_live = []
    row = lax.broadcasted_iota(jnp.int32, (wide, wide), 0)
    lane = lax.broadcasted_iota(jnp.int32, (wide, wide), 1)
    for pair in range(pairs):
        first = (row < narrow) & (lane < small_counts[0, 2 * pair])
        second = (row >= narrow) & (lane >= narrow) & (lane < narrow + small_counts[0, 2 * pair + 1])
        small_live.append(first | second)

    def attend(span, extra, live, mine):
        query = jnp.where(mine, qkv[0, span, :], 0.0)
        scores = jnp.where(live, dot(query, qkv[1, span, :], NT) * SCALE + extra, NEGATIVE_FILL)
        power = jnp.exp(scores - jnp.max(scores, axis=-1, keepdims=True))
        probs = power * (1.0 / jnp.sum(power, axis=-1, keepdims=True))
        out = dot(probs.astype(BF), qkv[2, span, :], NN)
        mixed[span, :] = jnp.where(mine, out.astype(BF), mixed[span, :])
        return probs

    def big_heads(at, carry):
        for head in (2 * at, 2 * at + 1):
            extra = jnp.concatenate(
                [jnp.concatenate([part[head, half] for part in big_bias], axis=0) for half in range(halves)], axis=1
            )
            big_probs[head] = attend(slice(0, width), extra, big_live, head_lanes(head, columns))
        return carry

    lax.fori_loop(0, heads // 2, big_heads, 0)
    done(2)

    def small_heads(at, carry):
        for head in (2 * at, 2 * at + 1):
            for pair in range(pairs):
                extra = small_bias[head, pair]
                extra = jnp.concatenate([extra, extra], axis=0)
                span = slice(width + pair * wide, width + (pair + 1) * wide)
                small_probs[head, pair] = attend(span, extra, small_live[pair], head_lanes(head, columns))
        return carry

    lax.fori_loop(0, heads // 2, small_heads, 0)
    done(3)
    for r in range(n_head):
        mixed_out[r][...] = mixed[peer_block(me, r, block), :]


def put_matrix(ref, k, value):
    if len(ref.shape) == 3:
        ref[k] = value
        return
    rows = ref.shape[2]
    for d in range(ref.shape[0]):
        ref[d, k] = value[d * rows : (d + 1) * rows]


def backward_body(n_head, need, done, *refs):
    need(*range(n_head), n_head + 1, n_head + 2)
    grads_in, refs = refs[:n_head], refs[n_head:]
    me, qkv, small_probs, big_probs, weights, small_rows, big_rows, dqkv, column_sums = refs[:9]
    rows_out, (grad_heads,) = refs[9 : 9 + n_head], refs[9 + n_head :]
    heads, width = big_probs.shape[:2]
    pairs, wide = small_probs.shape[1:3]
    narrow = wide // 2
    columns = qkv.shape[2]
    halves = width // LANES
    block = grads_in[0].shape[0]
    for r in range(n_head):
        grad_heads[peer_block(me, r, block), :] = grads_in[r][...]
    dqkv[...] = jnp.zeros_like(dqkv)

    def attend(span, probs, mine):
        upper = jnp.where(mine, grad_heads[span, :], 0.0)
        grad_probs = dot(upper, qkv[2, span, :], NT)
        inner = jnp.sum(probs * grad_probs, axis=-1, keepdims=True)
        wide_scores = probs * (grad_probs - inner)
        grad_scores = wide_scores.astype(BF)
        dq = (dot(grad_scores, qkv[1, span, :], NN) * SCALE).astype(BF)
        dk = (dot(grad_scores, qkv[0, span, :], TN) * SCALE).astype(BF)
        dv = dot(probs.astype(BF), upper, TN).astype(BF)
        for k, value in enumerate((dq, dk, dv)):
            dqkv[k, span, :] = jnp.where(mine, value, dqkv[k, span, :])
        return grad_scores.astype(F32)

    def small_heads(at, carry):
        for head in (2 * at, 2 * at + 1):
            for pair in range(pairs):
                span = slice(width + pair * wide, width + (pair + 1) * wide)
                grad_scores = attend(span, small_probs[head, pair], head_lanes(head, columns))
                small_rows[pl.ds(pair * narrow * SUB + head, narrow, stride=SUB), :] = (
                    grad_scores[:narrow] + grad_scores[narrow:]
                )
        return carry

    lax.fori_loop(0, heads // 2, small_heads, 0)
    done(0)
    need(n_head + 3)

    def big_heads(at, carry):
        for head in (2 * at, 2 * at + 1):
            grad_scores = attend(slice(0, width), big_probs[head], head_lanes(head, columns))
            for half in range(halves):
                big_rows[pl.ds(half * width * SUB + head, width, stride=SUB), :] = grad_scores[
                    :, LANES * half : LANES * (half + 1)
                ]
        return carry

    lax.fori_loop(0, heads // 2, big_heads, 0)
    done(1, 2)
    need(n_head + 4)
    column_sums[...] = jnp.zeros_like(column_sums)
    for i, k in enumerate((0, 2)):
        column_sums[i, pl.ds(me[0], 1), :] = jnp.sum(dqkv[k].astype(F32), axis=0, keepdims=True)
    for r in range(n_head):
        rows = peer_block(me, r, block)
        total = dot(dqkv[0, rows, :], whole_matrix(weights, 0), NT)
        total = total + dot(dqkv[1, rows, :], whole_matrix(weights, 1), NT)
        total = total + dot(dqkv[2, rows, :], whole_matrix(weights, 2), NT)
        rows_out[r][...] = total.astype(BF)


def middle_body(n_head, need, done, *refs):
    mixed, refs = refs[:n_head], refs[n_head:]
    me, rows, upper, vectors, hidden_bias = refs[:5]
    weights, refs = refs[5 : 5 + n_head], refs[5 + n_head :]
    layer_out, grad_hidden, sums, pre_sums, normed_grad, act_pre = refs[:6]
    grad_heads = refs[6:]
    need(*range(2 * n_head + 5))
    columns = mixed[0].shape[1]
    slot = parcel_slot(columns)
    hidden = rows[...].astype(F32) + vectors[6:7, :]
    for r in range(n_head):
        hidden = hidden + dot(mixed[r][...], whole_matrix(weights[r], 0), NT)
    xhat, spread = norm_parts(hidden)
    low = (xhat * vectors[2:3, :] + vectors[3:4, :]).astype(BF)
    normed_grad[0] = low
    cotangent = upper[...]
    final = hidden + vectors[8:9, :]
    grad_normed = jnp.zeros_like(hidden)
    for r in range(n_head):
        peer = me[0] ^ r
        into, down = whole_matrix(weights[r], 1), whole_matrix(weights[r], 2)
        pre = dot(low, into, NN) + hidden_bias[pl.ds(peer, 1), :]
        phi = 0.5 * (1.0 + lax.erf(pre * (0.5**0.5)))
        active = (pre * phi).astype(BF)
        final = final + dot(active, down, NT)
        slope = phi + pre * jnp.exp(-0.5 * pre * pre) * (0.5 / jnp.pi) ** 0.5
        low_grad = (dot(cotangent, down, NN) * slope).astype(BF)
        pre_sums[pl.ds(peer, 1), :] = jnp.sum(low_grad.astype(F32), axis=0, keepdims=True)
        grad_normed = grad_normed + dot(low_grad, into, NT)
        act_pre[peer, :, 0:columns] = active
        act_pre[peer, :, slot : slot + columns] = low_grad
    layer_out[...] = final.astype(BF)
    wide = cotangent.astype(F32)
    grad = wide + norm_back(grad_normed * vectors[2:3, :], xhat, spread)
    grad_hidden[...] = grad
    grad_small = grad.astype(BF)
    normed_grad[1] = grad_small
    for r in range(n_head):
        grad_heads[r][...] = dot(grad_small, whole_matrix(weights[r], 0), NN).astype(BF)
    sums[0:1, :] = jnp.sum(grad_normed * xhat, axis=0, keepdims=True)
    sums[1:2, :] = jnp.sum(grad_normed, axis=0, keepdims=True)
    sums[2:3, :] = jnp.sum(grad, axis=0, keepdims=True)
    sums[3:4, :] = jnp.sum(wide, axis=0, keepdims=True)


def parcel_slot(columns):
    return (columns + LANES - 1) // LANES * LANES


def weight_grads_body(n_head, need, done, *refs):
    given, mixed, refs = refs[:n_head], refs[n_head : 2 * n_head], refs[2 * n_head :]
    me, act_pre, normed_one, dqkv = refs[:4]
    normed_grad, out = refs[4 : 4 + n_head], refs[-1]
    columns = mixed[0].shape[1]
    slot = parcel_slot(columns)

    def all_rows(pick):
        return jnp.concatenate([pick(me[0] ^ r) for r in range(n_head)], axis=0)

    need(2 * n_head + 2, 2 * n_head + 3)
    for k in range(3):
        put_matrix(out, k, dot(normed_one[...], dqkv[k], TN).astype(BF))
    need(*range(2 * n_head), 2 * n_head + 1, *range(2 * n_head + 4, 3 * n_head + 4))
    heads_out = jnp.concatenate([m[...] for m in mixed], axis=0)
    put_matrix(out, 3, dot(jnp.concatenate([n[1] for n in normed_grad], axis=0), heads_out, TN).astype(BF))
    grad_pre = all_rows(lambda p: act_pre[p, :, slot : slot + columns])
    put_matrix(out, 4, dot(jnp.concatenate([n[0] for n in normed_grad], axis=0), grad_pre, TN).astype(BF))
    cotangent = jnp.concatenate([g[1] for g in given], axis=0)
    put_matrix(out, 5, dot(cotangent, all_rows(lambda p: act_pre[p, :, 0:columns]), TN).astype(BF))


def merge_body(need, done, *refs):
    parts, out = refs[:-1], refs[-1]
    need(*range(len(parts)))
    value = parts[0][...].astype(F32)
    for part in parts[1:]:
        value = value + part[...].astype(F32)
    out[...] = value.astype(BF)


def input_body(n_head, n_vectors, need, done, *refs):
    parts, refs = refs[:n_head], refs[n_head:]
    me, rows, grad_hidden, vectors, sums, column_sums, pre_sums, table_grad, input_grad, parcel, terms = refs
    need(*range(n_head), *range(n_head + 1, n_head + 8))
    grad_normed = parts[0][...].astype(F32)
    for part in parts[1:]:
        grad_normed = grad_normed + part[...].astype(F32)
    xhat, spread = norm_parts(rows[...].astype(F32))
    input_grad[...] = (grad_hidden[...] + norm_back(grad_normed * vectors[0:1, :], xhat, spread)).astype(BF)
    done(0)
    columns = column_sums.shape[2]
    terms[...] = jnp.zeros_like(terms)
    terms[0:1, :] = jnp.sum(grad_normed * xhat, axis=0, keepdims=True)
    terms[1:2, :] = jnp.sum(grad_normed, axis=0, keepdims=True)
    terms[2:4, :] = sums[0:2, :]
    terms[6:7, :] = sums[2:3, :]
    terms[8:9, :] = sums[3:4, :]
    for j in range(n_head):
        span = slice(j * columns, (j + 1) * columns)
        for i in range(2):
            terms[4 + i : 5 + i, span] = column_sums[i, j : j + 1, :]
        terms[7:8, span] = pre_sums[j : j + 1, :]
    inner, outer, height, _ = parcel.shape
    lanes, height = vectors.shape[1] // (inner * outer), height - VECTOR_ROWS
    parcel[:, :, :VECTOR_ROWS, :] = jnp.zeros((inner, outer, VECTOR_ROWS, LANES), BF)
    for d in range(inner * outer):
        at = me[1] ^ d
        a, b = at % inner, at // inner
        parcel[a, b, :VECTOR_ROWS, 0:lanes] = terms[:, d * lanes : (d + 1) * lanes].astype(BF)
        parcel[a, b, VECTOR_ROWS:, :] = table_grad[d * height : (d + 1) * height, :]


def adamw_update(weight, first_moment, second_moment, gradient, learn_rate):
    first_new = BETA_FIRST * first_moment + (1.0 - BETA_FIRST) * gradient
    second_new = BETA_SECOND * second_moment + (1.0 - BETA_SECOND) * gradient * gradient
    first_hat = first_new / (1.0 - BETA_FIRST**ADAM_STEP)
    second_hat = second_new / (1.0 - BETA_SECOND**ADAM_STEP)
    weight_new = weight - learn_rate * (
        first_hat / (jnp.sqrt(second_hat) + ADAM_EPSILON) + WEIGHT_DECAY * weight
    )
    return (weight_new, first_new, second_new)


def shard_body(need, done, arrived, shards, squares):
    need(0)
    value = arrived[0].astype(F32)
    for d in range(1, arrived.shape[0]):
        value = value + arrived[d].astype(F32)
    shards[...] = value
    squares[...] = jnp.broadcast_to(jnp.sum(value * value).reshape(1, 1), squares.shape)


def told_body(need, done, *refs):
    parts, (squares, shard, told) = refs[:-3], refs[-3:]
    need(*range(len(parts) + 1))
    value = parts[0][...].astype(F32)
    for part in parts[1:]:
        value = value + part[...].astype(F32)
    table = value[VECTOR_ROWS:]
    shard[...] = table
    here = jnp.sum(table * table).reshape(1, 1) + squares[0:1, 0:1]
    row = lax.broadcasted_iota(jnp.int32, (VECTOR_ROWS, LANES), 0)
    lane = lax.broadcasted_iota(jnp.int32, (VECTOR_ROWS, LANES), 1)
    message = jnp.where((row == VECTOR_ROWS - 1) & (lane == 0), here, value[:VECTOR_ROWS])
    told[...] = jnp.broadcast_to(message[None], told.shape)


def update_body(n_head, n_vectors, need, done, *refs):
    need(1)
    me, told, shards, out_shard, down_shard, table_shard = refs[:6]
    params, outs = refs[6:21], refs[21:36]
    norm_out = refs[36]
    n_dp = told.shape[0] // n_head

    def merged(d):
        value = told[d * n_head]
        for j in range(1, n_head):
            value = value + told[d * n_head + j]
        return value

    row = lax.broadcasted_iota(jnp.int32, (VECTOR_ROWS, LANES), 0)

    def square(d, total):
        value = merged(d)
        return total + jnp.where(row < n_vectors, value * value, jnp.where(row == VECTOR_ROWS - 1, value, 0.0))

    total = lax.fori_loop(0, n_dp, square, jnp.zeros((VECTOR_ROWS, LANES), F32))
    grad_norm = jnp.sqrt(jnp.sum(total).reshape(1, 1))
    norm_out[...] = jnp.broadcast_to(grad_norm, norm_out.shape)
    factor = CLIP_NORM / jnp.maximum(grad_norm, CLIP_NORM)

    def update(at, gradient, rate, pick=...):
        weight, first, second = (ref[pick] for ref in params[3 * at : 3 * at + 3])
        for ref, value in zip(outs[3 * at : 3 * at + 3], adamw_update(weight, first, second, gradient * factor, rate)):
            ref[pick] = value

    for k in range(3):
        update(0, shards[k], RATE_MATRIX, k)
    update(0, shards[4], RATE_MATRIX, 3)
    update(1, out_shard[...], RATE_OUTPUT)
    update(2, down_shard[...], RATE_MATRIX)
    mine = merged(me[1])
    size = params[9].shape[1]
    gradient = jnp.zeros((n_vectors, size), F32)
    for j in range(n_head):
        gradient = jnp.where(me[0] == j, mine[:n_vectors, j * size : (j + 1) * size], gradient)
    update(3, gradient, RATE_VECTOR)
    heads = params[12].shape[0]
    for c in range(table_shard.shape[0] // heads):
        update(4, table_shard[c * heads : (c + 1) * heads, :], RATE_VECTOR, (slice(None), slice(c * LANES, (c + 1) * LANES)))


def exchange(value, axis):
    return lax.all_to_all(value, axis, split_axis=0, concat_axis=0, tiled=True)


def spread_all(value, axis):
    size = lax.axis_size(axis)
    return exchange(jnp.broadcast_to(value[None], (size, *value.shape)), axis)


def swap(values, n_head):
    return [values[0]] + [
        lax.ppermute(values[r], "head", [(i, i ^ r) for i in range(n_head)]) for r in range(1, n_head)
    ]


def struct(shape, dtype):
    return jax.ShapeDtypeStruct(shape, dtype)


def on_device(
    node_rows,
    output_grad,
    weight_in,
    first_in,
    second_in,
    weight_out,
    first_out,
    second_out,
    weight_down,
    first_down,
    second_down,
    vectors,
    first_vectors,
    second_vectors,
    bias_table,
    first_table,
    second_table,
    big_counts,
    small_counts,
    big_distance,
    small_distance,
    big_paths,
    small_paths,
    big_lengths,
    small_lengths,
):
    everyone = ("dp", "head")
    n_dp, n_head = lax.axis_size("dp"), lax.axis_size("head")
    head_index, dp_index = lax.axis_index("head"), lax.axis_index("dp")
    me = head_index.reshape(1).astype(jnp.int32)
    shard_rows, columns = weight_in.shape[1], weight_in.shape[2]
    model = shard_rows * n_dp
    my_rows = node_rows.shape[0]
    group_rows = my_rows * n_head
    heads = columns // HEAD_DIM
    width, narrow = big_distance.shape[1], small_distance.shape[1]
    pairs = small_distance.shape[0] // 2
    table_chunks = bias_table.shape[0] // LANES
    all_chunks = table_chunks * n_dp
    n_vectors, shard_width = vectors.shape
    stacked = shard_rows % 16 == 0
    big_ints = (big_distance, big_paths, big_lengths)
    small_ints = (small_distance, small_paths, small_lengths)
    inner = inner_of(n_dp)
    outer = n_dp // inner
    dp_pairs = lambda k: [(i, i ^ k) for i in range(n_dp)]
    us = jnp.stack([head_index, dp_index]).astype(jnp.int32)
    lanes_used = model // n_dp

    def far_shards(value):
        return [value] + [lax.ppermute(value, "dp", dp_pairs(k)) for k in range(inner, n_dp, inner)]

    def near_shards(values):
        value = jnp.stack(values)
        return [value] + [lax.ppermute(value, "dp", dp_pairs(k)) for k in range(1, inner)]

    def to_head(value, r):
        return lax.ppermute(value, "head", [(i, i ^ r) for i in range(n_head)])

    far = n_head // 2
    near_heads = range(1, far)

    rest_sent = jnp.stack([weight_out.astype(BF).T, weight_in[3].astype(BF), weight_down.astype(BF).T])
    rest_sent, my_table = lax.optimization_barrier((rest_sent, bias_table))
    with jax.named_scope("rest_far"):
        rest_far = far_shards(rest_sent)
    table_sent = my_table.astype(BF).T.reshape(heads, table_chunks, LANES).transpose(1, 0, 2)
    with jax.named_scope("table_all"):
        table_all = spread_all(table_sent, "dp").reshape(all_chunks * heads, LANES)
    given = {0: jnp.stack([node_rows, output_grad])}
    with jax.named_scope("rows_far"):
        given[far] = to_head(given[0], far)
    qkv_sent = weight_in[:3].astype(BF)
    vectors_sent = jnp.pad(vectors, ((0, VECTOR_ROWS - n_vectors), (0, LANES - shard_width)))
    table_all, vectors_sent, qkv_sent, *rest_far = lax.optimization_barrier(
        (table_all, vectors_sent, qkv_sent, *rest_far)
    )
    with jax.named_scope("vectors_all"):
        vector_pieces = spread_all(vectors_sent, everyone)
    with jax.named_scope("rest_near"):
        rest_near = near_shards(rest_far)
    with jax.named_scope("qkv_far"):
        qkv_far = far_shards(qkv_sent)

    def pair_bias(part, table, ints):
        rows = width // sum(BIG_QUARTERS) * BIG_QUARTERS[part]
        big_range = struct((heads, width // LANES, rows, LANES), F32)
        return kernel_call(
            lambda *refs: bias_body(part, *refs),
            ([struct((heads, pairs, narrow, LANES), F32)] if part == 0 else []) + [big_range],
            "pair_bias",
            12 if part == 0 else 20,
            (table, *ints),
            [pltpu.VMEM((heads, all_chunks // 2, SUB, LANES), jnp.int32)],
        )

    small_bias, *big_bias = pair_bias(0, table_all, (*small_ints, *big_ints))
    held = lax.optimization_barrier((small_bias, vector_pieces, table_all, given[far], *rest_near, *qkv_far))
    (small_bias, vector_pieces, table_all, given[far]), held = held[:4], held[4:]
    rest_near, qkv_far = held[:inner], held[inner:]
    weights_rest = jnp.concatenate(rest_near)
    with jax.named_scope("qkv_near"):
        qkv_near = near_shards(qkv_far)
    if not stacked:
        order = jnp.argsort(jnp.array(xor_order(n_dp), jnp.int32) ^ dp_index)
        weights_rest = weights_rest[order].transpose(1, 0, 2, 3).reshape(3, model, columns)
    weights_held = {0: weights_rest}
    with jax.named_scope("rest_far_head"):
        weights_held[far] = to_head(weights_rest, far)
    with jax.named_scope("rows_near"):
        for r in near_heads:
            given[r], given[far + r] = to_head(given[0], r), to_head(given[far], r)
    for part in range(1, BIG_PARTS):
        big_bias += pair_bias(part, table_all, big_ints)
    held = lax.optimization_barrier((big_bias[-1], *qkv_near, *[given[r] for r in range(n_head)]))
    big_bias[-1], qkv_near, given = held[0], held[1 : 1 + inner], held[1 + inner :]
    with jax.named_scope("rest_near_head"):
        for r in near_heads:
            weights_held[r] = to_head(weights_held[0], r)
    weights_attend = jnp.concatenate(qkv_near)
    if not stacked:
        weights_attend = weights_attend[order].transpose(1, 0, 2, 3).reshape(3, model, columns)

    block = struct((my_rows, columns), BF)
    rows_block = struct((my_rows, model), BF)
    normed_one, qkv, big_probs, small_probs, all_vectors, hidden_bias, *mixed = kernel_call(
        lambda *refs: forward_body(n_head, *refs),
        [
            struct((group_rows, model), BF),
            struct((3, group_rows, columns), BF),
            struct((heads, width, width), F32),
            struct((heads, pairs, 2 * narrow, 2 * narrow), F32),
            struct((n_vectors, model), F32),
            struct((n_head, columns), F32),
            *[block] * n_head,
        ],
        "attend_forward",
        12,
        (*given, us, big_counts, small_counts, vector_pieces, weights_attend, small_bias, *big_bias),
        [pltpu.VMEM((group_rows, columns), BF)],
        range(n_head, n_head + 3),
        (n_head + 4,) if stacked else (),
        n_head,
    )
    with jax.named_scope("mixed_rows"):
        mixed_rows = swap(mixed, n_head)
    mixed_rows[0], *held = lax.optimization_barrier((mixed_rows[0], *[weights_held[r] for r in range(far + 1)]))
    weights_held.update(enumerate(held))
    with jax.named_scope("rest_near_head"):
        for r in near_heads:
            weights_held[far + r] = to_head(weights_held[far], r)
    weights_rest = [weights_held[r] for r in range(n_head)]

    layer_out, grad_hidden, sums, pre_sums, normed_grad, act_pre, *grad_heads = kernel_call(
        lambda *refs: middle_body(n_head, *refs),
        [
            rows_block,
            struct((my_rows, model), F32),
            struct((4, model), F32),
            struct((n_head, columns), F32),
            struct((2, my_rows, model), BF),
            struct((n_head, my_rows, 2 * parcel_slot(columns)), BF),
            *[block] * n_head,
        ],
        "feed_forward",
        6,
        (*mixed_rows, us, node_rows, output_grad, all_vectors, hidden_bias, *weights_rest),
        (),
        (n_head,),
        range(n_head + 5, 2 * n_head + 5) if stacked else (),
        n_head,
    )
    with jax.named_scope("grad_heads"):
        grad_heads = swap(grad_heads, n_head)
    with jax.named_scope("act_pre"):
        act_pre = exchange(act_pre, "head")
    with jax.named_scope("normed_grad"):
        rows_held = {0: normed_grad}
        for r in (far, *range(1, far)):
            rows_held[r] = lax.ppermute(normed_grad, "head", [(i, i ^ r) for i in range(n_head)])

    small_rows, big_rows, dqkv, column_sums, *rows_sent = kernel_call(
        lambda *refs: backward_body(n_head, *refs),
        [
            struct((pairs * narrow * SUB, LANES), F32),
            struct((width // LANES * width * SUB, LANES), F32),
            struct((3, group_rows, columns), BF),
            struct((2, n_head, columns), F32),
            *[rows_block] * n_head,
        ],
        "attend_backward",
        14,
        (*grad_heads, us, qkv, small_probs, big_probs, weights_attend),
        [pltpu.VMEM((group_rows, columns), BF)],
        (n_head,),
        (n_head + 4,) if stacked else (),
        n_head,
    )
    small_rows, *arrived = lax.optimization_barrier((small_rows, *[rows_held[r] for r in range(1, far + 1)]))
    rows_held.update(zip(range(1, far + 1), arrived))
    with jax.named_scope("normed_grad"):
        for r in range(1, far):
            rows_held[far + r] = lax.ppermute(rows_held[far], "head", [(i, i ^ r) for i in range(n_head)])
    (weight_grads,) = kernel_call(
        lambda *refs: weight_grads_body(n_head, *refs),
        [struct((n_dp, 6, shard_rows, columns) if stacked else (6, model, columns), BF)],
        "weight_grads",
        6,
        (*given, *mixed, us, act_pre, normed_one, dqkv, *[rows_held[r] for r in range(n_head)]),
        (),
        (2 * n_head,),
    )
    if not stacked:
        weight_grads = weight_grads.reshape(6, n_dp, shard_rows, columns).transpose(1, 0, 2, 3)
    weight_grads, small_rows, *rows_sent = lax.optimization_barrier((weight_grads, small_rows, *rows_sent))
    with jax.named_scope("weight_grads"):
        weights_arrived = exchange(weight_grads, "dp")
    with jax.named_scope("grad_normed_one"):
        rows_back = swap(rows_sent, n_head)
    (table_grad,) = kernel_call(
        scatter_body,
        [struct((all_chunks * heads, LANES), BF)],
        "table_scatter",
        40,
        (small_rows, *small_ints, big_rows, *big_ints),
        [pltpu.VMEM((LANES, all_chunks * heads), F32)],
    )
    table_grad, *rows_back = lax.optimization_barrier((table_grad, *rows_back))
    table_rows = table_chunks * heads
    block = struct((outer, VECTOR_ROWS + table_rows, LANES), BF)
    input_grad, *inner_sent = kernel_call(
        lambda *refs: input_body(n_head, n_vectors, *refs),
        [rows_block, (inner, block)],
        "input_grad",
        3,
        (*rows_back, us, node_rows, grad_hidden, all_vectors, sums, column_sums, pre_sums, table_grad),
        [pltpu.VMEM((VECTOR_ROWS, model), F32)],
        (n_head,),
    )
    with jax.named_scope("table_inner"):
        arrived = [inner_sent[0]] + [lax.ppermute(inner_sent[k], "dp", dp_pairs(k)) for k in range(1, inner)]
    weights_arrived, *arrived = lax.optimization_barrier((weights_arrived, *arrived))
    outer_sent = kernel_call(
        merge_body,
        [(outer, struct(block.shape[1:], BF))],
        "merge_table",
        1,
        tuple(arrived),
    )
    with jax.named_scope("table_outer"):
        parts = [outer_sent[0]] + [
            lax.ppermute(outer_sent[k], "dp", dp_pairs(k * inner)) for k in range(1, outer)
        ]
    shards, squares = kernel_call(
        shard_body,
        [struct((6, shard_rows, columns), F32), struct((1, LANES), F32)],
        "shard_sums",
        3,
        (weights_arrived,),
    )
    table_shard, told = kernel_call(
        told_body,
        [struct((table_rows, LANES), F32), struct((n_dp * n_head, VECTOR_ROWS, LANES), F32)],
        "table_sums",
        1,
        (*parts, squares),
    )
    with jax.named_scope("squares"):
        told = exchange(told, everyone)
    params = (weight_in, first_in, second_in, weight_out, first_out, second_out)
    params += (weight_down, first_down, second_down, vectors, first_vectors, second_vectors)
    params += (bias_table.T, first_table.T, second_table.T)
    *updated, grad_norm = kernel_call(
        lambda *refs: update_body(n_head, n_vectors, *refs),
        [*[struct(p.shape, F32) for p in params], struct((1, LANES), F32)],
        "update",
        3,
        (us, told, shards, shards[3].T, shards[5].T, table_shard, *params),
        (),
        (0,),
        ready=range(2, 21),
        limit=16 << 20,
    )
    updated = updated[:12] + [value.T for value in updated[12:]]
    return (layer_out, input_grad, grad_norm[0, 0], *updated)


def solution(mesh):
    rows = P(("dp", "head"), None)
    square = P(None, "dp", "head")
    across = P("head", "dp")
    thin = P(None, ("dp", "head"))
    table = P("dp", "head")
    return jax.shard_map(
        on_device,
        mesh=mesh,
        in_specs=(rows, rows)
        + (square,) * 3
        + (across,) * 6
        + (thin,) * 3
        + (table,) * 3
        + (P("dp"), P("dp", None))
        + (P("dp", None, None),) * 2
        + (P(None, "dp", None, None),) * 2
        + (P("dp", None, None),) * 2,
        out_specs=(rows, rows, P()) + (square,) * 3 + (across,) * 6 + (thin,) * 3 + (table,) * 3,
        check_vma=False,
    )
```

time: 432 us -> 225 us (0.52)
  waiting for transfers between devices: 95.5 us -> 29.9 us
  local copies, waits for them, and re-layouts: 67.3 us -> 11.3 us
  blocking collectives: 34.9 us -> 0 us
  between operations: 20.2 us -> 2.38 us
  other arithmetic: 19.4 us -> 1.96 us
  matrix products: 6.24 us -> 0 us
    all_to_all x14 -> x5, waiting for transfers between devices: 95.5 us -> 13 us  [exchange(): return lax.all_to_all(value, axis, split_axis=0, concat_axis=0, tiled=True)]
    all_gather x1 -> x0, blocking collectives: 34.9 us -> none  [on_device(): lax.all_gather(weight_in[:3].astype(BF), 'dp', axis=1, tiled=True)]
    all_to_all x14 -> x5, starting transfers between devices: 56.7 us -> 23.1 us  [exchange(): return lax.all_to_all(value, axis, split_axis=0, concat_axis=0, tiled=True)]
    ppermute x0 -> x30, starting transfers between devices: none -> 30.7 us  [the longest x6 10.1 us: far_shards(): lax.ppermute(value, 'dp', dp_pairs(k))]
    unnamed x159 -> x106, local copies, waits for them, and re-layouts: 37.2 us -> 7.8 us
    ppermute x0 -> x30, waiting for transfers between devices: none -> 16.9 us  [the longest x6 4.38 us: far_shards(): lax.ppermute(value, 'dp', dp_pairs(k))]
    reshape x15 -> x0, local copies, waits for them, and re-layouts: 9.88 us -> none  [the longest x1 4.99 us: on_device(): weights_rest.reshape(n_dp, n_head, 3, shard_rows, columns)]
    reduce_sum x14 -> x0, other arithmetic: 6.39 us -> none  [the longest x1 1.48 us: on_device(): jnp.sum(grad_normed_one, axis=0)[None]]
  transfers between devices with their start and end apart: 15 -> 35, of which waited for: 11 -> 11; matrix products, arithmetic and copies ran while one was open for 11% -> 2% of each run, Pallas kernels for 27% -> 47%
where the time goes in v2:
time: 225 us; the launch traced here: 224 us
  Pallas kernels  125 us (56%)
  starting transfers between devices  53.8 us (24%)
  waiting for transfers between devices  29.9 us (13%)
  local copies, waits for them, and re-layouts  11.3 us (5%)
  between operations  2.38 us (1%)
    pallas_call x12, Pallas kernels, kernel_call(): pl.pallas_call(wrapped, out_shape=tuple((shapes[i] for i, _ in flat)), in...  125 us
    all_to_all x5, starting transfers between devices, exchange(): return lax.all_to_all(value, axis, split_axis=0, concat_axis=0, tiled=True)  23.1 us
    all_to_all x5, waiting for transfers between devices, exchange(): return lax.all_to_all(value, axis, split_axis=0, concat_axis=0, tiled=True)  13 us
    ppermute x6, starting transfers between devices, far_shards(): lax.ppermute(value, 'dp', dp_pairs(k))  10.1 us
    unnamed x106, local copies, waits for them, and re-layouts  7.8 us
    ppermute x9, starting transfers between devices, swap(): lax.ppermute(values[r], 'head', [(i, i ^ r) for i in range(n_head)])  5.9 us
  transfers between devices with their start and end apart: 35, of which 11 were waited for; matrix products, arithmetic and copies ran while one was open for 2% of the time, Pallas kernels for 47%

profile of v2, /device:TPU:0, one launch (start us, length us, event | category | flops | bytes accessed | tf_op | source)
XLA Modules:
  0.0 224.3 jit_solution(9150000630151721110)
XLA Ops:
  3.8 5.1 %collective-permute-start.2 = (bf16[3,96,192]{2,1,0:T(8,128)(2,1)S(1)}, bf16[3,96,192]{2,1,0:T(8,128)(2,1)S(1)}, u32[]{:S(2)}, u32[]{:S(2)}) collective-permute-start(bf16[3,96,192]{2,1,0:T(8,128)(2,1)S(1)} %pad_maximum_fusion.3), channel_id=1, source_target_pairs={{0,24},{4,28},{8,16},{12,20},{16,8},{20,12},{24,0},{28,4},{1,25},{... | collective-permute-start | bytes 331784 | tf_op jit(solution)/shard_map/rest_far/ppermute | solution.py:714
  10.2 6.0 %all-to-all-start = ((bf16[8,8,8,128]{3,2,1,0:T(8,128)(2,1)}), bf16[8,8,8,128]{3,2,1,0:T(8,128)(2,1)S(1)}, u32[]{:S(2)}, u32[]{:S(2)}) async-start(bf16[8,8,8,128]{3,2,1,0:T(8,128)(2,1)} %broadcast_in_dim.4), calls=%async_computation | async-start | bytes 262144 | tf_op jit(solution)/shard_map/table_all/all_to_all | solution.py:645
  19.1 4.4 %collective-permute-done.1 = bf16[3,96,192]{2,1,0:T(8,128)(2,1)S(1)} collective-permute-done((bf16[3,96,192]{2,1,0:T(8,128)(2,1)S(1)}, bf16[3,96,192]{2,1,0:T(8,128)(2,1)S(1)}, u32[]{:S(2)}, u32[]{:S(2)}) %collective-permute-start.1) | collective-permute-done | bytes 110624 | tf_op jit(solution)/shard_map/rest_far/ppermute | solution.py:714
  24.6 2.5 %collective-permute-start.7 = (bf16[3,96,192]{2,1,0:T(8,128)(2,1)S(1)}, bf16[3,96,192]{2,1,0:T(8,128)(2,1)S(1)}, u32[]{:S(2)}, u32[]{:S(2)}) collective-permute-start(bf16[3,96,192]{2,1,0:T(8,128)(2,1)S(1)} %slice.23), channel_id=1, source_target_pairs={{0,24},{4,28},{8,16},{12,20},{16,8},{20,12},{24,0},{28,4},{1,25},{... | collective-permute-start | bytes 331784 | tf_op jit(solution)/shard_map/qkv_far/ppermute | solution.py:714
  29.8 4.3 %all-to-all-start.1 = ((f32[32,16,128]{2,1,0:T(8,128)}), f32[32,16,128]{2,1,0:T(8,128)S(1)}, u32[]{:S(2)}, u32[]{:S(2)}) async-start(f32[32,16,128]{2,1,0:T(8,128)} %broadcast_in_dim.5), calls=%async_computation.1 | async-start | bytes 524288 | tf_op jit(solution)/shard_map/vectors_all/all_to_all | solution.py:645
  36.1 13.2 %pair_bias.2 = (f32[8,2,64,128]{3,2,1,0:T(8,128)}, f32[8,2,64,128]{3,2,1,0:T(8,128)}) custom-call(bf16[512,128]{1,0:T(8,128)(2,1)} %bitcast.60, s32[4,64,64]{2,1,0:T(8,128)} %refs_1_.5, s32[5,4,64,64]{3,2,1,0:T(8,128)} %refs_2_.5, s32[4,64,64]{2,1,0:T(8,128)} %refs_3_.5, s32[1,256,256]{2,1,0:T(8,128)} %refs_5_.7, s32[5,1,256,256]{3,2,1,0:T(8,128)} %refs_6_.8, ...), custom_call_target="tpu_custom_call" | custom-call | flops 12000000000 | bytes 1048576 | tf_op jit(solution)/shard_map/pair_bias/pallas_call | solution.py:114
  49.5 2.9 %collective-permute-done.4 = bf16[4,3,96,192]{3,2,1,0:T(8,128)(2,1)S(1)} collective-permute-done((bf16[4,3,96,192]{3,2,1,0:T(8,128)(2,1)S(1)}, bf16[4,3,96,192]{3,2,1,0:T(8,128)(2,1)S(1)}, u32[]{:S(2)}, u32[]{:S(2)}) %collective-permute-start.4) | collective-permute-done | bytes 442400 | tf_op jit(solution)/shard_map/rest_near/ppermute | solution.py:718
  56.3 18.4 %pair_bias.3.refs_11_ = f32[8,2,192,128]{3,2,1,0:T(8,128)} custom-call(bf16[512,128]{1,0:T(8,128)(2,1)} %bitcast.61, s32[1,256,256]{2,1,0:T(8,128)} %refs_5_.7, s32[5,1,256,256]{3,2,1,0:T(8,128)} %refs_6_.8, s32[1,256,256]{2,1,0:T(8,128)} %refs_7_.2), custom_call_target="tpu_custom_call" | custom-call | flops 20000000000 | bytes 1048576 | tf_op jit(solution)/shard_map/pair_bias/pallas_call | solution.py:114
  76.1 12.0 %attend_forward.1 = (bf16[512,768]{1,0:T(8,128)(2,1)}, bf16[3,512,192]{2,1,0:T(8,128)(2,1)}, f32[8,256,256]{2,1,0:T(8,128)}, f32[8,2,128,128]{3,2,1,0:T(8,128)},...) custom-call(bf16[2,128,768]{2,1,0:T(8,128)(2,1)} %copy-done.19, ...), custom_call_target="tpu_custom_call" | custom-call | flops 12000000000 | bytes 1048576 | tf_op jit(solution)/shard_map/attend_forward/pallas_call | solution.py:114
  91.0 2.6 %collective-permute-done.14.refs_2_ = bf16[128,192]{1,0:T(8,128)(2,1)S(1)} collective-permute-done((bf16[128,192]{1,0:T(8,128)(2,1)}, bf16[128,192]{1,0:T(8,128)(2,1)S(1)}, u32[]{:S(2)}, u32[]{:S(2)}) %collective-permute-start.14) | collective-permute-done | bytes 49184 | tf_op jit(solution)/shard_map/mixed_rows/ppermute | solution.py:655
  95.3 8.0 %feed_forward.1 = (bf16[128,768]{1,0:T(8,128)(2,1)}, f32[128,768]{1,0:T(8,128)}, f32[4,768]{1,0:T(4,128)}, f32[4,192]{1,0:T(4,128)}, bf16[2,128,768]{2,1,0:T(8,1...) custom-call(bf16[128,192]{1,0:T(8,128)(2,1)} %get-tuple-element.151., ...), custom_call_target="tpu_custom_call" | custom-call | flops 6000000000 | bytes 1048576 | tf_op jit(solution)/shard_map/feed_forward/pallas_call | solution.py:114
  106.4 3.6 %all-to-all-start.2 = ((bf16[4,128,512]{2,1,0:T(8,128)(2,1)}), bf16[4,128,512]{2,1,0:T(8,128)(2,1)S(1)}, u32[]{:S(2)}, u32[]{:S(2)}) async-start(bf16[4,128,512]{2,1,0:T(8,128)(2,1)} %get-tuple-element.161), calls=%async_computation.2 | async-start | bytes 1048576 | tf_op jit(solution)/shard_map/act_pre/all_to_all | solution.py:645
  110.7 14.5 %attend_backward.1 = (f32[1024,128]{1,0:T(8,128)}, f32[4096,128]{1,0:T(8,128)}, bf16[3,512,192]{2,1,0:T(8,128)(2,1)}, f32[2,4,192]{2,1,0:T(4,128)}, bf16[128,768...) custom-call(bf16[128,192]{1,0:T(8,128)(2,1)} %get-tuple-element.163.refs_0_, ...), custom_call_target="tpu_custom_call" | custom-call | flops 14000000000 | bytes 1048576 | tf_op jit(solution)/shard_map/attend_backward/pallas_call | solution.py:114
  127.9 6.3 %weight_grads.1 = bf16[8,6,96,192]{3,2,1,0:T(8,128)(2,1)} custom-call(bf16[2,128,768]{2,1,0:T(8,128)(2,1)} %copy-done.19, bf16[2,128,768]{2,1,0:T(8,128)(2,1)} %copy-done.30, bf16[2,128,768]{2,1,0:T(8,128)(2,1)} %copy-done.29, bf16[2,128,768]{2,1,0:T(8,128)(2,1)} %copy-done.31, bf16[128,192]{1,0:T(8,128)(2,1)} %get-tuple-element.151.refs_0_.refs_4_, ...), custom_call_target="tpu_custom_call" | custom-call | flops 6000000000 | bytes 1048576 | tf_op jit(solution)/shard_map/weight_grads/pallas_call | solution.py:114
  134.2 5.2 %all-to-all-start.3 = ((bf16[8,6,96,192]{3,2,1,0:T(8,128)(2,1)}), bf16[8,6,96,192]{3,2,1,0:T(8,128)(2,1)}, u32[]{:S(2)}, u32[]{:S(2)}) async-start(bf16[8,6,96,192]{3,2,1,0:T(8,128)(2,1)} %weight_grads.1), calls=%async_computation.3 | async-start | bytes 4718592 | tf_op jit(solution)/shard_map/weight_grads/all_to_all | solution.py:645
  141.6 39.8 %table_scatter.1.refs_11_ = bf16[512,128]{1,0:T(8,128)(2,1)} custom-call(f32[1024,128]{1,0:T(8,128)} %get-tuple-element.180.refs_0_, s32[4,64,64]{2,1,0:T(8,128)} %refs_1_.5, s32[5,4,64,64]{3,2,1,0:T(8,128)} %refs_2_.5, s32[4,64,64]{2,1,0:T(8,128)} %refs_3_.5, f32[4096,128]{1,0:T(8,128)} %get-tuple-element.181.refs_4_, s32[1,256,256]{2,1,0:T(8,128)} %refs_5_.7, ...), custom_call_target="tpu_custom_call" | custom-call | flops 40000000000 | bytes 1048576 | tf_op jit(solution)/shard_map/table_scatter/pallas_call | solution.py:114
  182.2 3.4 %input_grad.1 = (bf16[128,768]{1,0:T(8,128)(2,1)}, bf16[4,80,128]{2,1,0:T(8,128)(2,1)}, bf16[4,80,128]{2,1,0:T(8,128)(2,1)}) custom-call(bf16[128,768]{1,0:T(8,128)(2,1)} %get-tuple-element.186.refs_0_, bf16[128,768]{1,0:T(8,128)(2,1)} %copy-done.38, bf16[128,768]{1,0:T(8,128)(2,1)} %copy-done.39, bf16[128,768]{1,0:T(8,128)(2,1)} %copy-done.40, ...), custom_call_target="tpu_custom_call" | custom-call | flops 3000000000 | bytes 1048576 | tf_op jit(solution)/shard_map/input_grad/pallas_call | solution.py:114
  187.6 3.1 %collective-permute-done.26.refs_1_ = bf16[4,80,128]{2,1,0:T(8,128)(2,1)S(1)} collective-permute-done((bf16[4,80,128]{2,1,0:T(8,128)(2,1)}, bf16[4,80,128]{2,1,0:T(8,128)(2,1)S(1)}, u32[]{:S(2)}, u32[]{:S(2)}) %collective-permute-start.26) | collective-permute-done | bytes 81952 | tf_op jit(solution)/shard_map/table_inner/ppermute | solution.py:904
  190.7 3.3 %all-to-all-done.3.refs_0_ = bf16[8,6,96,192]{3,2,1,0:T(8,128)(2,1)} async-done(((bf16[8,6,96,192]{3,2,1,0:T(8,128)(2,1)}), bf16[8,6,96,192]{3,2,1,0:T(8,128)(2,1)}, u32[]{:S(2)}, u32[]{:S(2)}) %all-to-all-start.3) | async-done | bytes 1769504 | tf_op jit(solution)/shard_map/weight_grads/all_to_all | solution.py:645
  195.7 2.8 %collective-permute-start.28 = (bf16[80,128]{1,0:T(8,128)(2,1)}, bf16[80,128]{1,0:T(8,128)(2,1)S(1)}, u32[]{:S(2)}, u32[]{:S(2)}) collective-permute-start(bf16[80,128]{1,0:T(8,128)(2,1)} %get-tuple-element.203), channel_id=1, source_target_pairs={{0,16},{4,20},{8,24},{12,28},{16,0},{20,4},{24,8},{28,12},{1,17},{... | collective-permute-start | bytes 61448 | tf_op jit(solution)/shard_map/table_outer/ppermute | solution.py:915
  200.0 3.1 %shard_sums.1 = (f32[6,96,192]{2,1,0:T(8,128)}, f32[1,128]{1,0:T(1,128)}) custom-call(bf16[8,6,96,192]{3,2,1,0:T(8,128)(2,1)} %all-to-all-done.3.refs_0_), custom_call_target="tpu_custom_call" | custom-call | flops 3000000000 | bytes 1048576 | tf_op jit(solution)/shard_map/shard_sums/pallas_call | solution.py:114
  206.9 3.9 %all-to-all-start.4 = ((f32[32,16,128]{2,1,0:T(8,128)}), f32[32,16,128]{2,1,0:T(8,128)S(1)}, u32[]{:S(2)}, u32[]{:S(2)}) async-start(f32[32,16,128]{2,1,0:T(8,128)} %get-tuple-element.207), calls=%async_computation.4 | async-start | bytes 524288 | tf_op jit(solution)/shard_map/squares/all_to_all | solution.py:645
  212.8 8.6 %all-to-all-done.4.refs_1_ = f32[32,16,128]{2,1,0:T(8,128)S(1)} async-done(((f32[32,16,128]{2,1,0:T(8,128)}), f32[32,16,128]{2,1,0:T(8,128)S(1)}, u32[]{:S(2)}, u32[]{:S(2)}) %all-to-all-start.4) | async-done | bytes 262176 | tf_op jit(solution)/shard_map/squares/all_to_all | solution.py:645
  221.5 2.7 %update.1 = (f32[4,96,192]{2,1,0:T(8,128)}, f32[4,96,192]{2,1,0:T(8,128)}, f32[4,96,192]{2,1,0:T(8,128)}, f32[192,96]{1,0:T(8,128)}, f32[192,96]{1,0:T(8,128)}, ...) custom-call(s32[2]{0:T(128)S(1)} %copy-done.16, ...), custom_call_target="tpu_custom_call" | custom-call | flops 3000000000 | bytes 1048576 | tf_op jit(solution)/shard_map/update/pallas_call | solution.py:114
  (180 shorter events, 42.0 us)
Async XLA Ops:
  3.8 15.3 %collective-permute-start.2 = (bf16[3,96,192]{2,1,0:T(8,128)(2,1)S(1)}, bf16[3,96,192]{2,1,0:T(8,128)(2,1)S(1)}, u32[]{:S(2)}, u32[]{:S(2)}) collective-permute-start(bf16[3,96,192]{2,1,0:T(8,128)(2,1)S(1)} %pad_maximum_fusion.3), channel_id=1, source_target_pairs={{0,24},{4,28},{8,16},{12,20},{16,8},{20,12},{24,0},{28,4},{1,25},{... | collective-permute-start | bytes 331784 | tf_op jit(solution)/shard_map/rest_far/ppermute | solution.py:714
  8.9 14.6 %collective-permute-start.1 = (bf16[3,96,192]{2,1,0:T(8,128)(2,1)S(1)}, bf16[3,96,192]{2,1,0:T(8,128)(2,1)S(1)}, u32[]{:S(2)}, u32[]{:S(2)}) collective-permute-start(bf16[3,96,192]{2,1,0:T(8,128)(2,1)S(1)} %pad_maximum_fusion.3), channel_id=1, source_target_pairs={{0,16},{4,20},{8,24},{12,28},{16,0},{20,4},{24,8},{28,12},{1,17},{... | collective-permute-start | bytes 331784 | tf_op jit(solution)/shard_map/rest_far/ppermute | solution.py:714
  8.9 14.6 %collective-permute-start = (bf16[3,96,192]{2,1,0:T(8,128)(2,1)S(1)}, bf16[3,96,192]{2,1,0:T(8,128)(2,1)S(1)}, u32[]{:S(2)}, u32[]{:S(2)}) collective-permute-start(bf16[3,96,192]{2,1,0:T(8,128)(2,1)S(1)} %pad_maximum_fusion.3), channel_id=1, source_target_pairs={{0,8},{4,12},{8,0},{12,4},{16,24},{20,28},{24,16},{28,20},{1,9},{5... | collective-permute-start | bytes 331784 | tf_op jit(solution)/shard_map/rest_far/ppermute | solution.py:714
  10.2 14.4 %all-to-all-start = ((bf16[8,8,8,128]{3,2,1,0:T(8,128)(2,1)}), bf16[8,8,8,128]{3,2,1,0:T(8,128)(2,1)S(1)}, u32[]{:S(2)}, u32[]{:S(2)}) async-start(bf16[8,8,8,128]{3,2,1,0:T(8,128)(2,1)} %broadcast_in_dim.4), calls=%async_computation | async-start | bytes 262144 | tf_op jit(solution)/shard_map/table_all/all_to_all | solution.py:645
  16.3 33.2 %collective-permute-start.3 = (bf16[2,128,768]{2,1,0:T(8,128)(2,1)S(1)}, bf16[2,128,768]{2,1,0:T(8,128)(2,1)S(1)}, u32[]{:S(2)}, u32[]{:S(2)}) collective-permute-start(bf16[2,128,768]{2,1,0:T(8,128)(2,1)S(1)} %pad_maximum_fusion.2.refs_0_), channel_id=1, source_target_pairs={{0,2},{1,3},{2,0},{3,1},{4,6},{5,7},{6,4},{7,5},{8,10},{9,11},{10,... | collective-permute-start | bytes 1179656 | tf_op jit(solution)/shard_map/rows_far/ppermute | solution.py:721
  24.6 24.7 %collective-permute-start.7 = (bf16[3,96,192]{2,1,0:T(8,128)(2,1)S(1)}, bf16[3,96,192]{2,1,0:T(8,128)(2,1)S(1)}, u32[]{:S(2)}, u32[]{:S(2)}) collective-permute-start(bf16[3,96,192]{2,1,0:T(8,128)(2,1)S(1)} %slice.23), channel_id=1, source_target_pairs={{0,24},{4,28},{8,16},{12,20},{16,8},{20,12},{24,0},{28,4},{1,25},{... | collective-permute-start | bytes 331784 | tf_op jit(solution)/shard_map/qkv_far/ppermute | solution.py:714
  27.2 22.3 %collective-permute-start.6 = (bf16[3,96,192]{2,1,0:T(8,128)(2,1)S(1)}, bf16[3,96,192]{2,1,0:T(8,128)(2,1)S(1)}, u32[]{:S(2)}, u32[]{:S(2)}) collective-permute-start(bf16[3,96,192]{2,1,0:T(8,128)(2,1)S(1)} %slice.23), channel_id=1, source_target_pairs={{0,16},{4,20},{8,24},{12,28},{16,0},{20,4},{24,8},{28,12},{1,17},{... | collective-permute-start | bytes 331784 | tf_op jit(solution)/shard_map/qkv_far/ppermute | solution.py:714
  27.2 22.3 %collective-permute-start.5 = (bf16[3,96,192]{2,1,0:T(8,128)(2,1)S(1)}, bf16[3,96,192]{2,1,0:T(8,128)(2,1)S(1)}, u32[]{:S(2)}, u32[]{:S(2)}) collective-permute-start(bf16[3,96,192]{2,1,0:T(8,128)(2,1)S(1)} %slice.23), channel_id=1, source_target_pairs={{0,8},{4,12},{8,0},{12,4},{16,24},{20,28},{24,16},{28,20},{1,9},{5... | collective-permute-start | bytes 331784 | tf_op jit(solution)/shard_map/qkv_far/ppermute | solution.py:714
  29.8 22.7 %all-to-all-start.1 = ((f32[32,16,128]{2,1,0:T(8,128)}), f32[32,16,128]{2,1,0:T(8,128)S(1)}, u32[]{:S(2)}, u32[]{:S(2)}) async-start(f32[32,16,128]{2,1,0:T(8,128)} %broadcast_in_dim.5), calls=%async_computation.1 | async-start | bytes 524288 | tf_op jit(solution)/shard_map/vectors_all/all_to_all | solution.py:645
  34.2 18.2 %collective-permute-start.4 = (bf16[4,3,96,192]{3,2,1,0:T(8,128)(2,1)S(1)}, bf16[4,3,96,192]{3,2,1,0:T(8,128)(2,1)S(1)}, u32[]{:S(2)}, u32[]{:S(2)}) collective-permute-start(bf16[4,3,96,192]{3,2,1,0:T(8,128)(2,1)S(1)} %pad_maximum_fusion), channel_id=1, source_target_pairs={{0,4},{4,0},{8,12},{12,8},{16,20},{20,16},{24,28},{28,24},{1,5},{5... | collective-permute-start | bytes 1327112 | tf_op jit(solution)/shard_map/rest_near/ppermute | solution.py:718
  49.4 25.4 %collective-permute-start.9 = (bf16[2,128,768]{2,1,0:T(8,128)(2,1)S(1)}, bf16[2,128,768]{2,1,0:T(8,128)(2,1)S(1)}, u32[]{:S(2)}, u32[]{:S(2)}) collective-permute-start(bf16[2,128,768]{2,1,0:T(8,128)(2,1)S(1)} %pad_maximum_fusion.2.refs_0_), channel_id=1, source_target_pairs={{0,1},{1,0},{2,3},{3,2},{4,5},{5,4},{6,7},{7,6},{8,9},{9,8},{10,11... | collective-permute-start | bytes 1179656 | tf_op jit(solution)/shard_map/rows_near/ppermute | solution.py:721
  53.1 35.0 %collective-permute-start.12 = (bf16[8,3,96,192]{3,2,1,0:T(8,128)(2,1)S(1)}, bf16[8,3,96,192]{3,2,1,0:T(8,128)(2,1)S(1)}, u32[]{:S(2)}, u32[]{:S(2)}) collective-permute-start(bf16[8,3,96,192]{3,2,1,0:T(8,128)(2,1)S(1)} %constant_dynamic-update-slice_fusion.2.refs_9_), channel_id=1, source_target_pairs={{0,2},{1,3},{2,0},{3,1},{4,6},{5,7},{6,4},{7,5},{8,10},{9,11},{10,... | collective-permute-start | bytes 2654216 | tf_op jit(solution)/shard_map/rest_far_head/ppermute | solution.py:721
  54.6 33.5 %collective-permute-start.11 = (bf16[8,3,96,192]{3,2,1,0:T(8,128)(2,1)S(1)}, bf16[8,3,96,192]{3,2,1,0:T(8,128)(2,1)S(1)}, u32[]{:S(2)}, u32[]{:S(2)}) collective-permute-start(bf16[8,3,96,192]{3,2,1,0:T(8,128)(2,1)S(1)} %constant_dynamic-update-slice_fusion.2.refs_9_), channel_id=1, source_target_pairs={{0,1},{1,0},{2,3},{3,2},{4,5},{5,4},{6,7},{7,6},{8,9},{9,8},{10,11... | collective-permute-start | bytes 2654216 | tf_op jit(solution)/shard_map/rest_near_head/ppermute | solution.py:721
  54.6 20.1 %collective-permute-start.10 = (bf16[2,128,768]{2,1,0:T(8,128)(2,1)S(1)}, bf16[2,128,768]{2,1,0:T(8,128)(2,1)S(1)}, u32[]{:S(2)}, u32[]{:S(2)}) collective-permute-start(bf16[2,128,768]{2,1,0:T(8,128)(2,1)S(1)} %collective-permute-done.3.refs_2_), channel_id=1, source_target_pairs={{0,1},{1,0},{2,3},{3,2},{4,5},{5,4},{6,7},{7,6},{8,9},{9,8},{10,11... | collective-permute-start | bytes 1179656 | tf_op jit(solution)/shard_map/rows_near/ppermute | solution.py:721
  55.3 19.5 %collective-permute-start.8 = (bf16[4,3,96,192]{3,2,1,0:T(8,128)(2,1)S(1)}, bf16[4,3,96,192]{3,2,1,0:T(8,128)(2,1)S(1)}, u32[]{:S(2)}, u32[]{:S(2)}) collective-permute-start(bf16[4,3,96,192]{3,2,1,0:T(8,128)(2,1)S(1)} %pad_maximum_fusion.1), channel_id=1, source_target_pairs={{0,4},{4,0},{8,12},{12,8},{16,20},{20,16},{24,28},{28,24},{1,5},{5... | collective-permute-start | bytes 1327112 | tf_op jit(solution)/shard_map/qkv_near/ppermute | solution.py:718
  105.2 20.1 %collective-permute-start.21 = (bf16[2,128,768]{2,1,0:T(8,128)(2,1)}, bf16[2,128,768]{2,1,0:T(8,128)(2,1)S(1)}, u32[]{:S(2)}, u32[]{:S(2)}) collective-permute-start(bf16[2,128,768]{2,1,0:T(8,128)(2,1)} %get-tuple-element.171.refs_12_), channel_id=1, source_target_pairs={{0,2},{1,3},{2,0},{3,1},{4,6},{5,7},{6,4},{7,5},{8,10},{9,11},{10,... | collective-permute-start | bytes 1179656 | tf_op jit(solution)/shard_map/normed_grad/ppermute | solution.py:843
  106.3 19.0 %collective-permute-start.20 = (bf16[2,128,768]{2,1,0:T(8,128)(2,1)}, bf16[2,128,768]{2,1,0:T(8,128)(2,1)S(1)}, u32[]{:S(2)}, u32[]{:S(2)}) collective-permute-start(bf16[2,128,768]{2,1,0:T(8,128)(2,1)} %get-tuple-element.171.refs_12_), channel_id=1, source_target_pairs={{0,1},{1,0},{2,3},{3,2},{4,5},{5,4},{6,7},{7,6},{8,9},{9,8},{10,11... | collective-permute-start | bytes 1179656 | tf_op jit(solution)/shard_map/normed_grad/ppermute | solution.py:843
  106.4 19.4 %all-to-all-start.2 = ((bf16[4,128,512]{2,1,0:T(8,128)(2,1)}), bf16[4,128,512]{2,1,0:T(8,128)(2,1)S(1)}, u32[]{:S(2)}, u32[]{:S(2)}) async-start(bf16[4,128,512]{2,1,0:T(8,128)(2,1)} %get-tuple-element.161), calls=%async_computation.2 | async-start | bytes 1048576 | tf_op jit(solution)/shard_map/act_pre/all_to_all | solution.py:645
  134.2 59.7 %all-to-all-start.3 = ((bf16[8,6,96,192]{3,2,1,0:T(8,128)(2,1)}), bf16[8,6,96,192]{3,2,1,0:T(8,128)(2,1)}, u32[]{:S(2)}, u32[]{:S(2)}) async-start(bf16[8,6,96,192]{3,2,1,0:T(8,128)(2,1)} %weight_grads.1), calls=%async_computation.3 | async-start | bytes 4718592 | tf_op jit(solution)/shard_map/weight_grads/all_to_all | solution.py:645
  139.5 41.9 %collective-permute-start.23 = (bf16[128,768]{1,0:T(8,128)(2,1)S(1)}, bf16[128,768]{1,0:T(8,128)(2,1)S(1)}, u32[]{:S(2)}, u32[]{:S(2)}) collective-permute-start(bf16[128,768]{1,0:T(8,128)(2,1)S(1)} %copy-done.37), channel_id=1, source_target_pairs={{0,1},{1,0},{2,3},{3,2},{4,5},{5,4},{6,7},{7,6},{8,9},{9,8},{10,11... | collective-permute-start | bytes 589832 | tf_op jit(solution)/shard_map/grad_normed_one/ppermute | solution.py:655
  139.6 41.8 %collective-permute-start.24 = (bf16[128,768]{1,0:T(8,128)(2,1)S(1)}, bf16[128,768]{1,0:T(8,128)(2,1)S(1)}, u32[]{:S(2)}, u32[]{:S(2)}) collective-permute-start(bf16[128,768]{1,0:T(8,128)(2,1)S(1)} %copy-done.36), channel_id=1, source_target_pairs={{0,2},{1,3},{2,0},{3,1},{4,6},{5,7},{6,4},{7,5},{8,10},{9,11},{10,... | collective-permute-start | bytes 589832 | tf_op jit(solution)/shard_map/grad_normed_one/ppermute | solution.py:655
  141.5 40.0 %collective-permute-start.25 = (bf16[128,768]{1,0:T(8,128)(2,1)S(1)}, bf16[128,768]{1,0:T(8,128)(2,1)S(1)}, u32[]{:S(2)}, u32[]{:S(2)}) collective-permute-start(bf16[128,768]{1,0:T(8,128)(2,1)S(1)} %copy-done.35), channel_id=1, source_target_pairs={{0,3},{1,2},{2,1},{3,0},{4,7},{5,6},{6,5},{7,4},{8,11},{9,10},{10,... | collective-permute-start | bytes 589832 | tf_op jit(solution)/shard_map/grad_normed_one/ppermute | solution.py:655
  195.6 7.6 %collective-permute-start.27 = (bf16[80,128]{1,0:T(8,128)(2,1)}, bf16[80,128]{1,0:T(8,128)(2,1)S(1)}, u32[]{:S(2)}, u32[]{:S(2)}) collective-permute-start(bf16[80,128]{1,0:T(8,128)(2,1)} %get-tuple-element.202), channel_id=1, source_target_pairs={{0,8},{4,12},{8,0},{12,4},{16,24},{20,28},{24,16},{28,20},{1,9},{5... | collective-permute-start | bytes 61448 | tf_op jit(solution)/shard_map/table_outer/ppermute | solution.py:915
  206.9 14.5 %all-to-all-start.4 = ((f32[32,16,128]{2,1,0:T(8,128)}), f32[32,16,128]{2,1,0:T(8,128)S(1)}, u32[]{:S(2)}, u32[]{:S(2)}) async-start(f32[32,16,128]{2,1,0:T(8,128)} %get-tuple-element.207), calls=%async_computation.4 | async-start | bytes 524288 | tf_op jit(solution)/shard_map/squares/all_to_all | solution.py:645
  (62 other events, 464.8 us)

commit v3 on v2

--- a/solution.py
+++ b/solution.py
@@ -30,6 +30,9 @@
 VECTOR_ROWS = 16
 BIG_QUARTERS = (1, 3)
 BIG_PARTS = len(BIG_QUARTERS)
+MESSAGE_ROWS = 8
+PIECES = 3
+PIECE_ROWS = 16
 FIXED = 8192.0
 NOWHERE = 4095
 SCALE = HEAD_DIM**-0.5
@@ -217,7 +220,7 @@
     each_block(big_block, big, first_block, count, big[0].shape[2] // LANES, 1, step(store_big))
 
 
-def scatter_body(need, done, small_grads, sd, sp, sl, big_grads, bd, bp, bl, out, total):
+def scatter_body(need, done, small_grads, sd, sp, sl, big_grads, bd, bp, bl, me, vector_rows, parcel, total):
     total[...] = jnp.zeros_like(total)
     sub = lax.broadcasted_iota(jnp.int32, (2 * SUB, LANES), 0)
     low_pattern = [(sub + 2 * SUB * k).astype(F32).astype(BF) for k in range(LANES // (2 * SUB))]
@@ -259,10 +262,24 @@
 
     need(0, 1, 2, 3)
     narrow, width = sd.shape[1], bd.shape[1]
-    each_block(small_block, (sd, sp, sl), 0, narrow // SUB, sd.shape[0] // 2, 2, step(small_grads, narrow))
+    each_block(small_block, (sd, sp, sl), 0, narrow // SUB, sd.shape[0] // 2, 4, step(small_grads, narrow))
     need(4, 5, 6, 7)
-    each_block(big_block, (bd, bp, bl), 0, width // SUB, width // LANES, 2, step(big_grads, width))
-    out[...] = total[...].T.astype(BF)
+    each_block(big_block, (bd, bp, bl), 0, width // SUB, width // LANES, 4, step(big_grads, width))
+    need(9)
+    inner, outer, height, _ = parcel.shape
+    height -= VECTOR_ROWS
+    parcel[:, :, :VECTOR_ROWS, :] = vector_rows[...]
+    table = total[...].T.astype(BF)
+    for d in range(inner * outer):
+        at = me[1] ^ d
+        parcel[at % inner, at // inner, VECTOR_ROWS:, :] = table[d * height : (d + 1) * height]
+
+
+def attend_matrix(ref, k, model):
+    if ref.shape[1] == model:
+        return ref[k]
+    rows = model // ref.shape[0]
+    return ref[:, k * rows : (k + 1) * rows, :].reshape(model, ref.shape[2])
 
 
 def whole_matrix(ref, k):
@@ -295,17 +312,23 @@
     return pl.ds(pl.multiple_of((me[0] ^ r) * rows, rows), rows)
 
 
-def forward_body(n_head, need, done, *refs):
+def forward_body(n_head, vector_row, need, done, *refs):
     rows_in, refs = refs[:n_head], refs[n_head:]
-    me, big_counts, small_counts, pieces, weights, small_bias = refs[:6]
-    big_bias, refs = refs[6 : 6 + BIG_PARTS], refs[6 + BIG_PARTS :]
+    me, big_counts, small_counts, weights, small_bias = refs[:5]
+    big_bias, refs = refs[5 : 5 + BIG_PARTS], refs[5 + BIG_PARTS :]
+    pieces = weights
+    if vector_row == 0:
+        pieces, refs = refs[0], refs[1:]
     normed, qkv, big_probs, small_probs, vectors, hidden_bias = refs[:6]
-    mixed_out, mixed = refs[6 : 6 + n_head], refs[6 + n_head]
+    mixed_out, (mixed, flat, stack) = refs[6 : 6 + n_head], refs[6 + n_head :]
     block = rows_in[0].shape[1]
     need(*range(n_head), n_head + 3)
+    if vector_row == 0:
+        need(n_head + 5 + BIG_PARTS)
     n_vectors, size = vectors.shape[0], vectors.shape[1] // pieces.shape[0]
-    for piece in range(pieces.shape[0]):
-        vectors[:, piece * size : (piece + 1) * size] = pieces[piece, :n_vectors, :size]
+    for d in range(pieces.shape[0]):
+        parts = [pieces[d, pl.ds(vector_row + p * PIECE_ROWS, PIECE_ROWS), 0:size].astype(F32) for p in range(PIECES)]
+        vectors[:, d * size : (d + 1) * size] = sum(parts[1:], parts[0])[:n_vectors]
     heads, width = big_probs.shape[:2]
     pairs, wide = small_probs.shape[1:3]
     narrow = wide // 2
@@ -322,15 +345,13 @@
         xhat, _ = norm_parts(rows_in[r][0].astype(F32))
         normed[peer_block(me, r, block), :] = (xhat * vectors[0:1, :] + vectors[1:2, :]).astype(BF)
     done(0, 4, 5)
-    need(n_head + 4)
     for k in range(3):
-        value = dot(normed[...], whole_matrix(weights, k), NN)
+        value = dot(normed[...], attend_matrix(weights, k, normed.shape[1]), NN)
         if k != 1:
             value = value + biases[k // 2]
         qkv[k] = value.astype(BF)
     done(1)
-    need(*range(n_head + 5, n_head + 6 + BIG_PARTS))
-    mixed[...] = jnp.zeros_like(mixed)
+    need(*range(n_head + 4, n_head + 5 + BIG_PARTS))
     big_live = lax.broadcasted_iota(jnp.int32, (1, width), 1) < big_counts[0]
     small_live = []
     row = lax.broadcasted_iota(jnp.int32, (wide, wide), 0)
@@ -340,36 +361,43 @@
         second = (row >= narrow) & (lane >= narrow) & (lane < narrow + small_counts[0, 2 * pair + 1])
         small_live.append(first | second)
 
-    def attend(span, extra, live, mine):
-        query = jnp.where(mine, qkv[0, span, :], 0.0)
-        scores = jnp.where(live, dot(query, qkv[1, span, :], NT) * SCALE + extra, NEGATIVE_FILL)
-        power = jnp.exp(scores - jnp.max(scores, axis=-1, keepdims=True))
-        probs = power * (1.0 / jnp.sum(power, axis=-1, keepdims=True))
-        out = dot(probs.astype(BF), qkv[2, span, :], NN)
-        mixed[span, :] = jnp.where(mine, out.astype(BF), mixed[span, :])
-        return probs
-
-    def big_heads(at, carry):
-        for head in (2 * at, 2 * at + 1):
-            extra = jnp.concatenate(
-                [jnp.concatenate([part[head, half] for part in big_bias], axis=0) for half in range(halves)], axis=1
-            )
-            big_probs[head] = attend(slice(0, width), extra, big_live, head_lanes(head, columns))
-        return carry
-
-    lax.fori_loop(0, heads // 2, big_heads, 0)
+    def attend(span, extra, live, store):
+        for head in range(heads):
+            mine = head_lanes(head, columns)
+            query = jnp.where(mine, qkv[0, span, :], 0.0)
+            size = query.shape[0]
+            scores = dot(query, qkv[1, span, :], NT) * SCALE + extra(head)
+            scores = jnp.where(live, scores, NEGATIVE_FILL)
+            power = jnp.exp(scores - jnp.max(scores, axis=-1, keepdims=True))
+            probs = power * (1.0 / jnp.sum(power, axis=-1, keepdims=True))
+            store(head, probs)
+            rows = slice(head * size, (head + 1) * size)
+            flat[:size, rows] = probs.astype(BF)
+            stack[rows, :] = jnp.where(mine, qkv[2, span, :], 0.0)
+        every = slice(0, heads * size)
+        mixed[span, :] = dot(flat[:size, every], stack[every, :], NN).astype(BF)
+
+    def big_extra(head):
+        return jnp.concatenate(
+            [jnp.concatenate([part[head, half] for part in big_bias], axis=0) for half in range(halves)], axis=1
+        )
+
+    def store_big(head, probs):
+        big_probs[head] = probs
+
+    attend(slice(0, width), big_extra, big_live, store_big)
     done(2)
-
-    def small_heads(at, carry):
-        for head in (2 * at, 2 * at + 1):
-            for pair in range(pairs):
-                extra = small_bias[head, pair]
-                extra = jnp.concatenate([extra, extra], axis=0)
-                span = slice(width + pair * wide, width + (pair + 1) * wide)
-                small_probs[head, pair] = attend(span, extra, small_live[pair], head_lanes(head, columns))
-        return carry
-
-    lax.fori_loop(0, heads // 2, small_heads, 0)
+    for pair in range(pairs):
+
+        def small_extra(head, pair=pair):
+            extra = small_bias[head, pair]
+            return jnp.concatenate([extra, extra], axis=0)
+
+        def store_small(head, probs, pair=pair):
+            small_probs[head, pair] = probs
+
+        span = slice(width + pair * wide, width + (pair + 1) * wide)
+        attend(span, small_extra, small_live[pair], store_small)
     done(3)
     for r in range(n_head):
         mixed_out[r][...] = mixed[peer_block(me, r, block), :]
@@ -388,7 +416,7 @@
     need(*range(n_head), n_head + 1, n_head + 2)
     grads_in, refs = refs[:n_head], refs[n_head:]
     me, qkv, small_probs, big_probs, weights, small_rows, big_rows, dqkv, column_sums = refs[:9]
-    rows_out, (grad_heads,) = refs[9 : 9 + n_head], refs[9 + n_head :]
+    rows_out, (grad_heads, tall, flat, stacks) = refs[9 : 9 + n_head], refs[9 + n_head :]
     heads, width = big_probs.shape[:2]
     pairs, wide = small_probs.shape[1:3]
     narrow = wide // 2
@@ -397,45 +425,47 @@
     block = grads_in[0].shape[0]
     for r in range(n_head):
         grad_heads[peer_block(me, r, block), :] = grads_in[r][...]
-    dqkv[...] = jnp.zeros_like(dqkv)
-
-    def attend(span, probs, mine):
-        upper = jnp.where(mine, grad_heads[span, :], 0.0)
-        grad_probs = dot(upper, qkv[2, span, :], NT)
-        inner = jnp.sum(probs * grad_probs, axis=-1, keepdims=True)
-        wide_scores = probs * (grad_probs - inner)
-        grad_scores = wide_scores.astype(BF)
-        dq = (dot(grad_scores, qkv[1, span, :], NN) * SCALE).astype(BF)
-        dk = (dot(grad_scores, qkv[0, span, :], TN) * SCALE).astype(BF)
-        dv = dot(probs.astype(BF), upper, TN).astype(BF)
-        for k, value in enumerate((dq, dk, dv)):
-            dqkv[k, span, :] = jnp.where(mine, value, dqkv[k, span, :])
-        return grad_scores.astype(F32)
-
-    def small_heads(at, carry):
-        for head in (2 * at, 2 * at + 1):
-            for pair in range(pairs):
-                span = slice(width + pair * wide, width + (pair + 1) * wide)
-                grad_scores = attend(span, small_probs[head, pair], head_lanes(head, columns))
-                small_rows[pl.ds(pair * narrow * SUB + head, narrow, stride=SUB), :] = (
-                    grad_scores[:narrow] + grad_scores[narrow:]
-                )
-        return carry
-
-    lax.fori_loop(0, heads // 2, small_heads, 0)
+
+    need(n_head + 3)
+
+    def attend(span, all_probs, store):
+        for head in range(heads):
+            mine = head_lanes(head, columns)
+            probs = all_probs(head)
+            upper = jnp.where(mine, grad_heads[span, :], 0.0)
+            size = upper.shape[0]
+            grad_probs = dot(upper, qkv[2, span, :], NT)
+            inner = jnp.sum(probs * grad_probs, axis=-1, keepdims=True)
+            grad_scores = (probs * (grad_probs - inner)).astype(BF)
+            rows = slice(head * size, (head + 1) * size)
+            tall[0, rows, :size] = grad_scores
+            tall[1, rows, :size] = probs.astype(BF)
+            flat[:size, rows] = grad_scores
+            stacks[0, rows, :] = jnp.where(mine, qkv[0, span, :], 0.0)
+            stacks[1, rows, :] = jnp.where(mine, qkv[1, span, :], 0.0)
+            stacks[2, rows, :] = upper
+            store(head, grad_scores.astype(F32))
+        every = slice(0, heads * size)
+        dqkv[0, span, :] = (dot(flat[:size, every], stacks[1, every, :], NN) * SCALE).astype(BF)
+        dqkv[1, span, :] = (dot(tall[0, every, :size], stacks[0, every, :], TN) * SCALE).astype(BF)
+        dqkv[2, span, :] = dot(tall[1, every, :size], stacks[2, every, :], TN).astype(BF)
+
+    for pair in range(pairs):
+
+        def store_small(head, value, at=pair * narrow * SUB):
+            small_rows[pl.ds(at + head, narrow, stride=SUB), :] = value[:narrow] + value[narrow:]
+
+        span = slice(width + pair * wide, width + (pair + 1) * wide)
+        attend(span, lambda head, pair=pair: small_probs[head, pair], store_small)
     done(0)
-    need(n_head + 3)
-
-    def big_heads(at, carry):
-        for head in (2 * at, 2 * at + 1):
-            grad_scores = attend(slice(0, width), big_probs[head], head_lanes(head, columns))
-            for half in range(halves):
-                big_rows[pl.ds(half * width * SUB + head, width, stride=SUB), :] = grad_scores[
-                    :, LANES * half : LANES * (half + 1)
-                ]
-        return carry
-
-    lax.fori_loop(0, heads // 2, big_heads, 0)
+
+    def store_big(head, value):
+        for half in range(halves):
+            big_rows[pl.ds(half * width * SUB + head, width, stride=SUB), :] = value[
+                :, LANES * half : LANES * (half + 1)
+            ]
+
+    attend(slice(0, width), lambda head: big_probs[head], store_big)
     done(1, 2)
     need(n_head + 4)
     column_sums[...] = jnp.zeros_like(column_sums)
@@ -443,9 +473,10 @@
         column_sums[i, pl.ds(me[0], 1), :] = jnp.sum(dqkv[k].astype(F32), axis=0, keepdims=True)
     for r in range(n_head):
         rows = peer_block(me, r, block)
-        total = dot(dqkv[0, rows, :], whole_matrix(weights, 0), NT)
-        total = total + dot(dqkv[1, rows, :], whole_matrix(weights, 1), NT)
-        total = total + dot(dqkv[2, rows, :], whole_matrix(weights, 2), NT)
+        model = rows_out[r].shape[1]
+        total = dot(dqkv[0, rows, :], attend_matrix(weights, 0, model), NT)
+        total = total + dot(dqkv[1, rows, :], attend_matrix(weights, 1, model), NT)
+        total = total + dot(dqkv[2, rows, :], attend_matrix(weights, 2, model), NT)
         rows_out[r][...] = total.astype(BF)
 
 
@@ -531,8 +562,8 @@
 
 def input_body(n_head, n_vectors, need, done, *refs):
     parts, refs = refs[:n_head], refs[n_head:]
-    me, rows, grad_hidden, vectors, sums, column_sums, pre_sums, table_grad, input_grad, parcel, terms = refs
-    need(*range(n_head), *range(n_head + 1, n_head + 8))
+    me, rows, grad_hidden, vectors, sums, column_sums, pre_sums, input_grad, vector_rows, terms = refs
+    need(*range(n_head), *range(n_head + 1, n_head + 7))
     grad_normed = parts[0][...].astype(F32)
     for part in parts[1:]:
         grad_normed = grad_normed + part[...].astype(F32)
@@ -551,14 +582,12 @@
         for i in range(2):
             terms[4 + i : 5 + i, span] = column_sums[i, j : j + 1, :]
         terms[7:8, span] = pre_sums[j : j + 1, :]
-    inner, outer, height, _ = parcel.shape
-    lanes, height = vectors.shape[1] // (inner * outer), height - VECTOR_ROWS
-    parcel[:, :, :VECTOR_ROWS, :] = jnp.zeros((inner, outer, VECTOR_ROWS, LANES), BF)
+    inner, outer = vector_rows.shape[:2]
+    lanes = vectors.shape[1] // (inner * outer)
+    vector_rows[...] = jnp.zeros_like(vector_rows)
     for d in range(inner * outer):
         at = me[1] ^ d
-        a, b = at % inner, at // inner
-        parcel[a, b, :VECTOR_ROWS, 0:lanes] = terms[:, d * lanes : (d + 1) * lanes].astype(BF)
-        parcel[a, b, VECTOR_ROWS:, :] = table_grad[d * height : (d + 1) * height, :]
+        vector_rows[at % inner, at // inner, :, 0:lanes] = terms[:, d * lanes : (d + 1) * lanes].astype(BF)
 
 
 def adamw_update(weight, first_moment, second_moment, gradient, learn_rate):
@@ -590,10 +619,19 @@
     table = value[VECTOR_ROWS:]
     shard[...] = table
     here = jnp.sum(table * table).reshape(1, 1) + squares[0:1, 0:1]
-    row = lax.broadcasted_iota(jnp.int32, (VECTOR_ROWS, LANES), 0)
-    lane = lax.broadcasted_iota(jnp.int32, (VECTOR_ROWS, LANES), 1)
-    message = jnp.where((row == VECTOR_ROWS - 1) & (lane == 0), here, value[:VECTOR_ROWS])
+    tail = value[MESSAGE_ROWS : MESSAGE_ROWS + 1]
+    free = LANES // 4
+    gap = jnp.zeros((1, LANES - free), F32)
+    spill = [jnp.concatenate([gap, tail[:, q * free : (q + 1) * free]], axis=1) for q in range(3)]
+    spill = jnp.concatenate(spill + [jnp.zeros((MESSAGE_ROWS - 3, LANES), F32)], axis=0)
+    message = jnp.where(corner_mask(), here, value[:MESSAGE_ROWS] + spill)
     told[...] = jnp.broadcast_to(message[None], told.shape)
+
+
+def corner_mask():
+    row = lax.broadcasted_iota(jnp.int32, (MESSAGE_ROWS, LANES), 0)
+    lane = lax.broadcasted_iota(jnp.int32, (MESSAGE_ROWS, LANES), 1)
+    return (row == MESSAGE_ROWS - 1) & (lane == LANES - 1)
 
 
 def update_body(n_head, n_vectors, need, done, *refs):
@@ -609,13 +647,13 @@
             value = value + told[d * n_head + j]
         return value
 
-    row = lax.broadcasted_iota(jnp.int32, (VECTOR_ROWS, LANES), 0)
+    corner = corner_mask()
 
     def square(d, total):
         value = merged(d)
-        return total + jnp.where(row < n_vectors, value * value, jnp.where(row == VECTOR_ROWS - 1, value, 0.0))
-
-    total = lax.fori_loop(0, n_dp, square, jnp.zeros((VECTOR_ROWS, LANES), F32))
+        return total + jnp.where(corner, value, value * value)
+
+    total = lax.fori_loop(0, n_dp, square, jnp.zeros((MESSAGE_ROWS, LANES), F32))
     grad_norm = jnp.sqrt(jnp.sum(total).reshape(1, 1))
     norm_out[...] = jnp.broadcast_to(grad_norm, norm_out.shape)
     factor = CLIP_NORM / jnp.maximum(grad_norm, CLIP_NORM)
@@ -630,7 +668,9 @@
     update(0, shards[4], RATE_MATRIX, 3)
     update(1, out_shard[...], RATE_OUTPUT)
     update(2, down_shard[...], RATE_MATRIX)
-    mine = merged(me[1])
+    mine, free = merged(me[1]), LANES // 4
+    tail = jnp.concatenate([mine[q : q + 1, LANES - free :] for q in range(3)], axis=1)
+    mine = jnp.concatenate([mine[:, : LANES - free], tail], axis=0)
     size = params[9].shape[1]
     gradient = jnp.zeros((n_vectors, size), F32)
     for j in range(n_head):
@@ -734,12 +774,21 @@
     with jax.named_scope("rows_far"):
         given[far] = to_head(given[0], far)
     qkv_sent = weight_in[:3].astype(BF)
-    vectors_sent = jnp.pad(vectors, ((0, VECTOR_ROWS - n_vectors), (0, LANES - shard_width)))
-    table_all, vectors_sent, qkv_sent, *rest_far = lax.optimization_barrier(
-        (table_all, vectors_sent, qkv_sent, *rest_far)
-    )
-    with jax.named_scope("vectors_all"):
-        vector_pieces = spread_all(vectors_sent, everyone)
+    with jax.named_scope("vectors_head"):
+        own_vectors = lax.dynamic_update_slice_in_dim(
+            jnp.zeros((n_vectors, lanes_used), F32), vectors, head_index * shard_width, 1
+        )
+        step = far
+        while step:
+            own_vectors = own_vectors + to_head(own_vectors, step)
+            step //= 2
+    rest, pieces = own_vectors, []
+    for _ in range(PIECES):
+        piece = lax.reduce_precision(rest, 8, 7)
+        rest = rest - piece
+        pieces.append(jnp.pad(piece.astype(BF), ((0, PIECE_ROWS - n_vectors), (0, columns - lanes_used))))
+    qkv_sent = jnp.concatenate([qkv_sent.reshape(3 * shard_rows, columns), *pieces])
+    table_all, qkv_sent, *rest_far = lax.optimization_barrier((table_all, qkv_sent, *rest_far))
     with jax.named_scope("rest_near"):
         rest_near = near_shards(rest_far)
     with jax.named_scope("qkv_far"):
@@ -758,8 +807,8 @@
         )
 
     small_bias, *big_bias = pair_bias(0, table_all, (*small_ints, *big_ints))
-    held = lax.optimization_barrier((small_bias, vector_pieces, table_all, given[far], *rest_near, *qkv_far))
-    (small_bias, vector_pieces, table_all, given[far]), held = held[:4], held[4:]
+    held = lax.optimization_barrier((small_bias, table_all, given[far], *rest_near, *qkv_far))
+    (small_bias, table_all, given[far]), held = held[:3], held[3:]
     rest_near, qkv_far = held[:inner], held[inner:]
     weights_rest = jnp.concatenate(rest_near)
     with jax.named_scope("qkv_near"):
@@ -781,13 +830,17 @@
         for r in near_heads:
             weights_held[r] = to_head(weights_held[0], r)
     weights_attend = jnp.concatenate(qkv_near)
+    vector_row, vector_pieces = 3 * shard_rows, ()
     if not stacked:
-        weights_attend = weights_attend[order].transpose(1, 0, 2, 3).reshape(3, model, columns)
+        weights_attend = weights_attend[order]
+        vector_row, vector_pieces = 0, (weights_attend[:, 3 * shard_rows :],)
+        weights_attend = weights_attend[:, : 3 * shard_rows].reshape(n_dp, 3, shard_rows, columns)
+        weights_attend = weights_attend.transpose(1, 0, 2, 3).reshape(3, model, columns)
 
     block = struct((my_rows, columns), BF)
     rows_block = struct((my_rows, model), BF)
     normed_one, qkv, big_probs, small_probs, all_vectors, hidden_bias, *mixed = kernel_call(
-        lambda *refs: forward_body(n_head, *refs),
+        lambda *refs: forward_body(n_head, vector_row, *refs),
         [
             struct((group_rows, model), BF),
             struct((3, group_rows, columns), BF),
@@ -799,10 +852,14 @@
         ],
         "attend_forward",
         12,
-        (*given, us, big_counts, small_counts, vector_pieces, weights_attend, small_bias, *big_bias),
-        [pltpu.VMEM((group_rows, columns), BF)],
+        (*given, us, big_counts, small_counts, weights_attend, small_bias, *big_bias, *vector_pieces),
+        [
+            pltpu.VMEM((group_rows, columns), BF),
+            pltpu.VMEM((width, heads * width), BF),
+            pltpu.VMEM((heads * width, columns), BF),
+        ],
         range(n_head, n_head + 3),
-        (n_head + 4,) if stacked else (),
+        (n_head + 3,) if stacked else (),
         n_head,
     )
     with jax.named_scope("mixed_rows"):
@@ -854,7 +911,12 @@
         "attend_backward",
         14,
         (*grad_heads, us, qkv, small_probs, big_probs, weights_attend),
-        [pltpu.VMEM((group_rows, columns), BF)],
+        [
+            pltpu.VMEM((group_rows, columns), BF),
+            pltpu.VMEM((2, heads * width, width), BF),
+            pltpu.VMEM((width, heads * width), BF),
+            pltpu.VMEM((3, heads * width, columns), BF),
+        ],
         (n_head,),
         (n_head + 4,) if stacked else (),
         n_head,
@@ -875,34 +937,33 @@
     )
     if not stacked:
         weight_grads = weight_grads.reshape(6, n_dp, shard_rows, columns).transpose(1, 0, 2, 3)
-    weight_grads, small_rows, *rows_sent = lax.optimization_barrier((weight_grads, small_rows, *rows_sent))
+    with jax.named_scope("grad_normed_one"):
+        rows_back = swap(rows_sent, n_head)
+    weight_grads, *rows_back = lax.optimization_barrier((weight_grads, *rows_back))
     with jax.named_scope("weight_grads"):
         weights_arrived = exchange(weight_grads, "dp")
-    with jax.named_scope("grad_normed_one"):
-        rows_back = swap(rows_sent, n_head)
-    (table_grad,) = kernel_call(
+    input_grad, vector_rows = kernel_call(
+        lambda *refs: input_body(n_head, n_vectors, *refs),
+        [rows_block, struct((inner, outer, VECTOR_ROWS, LANES), BF)],
+        "input_grad",
+        3,
+        (*rows_back, us, node_rows, grad_hidden, all_vectors, sums, column_sums, pre_sums),
+        [pltpu.VMEM((VECTOR_ROWS, model), F32)],
+        (n_head,),
+    )
+    table_rows = table_chunks * heads
+    block = struct((outer, VECTOR_ROWS + table_rows, LANES), BF)
+    inner_sent = kernel_call(
         scatter_body,
-        [struct((all_chunks * heads, LANES), BF)],
+        [(inner, block)],
         "table_scatter",
         40,
-        (small_rows, *small_ints, big_rows, *big_ints),
+        (small_rows, *small_ints, big_rows, *big_ints, us, vector_rows),
         [pltpu.VMEM((LANES, all_chunks * heads), F32)],
-    )
-    table_grad, *rows_back = lax.optimization_barrier((table_grad, *rows_back))
-    table_rows = table_chunks * heads
-    block = struct((outer, VECTOR_ROWS + table_rows, LANES), BF)
-    input_grad, *inner_sent = kernel_call(
-        lambda *refs: input_body(n_head, n_vectors, *refs),
-        [rows_block, (inner, block)],
-        "input_grad",
-        3,
-        (*rows_back, us, node_rows, grad_hidden, all_vectors, sums, column_sums, pre_sums, table_grad),
-        [pltpu.VMEM((VECTOR_ROWS, model), F32)],
-        (n_head,),
+        (8,),
     )
     with jax.named_scope("table_inner"):
         arrived = [inner_sent[0]] + [lax.ppermute(inner_sent[k], "dp", dp_pairs(k)) for k in range(1, inner)]
-    weights_arrived, *arrived = lax.optimization_barrier((weights_arrived, *arrived))
     outer_sent = kernel_call(
         merge_body,
         [(outer, struct(block.shape[1:], BF))],
@@ -910,6 +971,7 @@
         1,
         tuple(arrived),
     )
+    weights_arrived, *outer_sent = lax.optimization_barrier((weights_arrived, *outer_sent))
     with jax.named_scope("table_outer"):
         parts = [outer_sent[0]] + [
             lax.ppermute(outer_sent[k], "dp", dp_pairs(k * inner)) for k in range(1, outer)
@@ -923,7 +985,7 @@
     )
     table_shard, told = kernel_call(
         told_body,
-        [struct((table_rows, LANES), F32), struct((n_dp * n_head, VECTOR_ROWS, LANES), F32)],
+        [struct((table_rows, LANES), F32), struct((n_dp * n_head, MESSAGE_ROWS, LANES), F32)],
         "table_sums",
         1,
         (*parts, squares),

time: 225 us -> 208 us (0.924)
  Pallas kernels: 125 us -> 114 us
  starting transfers between devices: 53.8 us -> 46.7 us
    pallas_call x12, Pallas kernels: 125 us -> 114 us  [kernel_call(): pl.pallas_call(wrapped, out_shape=tuple((shapes[i] for i, _ in flat)), in...]
    all_to_all x5 -> x4, starting transfers between devices: 23.1 us -> 17.2 us  [exchange(): return lax.all_to_all(value, axis, split_axis=0, concat_axis=0, tiled=True)]
    all_to_all x5 -> x4, waiting for transfers between devices: 13 us -> 16.3 us  [exchange(): return lax.all_to_all(value, axis, split_axis=0, concat_axis=0, tiled=True)]
    ppermute x6, waiting for transfers between devices: 4.38 us -> 1.31 us  [far_shards(): lax.ppermute(value, 'dp', dp_pairs(k))]
    ppermute x2, waiting for transfers between devices: 2.95 us -> 0.01 us  [near_shards(): lax.ppermute(value, 'dp', dp_pairs(k))]
    ppermute x1, waiting for transfers between devices: 3.05 us -> 5.46 us  [on_device(): lax.ppermute(inner_sent[k], 'dp', dp_pairs(k))]
    unnamed x106 -> x89, local copies, waits for them, and re-layouts: 7.8 us -> 8.35 us
  transfers between devices with their start and end apart: 35 -> 36, of which waited for: 11 -> 11; matrix products, arithmetic and copies ran while one was open for 2% -> 3% of each run, Pallas kernels for 47% -> 49%
where the time goes in v3:
time: 208 us; the launch traced here: 207 us
  Pallas kernels  114 us (55%)
  starting transfers between devices  46.7 us (22%)
  waiting for transfers between devices  29.4 us (14%)
  local copies, waits for them, and re-layouts  11.8 us (6%)
  other arithmetic  3.44 us (2%)
  between operations  2.31 us (1%)
    pallas_call x12, Pallas kernels, kernel_call(): pl.pallas_call(wrapped, out_shape=tuple((shapes[i] for i, _ in flat)), in...  114 us
    all_to_all x4, starting transfers between devices, exchange(): return lax.all_to_all(value, axis, split_axis=0, concat_axis=0, tiled=True)  17.2 us
    all_to_all x4, waiting for transfers between devices, exchange(): return lax.all_to_all(value, axis, split_axis=0, concat_axis=0, tiled=True)  16.3 us
    ppermute x6, starting transfers between devices, far_shards(): lax.ppermute(value, 'dp', dp_pairs(k))  10.1 us
    unnamed x89, local copies, waits for them, and re-layouts  8.35 us
    ppermute x9, starting transfers between devices, swap(): lax.ppermute(values[r], 'head', [(i, i ^ r) for i in range(n_head)])  6.05 us
    ppermute x1, waiting for transfers between devices, on_device(): lax.ppermute(inner_sent[k], 'dp', dp_pairs(k))  5.46 us
    ppermute x9, waiting for transfers between devices, swap(): lax.ppermute(values[r], 'head', [(i, i ^ r) for i in range(n_head)])  5.15 us
  transfers between devices with their start and end apart: 36, of which 11 were waited for; matrix products, arithmetic and copies ran while one was open for 3% of the time, Pallas kernels for 49%

profile of v3, /device:TPU:0, one launch (start us, length us, event | category | flops | bytes accessed | tf_op | source)
XLA Modules:
  0.0 207.2 jit_solution(5003347477468042265)
XLA Ops:
  3.8 5.1 %collective-permute-start.4 = (bf16[3,96,192]{2,1,0:T(8,128)(2,1)S(1)}, bf16[3,96,192]{2,1,0:T(8,128)(2,1)S(1)}, u32[]{:S(2)}, u32[]{:S(2)}) collective-permute-start(bf16[3,96,192]{2,1,0:T(8,128)(2,1)S(1)} %pad_maximum_fusion.4), channel_id=1, source_target_pairs={{0,24},{4,28},{8,16},{12,20},{16,8},{20,12},{24,0},{28,4},{1,25},{... | collective-permute-start | bytes 331784 | tf_op jit(solution)/shard_map/rest_far/ppermute | solution.py:754
  12.8 5.8 %all-to-all-start = ((bf16[8,8,8,128]{3,2,1,0:T(8,128)(2,1)}), bf16[8,8,8,128]{3,2,1,0:T(8,128)(2,1)S(1)}, u32[]{:S(2)}, u32[]{:S(2)}) async-start(bf16[8,8,8,128]{3,2,1,0:T(8,128)(2,1)} %broadcast_in_dim.4), calls=%async_computation | async-start | bytes 262144 | tf_op jit(solution)/shard_map/table_all/all_to_all | solution.py:685
  22.2 3.8 %all-to-all-done = bf16[8,8,8,128]{3,2,1,0:T(8,128)(2,1)S(1)} async-done(((bf16[8,8,8,128]{3,2,1,0:T(8,128)(2,1)}), bf16[8,8,8,128]{3,2,1,0:T(8,128)(2,1)S(1)}, u32[]{:S(2)}, u32[]{:S(2)}) %all-to-all-start) | async-done | bytes 131104 | tf_op jit(solution)/shard_map/table_all/all_to_all | solution.py:685
  27.3 3.1 %collective-permute-start.7 = (bf16[336,192]{1,0:T(8,128)(2,1)S(1)}, bf16[336,192]{1,0:T(8,128)(2,1)S(1)}, u32[]{:S(2)}, u32[]{:S(2)}) collective-permute-start(bf16[336,192]{1,0:T(8,128)(2,1)S(1)} %fusion.6), channel_id=1, source_target_pairs={{0,8},{4,12},{8,0},{12,4},{16,24},{20,28},{24,16},{28,20},{1,9},{5... | collective-permute-start | bytes 387080 | tf_op jit(solution)/shard_map/qkv_far/ppermute | solution.py:754
  30.8 13.2 %pair_bias.2 = (f32[8,2,64,128]{3,2,1,0:T(8,128)}, f32[8,2,64,128]{3,2,1,0:T(8,128)}) custom-call(bf16[512,128]{1,0:T(8,128)(2,1)} %bitcast.62, s32[4,64,64]{2,1,0:T(8,128)} %refs_1_.5, s32[5,4,64,64]{3,2,1,0:T(8,128)} %refs_2_.5, s32[4,64,64]{2,1,0:T(8,128)} %refs_3_.5, s32[1,256,256]{2,1,0:T(8,128)} %refs_5_.8, s32[5,1,256,256]{3,2,1,0:T(8,128)} %refs_6_.8, ...), custom_call_target="tpu_custom_call" | custom-call | flops 12000000000 | bytes 1048576 | tf_op jit(solution)/shard_map/pair_bias/pallas_call | solution.py:117
  49.3 18.5 %pair_bias.3.refs_10_ = f32[8,2,192,128]{3,2,1,0:T(8,128)} custom-call(bf16[512,128]{1,0:T(8,128)(2,1)} %bitcast.63, s32[1,256,256]{2,1,0:T(8,128)} %refs_5_.8, s32[5,1,256,256]{3,2,1,0:T(8,128)} %refs_6_.8, s32[1,256,256]{2,1,0:T(8,128)} %refs_7_.2), custom_call_target="tpu_custom_call" | custom-call | flops 20000000000 | bytes 1048576 | tf_op jit(solution)/shard_map/pair_bias/pallas_call | solution.py:117
  69.5 7.7 %attend_forward.1 = (bf16[512,768]{1,0:T(8,128)(2,1)}, bf16[3,512,192]{2,1,0:T(8,128)(2,1)}, f32[8,256,256]{2,1,0:T(8,128)}, f32[8,2,128,128]{3,2,1,0:T(8,128)},...) custom-call(bf16[2,128,768]{2,1,0:T(8,128)(2,1)} %copy-done.20, ...), custom_call_target="tpu_custom_call" | custom-call | flops 12000000000 | bytes 1048576 | tf_op jit(solution)/shard_map/attend_forward/pallas_call | solution.py:117
  80.4 1.8 collective-permute-done.16.refs_2_
  85.0 8.0 %feed_forward.1 = (bf16[128,768]{1,0:T(8,128)(2,1)}, f32[128,768]{1,0:T(8,128)}, f32[4,768]{1,0:T(4,128)}, f32[4,192]{1,0:T(4,128)}, bf16[2,128,768]{2,1,0:T(8,1...) custom-call(bf16[128,192]{1,0:T(8,128)(2,1)} %get-tuple-element.144., ...), custom_call_target="tpu_custom_call" | custom-call | flops 6000000000 | bytes 1048576 | tf_op jit(solution)/shard_map/feed_forward/pallas_call | solution.py:117
  95.9 3.6 %all-to-all-start.1 = ((bf16[4,128,512]{2,1,0:T(8,128)(2,1)}), bf16[4,128,512]{2,1,0:T(8,128)(2,1)S(1)}, u32[]{:S(2)}, u32[]{:S(2)}) async-start(bf16[4,128,512]{2,1,0:T(8,128)(2,1)} %get-tuple-element.154), calls=%async_computation.1 | async-start | bytes 1048576 | tf_op jit(solution)/shard_map/act_pre/all_to_all | solution.py:685
  100.2 9.2 %attend_backward.1 = (f32[1024,128]{1,0:T(8,128)}, f32[4096,128]{1,0:T(8,128)}, bf16[3,512,192]{2,1,0:T(8,128)(2,1)}, f32[2,4,192]{2,1,0:T(4,128)}, bf16[128,768...) custom-call(bf16[128,192]{1,0:T(8,128)(2,1)} %get-tuple-element.156.refs_0_, ...), custom_call_target="tpu_custom_call" | custom-call | flops 14000000000 | bytes 1048576 | tf_op jit(solution)/shard_map/attend_backward/pallas_call | solution.py:117
  110.1 1.8 collective-permute-start.26
  114.2 6.3 %weight_grads.1 = bf16[8,6,96,192]{3,2,1,0:T(8,128)(2,1)} custom-call(bf16[2,128,768]{2,1,0:T(8,128)(2,1)} %copy-done.20, bf16[2,128,768]{2,1,0:T(8,128)(2,1)} %copy-done.26, bf16[2,128,768]{2,1,0:T(8,128)(2,1)} %copy-done.25, bf16[2,128,768]{2,1,0:T(8,128)(2,1)} %collective-permute-done.12.refs_3_, bf16[128,192]{1,0:T(8,128)(2,1)} %get-tuple-element.144.refs_0_.refs_4_, ...), custom_call_target="tpu_custom_call" | custom-call | flops 6000000000 | bytes 1048576 | tf_op jit(solution)/shard_map/weight_grads/pallas_call | solution.py:117
  121.8 3.8 %all-to-all-start.2 = ((bf16[8,6,96,192]{3,2,1,0:T(8,128)(2,1)}), bf16[8,6,96,192]{3,2,1,0:T(8,128)(2,1)S(1)}, u32[]{:S(2)}, u32[]{:S(2)}) async-start(bf16[8,6,96,192]{3,2,1,0:T(8,128)(2,1)} %weight_grads.1), calls=%async_computation.2 | async-start | bytes 4718592 | tf_op jit(solution)/shard_map/weight_grads/all_to_all | solution.py:685
  125.6 3.3 %input_grad.1 = (bf16[128,768]{1,0:T(8,128)(2,1)}, bf16[2,4,16,128]{3,2,1,0:T(8,128)(2,1)}) custom-call(bf16[128,768]{1,0:T(8,128)(2,1)} %get-tuple-element.172.refs_0_, bf16[128,768]{1,0:T(8,128)(2,1)} %copy-done.30, bf16[128,768]{1,0:T(8,128)(2,1)} %copy-done.31, bf16[128,768]{1,0:T(8,128)(2,1)} %copy-done.32, s32[2]{0:T(128)} %pad_add_fusion.refs_4_.refs_8_.refs_0_, ...), custom_call_target="tpu_custom_call" | custom-call | flops 3000000000 | bytes 1048576 | tf_op jit(solution)/shard_map/input_grad/pallas_call | solution.py:117
  128.9 38.1 %table_scatter.1 = (bf16[4,80,128]{2,1,0:T(8,128)(2,1)}, bf16[4,80,128]{2,1,0:T(8,128)(2,1)}) custom-call(f32[1024,128]{1,0:T(8,128)} %get-tuple-element.182.refs_0_, s32[4,64,64]{2,1,0:T(8,128)} %refs_1_.5, s32[5,4,64,64]{3,2,1,0:T(8,128)} %refs_2_.5, s32[4,64,64]{2,1,0:T(8,128)} %refs_3_.5, f32[4096,128]{1,0:T(8,128)} %get-tuple-element.183.refs_4_, ...), custom_call_target="tpu_custom_call" | custom-call | flops 40000000000 | bytes 1048576 | tf_op jit(solution)/shard_map/table_scatter/pallas_call | solution.py:117
  167.0 2.1 collective-permute-start.28
  169.1 5.5 %collective-permute-done.28.refs_1_ = bf16[4,80,128]{2,1,0:T(8,128)(2,1)S(1)} collective-permute-done((bf16[4,80,128]{2,1,0:T(8,128)(2,1)}, bf16[4,80,128]{2,1,0:T(8,128)(2,1)S(1)}, u32[]{:S(2)}, u32[]{:S(2)}) %collective-permute-start.28) | collective-permute-done | bytes 81952 | tf_op jit(solution)/shard_map/table_inner/ppermute | solution.py:966
  176.8 3.3 %all-to-all-done.2.refs_0_ = bf16[8,6,96,192]{3,2,1,0:T(8,128)(2,1)S(1)} async-done(((bf16[8,6,96,192]{3,2,1,0:T(8,128)(2,1)}), bf16[8,6,96,192]{3,2,1,0:T(8,128)(2,1)S(1)}, u32[]{:S(2)}, u32[]{:S(2)}) %all-to-all-start.2) | async-done | bytes 1769504 | tf_op jit(solution)/shard_map/weight_grads/all_to_all | solution.py:685
  180.1 2.8 %collective-permute-start.30 = (bf16[80,128]{1,0:T(8,128)(2,1)}, bf16[80,128]{1,0:T(8,128)(2,1)S(1)}, u32[]{:S(2)}, u32[]{:S(2)}) collective-permute-start(bf16[80,128]{1,0:T(8,128)(2,1)} %get-tuple-element.193), channel_id=1, source_target_pairs={{0,16},{4,20},{8,24},{12,28},{16,0},{20,4},{24,8},{28,12},{1,17},{... | collective-permute-start | bytes 61448 | tf_op jit(solution)/shard_map/table_outer/ppermute | solution.py:977
  184.4 3.1 %shard_sums.1 = (f32[6,96,192]{2,1,0:T(8,128)}, f32[1,128]{1,0:T(1,128)}) custom-call(bf16[8,6,96,192]{3,2,1,0:T(8,128)(2,1)} %copy-done.18), custom_call_target="tpu_custom_call" | custom-call | flops 3000000000 | bytes 1048576 | tf_op jit(solution)/shard_map/shard_sums/pallas_call | solution.py:117
  191.2 3.9 %all-to-all-start.3 = ((f32[32,8,128]{2,1,0:T(8,128)}), f32[32,8,128]{2,1,0:T(8,128)S(1)}, u32[]{:S(2)}, u32[]{:S(2)}) async-start(f32[32,8,128]{2,1,0:T(8,128)} %get-tuple-element.197), calls=%async_computation.3 | async-start | bytes 262144 | tf_op jit(solution)/shard_map/squares/all_to_all | solution.py:685
  195.4 7.9 %all-to-all-done.3.refs_1_ = f32[32,8,128]{2,1,0:T(8,128)S(1)} async-done(((f32[32,8,128]{2,1,0:T(8,128)}), f32[32,8,128]{2,1,0:T(8,128)S(1)}, u32[]{:S(2)}, u32[]{:S(2)}) %all-to-all-start.3) | async-done | bytes 131104 | tf_op jit(solution)/shard_map/squares/all_to_all | solution.py:685
  204.2 2.8 %update.1 = (f32[4,96,192]{2,1,0:T(8,128)}, f32[4,96,192]{2,1,0:T(8,128)}, f32[4,96,192]{2,1,0:T(8,128)}, f32[192,96]{1,0:T(8,128)}, f32[192,96]{1,0:T(8,128)}, ...) custom-call(s32[2]{0:T(128)S(1)} %copy-done.16, ...), custom_call_target="tpu_custom_call" | custom-call | flops 3000000000 | bytes 1048576 | tf_op jit(solution)/shard_map/update/pallas_call | solution.py:117
  (171 shorter events, 40.3 us)
Async XLA Ops:
  3.8 17.0 %collective-permute-start.4 = (bf16[3,96,192]{2,1,0:T(8,128)(2,1)S(1)}, bf16[3,96,192]{2,1,0:T(8,128)(2,1)S(1)}, u32[]{:S(2)}, u32[]{:S(2)}) collective-permute-start(bf16[3,96,192]{2,1,0:T(8,128)(2,1)S(1)} %pad_maximum_fusion.4), channel_id=1, source_target_pairs={{0,24},{4,28},{8,16},{12,20},{16,8},{20,12},{24,0},{28,4},{1,25},{... | collective-permute-start | bytes 331784 | tf_op jit(solution)/shard_map/rest_far/ppermute | solution.py:754
  8.9 13.2 %collective-permute-start.3 = (bf16[3,96,192]{2,1,0:T(8,128)(2,1)S(1)}, bf16[3,96,192]{2,1,0:T(8,128)(2,1)S(1)}, u32[]{:S(2)}, u32[]{:S(2)}) collective-permute-start(bf16[3,96,192]{2,1,0:T(8,128)(2,1)S(1)} %pad_maximum_fusion.4), channel_id=1, source_target_pairs={{0,16},{4,20},{8,24},{12,28},{16,0},{20,4},{24,8},{28,12},{1,17},{... | collective-permute-start | bytes 331784 | tf_op jit(solution)/shard_map/rest_far/ppermute | solution.py:754
  8.9 13.2 %collective-permute-start.2 = (bf16[3,96,192]{2,1,0:T(8,128)(2,1)S(1)}, bf16[3,96,192]{2,1,0:T(8,128)(2,1)S(1)}, u32[]{:S(2)}, u32[]{:S(2)}) collective-permute-start(bf16[3,96,192]{2,1,0:T(8,128)(2,1)S(1)} %pad_maximum_fusion.4), channel_id=1, source_target_pairs={{0,8},{4,12},{8,0},{12,4},{16,24},{20,28},{24,16},{28,20},{1,9},{5... | collective-permute-start | bytes 331784 | tf_op jit(solution)/shard_map/rest_far/ppermute | solution.py:754
  10.3 8.9 %collective-permute-start = (f32[9,96]{1,0:T(8,128)S(1)}, f32[9,96]{1,0:T(8,128)S(1)}, u32[]{:S(2)}, u32[]{:S(2)}) collective-permute-start(f32[9,96]{1,0:T(8,128)S(1)} %dynamic_update_slice.5), channel_id=1, source_target_pairs={{0,2},{1,3},{2,0},{3,1},{4,6},{5,7},{6,4},{7,5},{8,10},{9,11},{10,... | collective-permute-start | bytes 10376 | tf_op jit(solution)/shard_map/vectors_head/ppermute | solution.py:761
  12.8 13.2 %all-to-all-start = ((bf16[8,8,8,128]{3,2,1,0:T(8,128)(2,1)}), bf16[8,8,8,128]{3,2,1,0:T(8,128)(2,1)S(1)}, u32[]{:S(2)}, u32[]{:S(2)}) async-start(bf16[8,8,8,128]{3,2,1,0:T(8,128)(2,1)} %broadcast_in_dim.4), calls=%async_computation | async-start | bytes 262144 | tf_op jit(solution)/shard_map/table_all/all_to_all | solution.py:685
  18.7 25.4 %collective-permute-start.5 = (bf16[2,128,768]{2,1,0:T(8,128)(2,1)S(1)}, bf16[2,128,768]{2,1,0:T(8,128)(2,1)S(1)}, u32[]{:S(2)}, u32[]{:S(2)}) collective-permute-start(bf16[2,128,768]{2,1,0:T(8,128)(2,1)S(1)} %pad_maximum_fusion.3.refs_0_), channel_id=1, source_target_pairs={{0,2},{1,3},{2,0},{3,1},{4,6},{5,7},{6,4},{7,5},{8,10},{9,11},{10,... | collective-permute-start | bytes 1179656 | tf_op jit(solution)/shard_map/rows_far/ppermute | solution.py:761
  26.0 18.0 %collective-permute-start.9 = (bf16[336,192]{1,0:T(8,128)(2,1)S(1)}, bf16[336,192]{1,0:T(8,128)(2,1)S(1)}, u32[]{:S(2)}, u32[]{:S(2)}) collective-permute-start(bf16[336,192]{1,0:T(8,128)(2,1)S(1)} %fusion.6), channel_id=1, source_target_pairs={{0,24},{4,28},{8,16},{12,20},{16,8},{20,12},{24,0},{28,4},{1,25},{... | collective-permute-start | bytes 387080 | tf_op jit(solution)/shard_map/qkv_far/ppermute | solution.py:754
  27.2 16.9 %collective-permute-start.8 = (bf16[336,192]{1,0:T(8,128)(2,1)S(1)}, bf16[336,192]{1,0:T(8,128)(2,1)S(1)}, u32[]{:S(2)}, u32[]{:S(2)}) collective-permute-start(bf16[336,192]{1,0:T(8,128)(2,1)S(1)} %fusion.6), channel_id=1, source_target_pairs={{0,16},{4,20},{8,24},{12,28},{16,0},{20,4},{24,8},{28,12},{1,17},{... | collective-permute-start | bytes 387080 | tf_op jit(solution)/shard_map/qkv_far/ppermute | solution.py:754
  27.3 16.8 %collective-permute-start.7 = (bf16[336,192]{1,0:T(8,128)(2,1)S(1)}, bf16[336,192]{1,0:T(8,128)(2,1)S(1)}, u32[]{:S(2)}, u32[]{:S(2)}) collective-permute-start(bf16[336,192]{1,0:T(8,128)(2,1)S(1)} %fusion.6), channel_id=1, source_target_pairs={{0,8},{4,12},{8,0},{12,4},{16,24},{20,28},{24,16},{28,20},{1,9},{5... | collective-permute-start | bytes 387080 | tf_op jit(solution)/shard_map/qkv_far/ppermute | solution.py:754
  30.5 13.6 %collective-permute-start.6 = (bf16[4,3,96,192]{3,2,1,0:T(8,128)(2,1)S(1)}, bf16[4,3,96,192]{3,2,1,0:T(8,128)(2,1)S(1)}, u32[]{:S(2)}, u32[]{:S(2)}) collective-permute-start(bf16[4,3,96,192]{3,2,1,0:T(8,128)(2,1)S(1)} %pad_maximum_fusion.2), channel_id=1, source_target_pairs={{0,4},{4,0},{8,12},{12,8},{16,20},{20,16},{24,28},{28,24},{1,5},{5... | collective-permute-start | bytes 1327112 | tf_op jit(solution)/shard_map/rest_near/ppermute | solution.py:758
  44.0 23.8 %collective-permute-start.11 = (bf16[2,128,768]{2,1,0:T(8,128)(2,1)S(1)}, bf16[2,128,768]{2,1,0:T(8,128)(2,1)S(1)}, u32[]{:S(2)}, u32[]{:S(2)}) collective-permute-start(bf16[2,128,768]{2,1,0:T(8,128)(2,1)S(1)} %pad_maximum_fusion.3.refs_0_), channel_id=1, source_target_pairs={{0,1},{1,0},{2,3},{3,2},{4,5},{5,4},{6,7},{7,6},{8,9},{9,8},{10,11... | collective-permute-start | bytes 1179656 | tf_op jit(solution)/shard_map/rows_near/ppermute | solution.py:761
  46.0 31.2 %collective-permute-start.14 = (bf16[8,3,96,192]{3,2,1,0:T(8,128)(2,1)}, bf16[8,3,96,192]{3,2,1,0:T(8,128)(2,1)}, u32[]{:S(2)}, u32[]{:S(2)}) collective-permute-start(bf16[8,3,96,192]{3,2,1,0:T(8,128)(2,1)} %constant_dynamic-update-slice_fusion.refs_9_), channel_id=1, source_target_pairs={{0,2},{1,3},{2,0},{3,1},{4,6},{5,7},{6,4},{7,5},{8,10},{9,11},{10,... | collective-permute-start | bytes 2654216 | tf_op jit(solution)/shard_map/rest_far_head/ppermute | solution.py:761
  47.1 30.2 %collective-permute-start.13 = (bf16[8,3,96,192]{3,2,1,0:T(8,128)(2,1)}, bf16[8,3,96,192]{3,2,1,0:T(8,128)(2,1)}, u32[]{:S(2)}, u32[]{:S(2)}) collective-permute-start(bf16[8,3,96,192]{3,2,1,0:T(8,128)(2,1)} %constant_dynamic-update-slice_fusion.refs_9_), channel_id=1, source_target_pairs={{0,1},{1,0},{2,3},{3,2},{4,5},{5,4},{6,7},{7,6},{8,9},{9,8},{10,11... | collective-permute-start | bytes 2654216 | tf_op jit(solution)/shard_map/rest_near_head/ppermute | solution.py:761
  47.3 20.6 %collective-permute-start.12 = (bf16[2,128,768]{2,1,0:T(8,128)(2,1)S(1)}, bf16[2,128,768]{2,1,0:T(8,128)(2,1)}, u32[]{:S(2)}, u32[]{:S(2)}) collective-permute-start(bf16[2,128,768]{2,1,0:T(8,128)(2,1)S(1)} %collective-permute-done.5.refs_2_), channel_id=1, source_target_pairs={{0,1},{1,0},{2,3},{3,2},{4,5},{5,4},{6,7},{7,6},{8,9},{9,8},{10,11... | collective-permute-start | bytes 1179656 | tf_op jit(solution)/shard_map/rows_near/ppermute | solution.py:761
  48.1 19.8 %collective-permute-start.10 = (bf16[4,336,192]{1,2,0:T(8,128)(2,1)S(1)}, bf16[4,336,192]{1,2,0:T(8,128)(2,1)S(1)}, u32[]{:S(2)}, u32[]{:S(2)}) collective-permute-start(bf16[4,336,192]{1,2,0:T(8,128)(2,1)S(1)} %copy.49), channel_id=1, source_target_pairs={{0,4},{4,0},{8,12},{12,8},{16,20},{20,16},{24,28},{28,24},{1,5},{5... | collective-permute-start | bytes 1548296 | tf_op jit(solution)/shard_map/qkv_near/ppermute | solution.py:758
  94.9 14.5 %collective-permute-start.23 = (bf16[2,128,768]{2,1,0:T(8,128)(2,1)}, bf16[2,128,768]{2,1,0:T(8,128)(2,1)S(1)}, u32[]{:S(2)}, u32[]{:S(2)}) collective-permute-start(bf16[2,128,768]{2,1,0:T(8,128)(2,1)} %get-tuple-element.164.refs_12_), channel_id=1, source_target_pairs={{0,2},{1,3},{2,0},{3,1},{4,6},{5,7},{6,4},{7,5},{8,10},{9,11},{10,... | collective-permute-start | bytes 1179656 | tf_op jit(solution)/shard_map/normed_grad/ppermute | solution.py:900
  95.5 14.0 %collective-permute-start.22 = (bf16[2,128,768]{2,1,0:T(8,128)(2,1)}, bf16[2,128,768]{2,1,0:T(8,128)(2,1)S(1)}, u32[]{:S(2)}, u32[]{:S(2)}) collective-permute-start(bf16[2,128,768]{2,1,0:T(8,128)(2,1)} %get-tuple-element.164.refs_12_), channel_id=1, source_target_pairs={{0,1},{1,0},{2,3},{3,2},{4,5},{5,4},{6,7},{7,6},{8,9},{9,8},{10,11... | collective-permute-start | bytes 1179656 | tf_op jit(solution)/shard_map/normed_grad/ppermute | solution.py:900
  95.9 17.3 %all-to-all-start.1 = ((bf16[4,128,512]{2,1,0:T(8,128)(2,1)}), bf16[4,128,512]{2,1,0:T(8,128)(2,1)S(1)}, u32[]{:S(2)}, u32[]{:S(2)}) async-start(bf16[4,128,512]{2,1,0:T(8,128)(2,1)} %get-tuple-element.154), calls=%async_computation.1 | async-start | bytes 1048576 | tf_op jit(solution)/shard_map/act_pre/all_to_all | solution.py:685
  109.9 10.6 %collective-permute-start.25 = (bf16[128,768]{1,0:T(8,128)(2,1)}, bf16[128,768]{1,0:T(8,128)(2,1)S(1)}, u32[]{:S(2)}, u32[]{:S(2)}) collective-permute-start(bf16[128,768]{1,0:T(8,128)(2,1)} %get-tuple-element.169), channel_id=1, source_target_pairs={{0,1},{1,0},{2,3},{3,2},{4,5},{5,4},{6,7},{7,6},{8,9},{9,8},{10,11... | collective-permute-start | bytes 589832 | tf_op jit(solution)/shard_map/grad_normed_one/ppermute | solution.py:695
  110.1 10.4 %collective-permute-start.26 = (bf16[128,768]{1,0:T(8,128)(2,1)}, bf16[128,768]{1,0:T(8,128)(2,1)S(1)}, u32[]{:S(2)}, u32[]{:S(2)}) collective-permute-start(bf16[128,768]{1,0:T(8,128)(2,1)} %get-tuple-element.170), channel_id=1, source_target_pairs={{0,2},{1,3},{2,0},{3,1},{4,6},{5,7},{6,4},{7,5},{8,10},{9,11},{10,... | collective-permute-start | bytes 589832 | tf_op jit(solution)/shard_map/grad_normed_one/ppermute | solution.py:695
  111.9 9.2 %collective-permute-start.27 = (bf16[128,768]{1,0:T(8,128)(2,1)}, bf16[128,768]{1,0:T(8,128)(2,1)S(1)}, u32[]{:S(2)}, u32[]{:S(2)}) collective-permute-start(bf16[128,768]{1,0:T(8,128)(2,1)} %get-tuple-element.171), channel_id=1, source_target_pairs={{0,3},{1,2},{2,1},{3,0},{4,7},{5,6},{6,5},{7,4},{8,11},{9,10},{10,... | collective-permute-start | bytes 589832 | tf_op jit(solution)/shard_map/grad_normed_one/ppermute | solution.py:695
  121.8 58.3 %all-to-all-start.2 = ((bf16[8,6,96,192]{3,2,1,0:T(8,128)(2,1)}), bf16[8,6,96,192]{3,2,1,0:T(8,128)(2,1)S(1)}, u32[]{:S(2)}, u32[]{:S(2)}) async-start(bf16[8,6,96,192]{3,2,1,0:T(8,128)(2,1)} %weight_grads.1), calls=%async_computation.2 | async-start | bytes 4718592 | tf_op jit(solution)/shard_map/weight_grads/all_to_all | solution.py:685
  180.1 7.5 %collective-permute-start.30 = (bf16[80,128]{1,0:T(8,128)(2,1)}, bf16[80,128]{1,0:T(8,128)(2,1)S(1)}, u32[]{:S(2)}, u32[]{:S(2)}) collective-permute-start(bf16[80,128]{1,0:T(8,128)(2,1)} %get-tuple-element.193), channel_id=1, source_target_pairs={{0,16},{4,20},{8,24},{12,28},{16,0},{20,4},{24,8},{28,12},{1,17},{... | collective-permute-start | bytes 61448 | tf_op jit(solution)/shard_map/table_outer/ppermute | solution.py:977
  191.2 12.1 %all-to-all-start.3 = ((f32[32,8,128]{2,1,0:T(8,128)}), f32[32,8,128]{2,1,0:T(8,128)S(1)}, u32[]{:S(2)}, u32[]{:S(2)}) async-start(f32[32,8,128]{2,1,0:T(8,128)} %get-tuple-element.197), calls=%async_computation.3 | async-start | bytes 262144 | tf_op jit(solution)/shard_map/squares/all_to_all | solution.py:685
  (55 other events, 372.3 us)

commit v4 on v3

--- a/solution.py
+++ b/solution.py
@@ -34,6 +34,9 @@
 PIECES = 3
 PIECE_ROWS = 16
 FIXED = 8192.0
+SPLIT = 112
+SPLIT_RECIPROCAL, SPLIT_SHIFT = 4682, 19
+HIGHS = [-(-(n * LANES) // (2 * SPLIT)) * 2 for n in CHUNKS]
 NOWHERE = 4095
 SCALE = HEAD_DIM**-0.5
 BF = jnp.bfloat16
@@ -58,7 +61,7 @@
     return [a * inner + b for b in range(inner) for a in range(size // inner)]
 
 
-def kernel_call(body, outs, name, micros, args, scratch=(), smem_in=(), placed=(), us_at=None, ready=(), limit=VMEM_BYTES):
+def kernel_call(body, outs, name, micros, args, scratch=(), smem_in=(), placed=(), us_at=None, ready=(), limit=VMEM_BYTES, early=()):
     n_in, n_out = len(args), len(outs)
     moved = [i for i in range(n_in) if i not in smem_in and i not in ready]
     blocks = [out[0] if isinstance(out, tuple) else 0 for out in outs]
@@ -86,7 +89,7 @@
             pltpu.make_async_copy(made[i].at[k] if blocks[i] else made[i], results[at], out_sems.at[at])
             for at, (i, k) in enumerate(flat)
         ]
-        for i in moved:
+        for i in [*early, *[i for i in moved if i not in early]]:
             for copy in arriving[i]:
                 copy.start()
         waiting, unsent = list(moved), list(range(n_out))
@@ -223,9 +226,9 @@
 def scatter_body(need, done, small_grads, sd, sp, sl, big_grads, bd, bp, bl, me, vector_rows, parcel, total):
     total[...] = jnp.zeros_like(total)
     sub = lax.broadcasted_iota(jnp.int32, (2 * SUB, LANES), 0)
-    low_pattern = [(sub + 2 * SUB * k).astype(F32).astype(BF) for k in range(LANES // (2 * SUB))]
+    low_pattern = [(sub + 2 * SUB * k).astype(F32).astype(BF) for k in range(SPLIT // (2 * SUB))]
     upper = (sub >= SUB).astype(jnp.int32)
-    high_pattern = [(2 * k + upper).astype(F32).astype(BF) for k in range(max(CHUNKS) // 2)]
+    high_pattern = [(2 * k + upper).astype(F32).astype(BF) for k in range(max(HIGHS) // 2)]
     zero, one = jnp.zeros((2 * SUB, LANES), BF), jnp.ones((2 * SUB, LANES), BF)
 
     def twice(value):
@@ -243,7 +246,10 @@
             for t in range(LOOKUPS):
                 left, right = [], []
                 for part, (index, lengths, _, _) in enumerate(parts):
-                    code = index[t] if t == 0 else jnp.where(lengths > t - 1, index[t], NOWHERE)
+                    high = index[t] * SPLIT_RECIPROCAL >> SPLIT_SHIFT
+                    code = (high << 7) | (index[t] - high * SPLIT)
+                    if t > 0:
+                        code = jnp.where(lengths > t - 1, code, NOWHERE)
                     for s in range(SUB):
                         spread = jnp.broadcast_to(code[s : s + 1], (SUB, LANES))
                         low = twice((spread & (LANES - 1)).astype(F32))
@@ -252,11 +258,11 @@
                         left.append(jnp.concatenate([jnp.where(low == p, one, zero) for p in low_pattern], axis=0))
                         right.append(
                             jnp.concatenate(
-                                [jnp.where(high == p, source, zero) for p in high_pattern[: CHUNKS[t] // 2]], axis=0
+                                [jnp.where(high == p, source, zero) for p in high_pattern[: HIGHS[t] // 2]], axis=0
                             )
                         )
-                span = slice(SUB * FIRST[t], SUB * (FIRST[t] + CHUNKS[t]))
-                total[:, span] += dot(jnp.concatenate(left, axis=1), jnp.concatenate(right, axis=1), NT)
+                span = slice(0, SUB * HIGHS[t])
+                total[t, :, span] += dot(jnp.concatenate(left, axis=1), jnp.concatenate(right, axis=1), NT)
 
         return run
 
@@ -269,7 +275,17 @@
     inner, outer, height, _ = parcel.shape
     height -= VECTOR_ROWS
     parcel[:, :, :VECTOR_ROWS, :] = vector_rows[...]
-    table = total[...].T.astype(BF)
+    chunks = []
+    for t in range(LOOKUPS):
+        rows = total[t, :, 0 : SUB * HIGHS[t]].T
+        for c in range(CHUNKS[t]):
+            first, last = c * LANES, (c + 1) * LANES
+            pieces = []
+            for high in range(first // SPLIT, (last - 1) // SPLIT + 1):
+                start, end = max(first - high * SPLIT, 0), min(last - high * SPLIT, SPLIT)
+                pieces.append(rows[SUB * high : SUB * (high + 1), start:end])
+            chunks.append(jnp.concatenate(pieces, axis=1))
+    table = jnp.concatenate(chunks, axis=0).astype(BF)
     for d in range(inner * outer):
         at = me[1] ^ d
         parcel[at % inner, at // inner, VECTOR_ROWS:, :] = table[d * height : (d + 1) * height]
@@ -486,11 +502,12 @@
     weights, refs = refs[5 : 5 + n_head], refs[5 + n_head :]
     layer_out, grad_hidden, sums, pre_sums, normed_grad, act_pre = refs[:6]
     grad_heads = refs[6:]
-    need(*range(2 * n_head + 5))
+    need(*range(n_head + 5))
     columns = mixed[0].shape[1]
     slot = parcel_slot(columns)
     hidden = rows[...].astype(F32) + vectors[6:7, :]
     for r in range(n_head):
+        need(n_head + 5 + r)
         hidden = hidden + dot(mixed[r][...], whole_matrix(weights[r], 0), NT)
     xhat, spread = norm_parts(hidden)
     low = (xhat * vectors[2:3, :] + vectors[3:4, :]).astype(BF)
@@ -601,24 +618,21 @@
     return (weight_new, first_new, second_new)
 
 
-def shard_body(need, done, arrived, shards, squares):
+def told_body(need, done, arrived, *refs):
+    parts, (shards, shard, told) = refs[:-3], refs[-3:]
     need(0)
-    value = arrived[0].astype(F32)
+    rest = arrived[0].astype(F32)
     for d in range(1, arrived.shape[0]):
-        value = value + arrived[d].astype(F32)
-    shards[...] = value
-    squares[...] = jnp.broadcast_to(jnp.sum(value * value).reshape(1, 1), squares.shape)
-
-
-def told_body(need, done, *refs):
-    parts, (squares, shard, told) = refs[:-3], refs[-3:]
-    need(*range(len(parts) + 1))
+        rest = rest + arrived[d].astype(F32)
+    shards[...] = rest
+    done(0)
+    need(*range(1, len(parts) + 1))
     value = parts[0][...].astype(F32)
     for part in parts[1:]:
         value = value + part[...].astype(F32)
     table = value[VECTOR_ROWS:]
     shard[...] = table
-    here = jnp.sum(table * table).reshape(1, 1) + squares[0:1, 0:1]
+    here = jnp.sum(table * table).reshape(1, 1) + jnp.sum(rest * rest).reshape(1, 1)
     tail = value[MESSAGE_ROWS : MESSAGE_ROWS + 1]
     free = LANES // 4
     gap = jnp.zeros((1, LANES - free), F32)
@@ -788,7 +802,7 @@
         rest = rest - piece
         pieces.append(jnp.pad(piece.astype(BF), ((0, PIECE_ROWS - n_vectors), (0, columns - lanes_used))))
     qkv_sent = jnp.concatenate([qkv_sent.reshape(3 * shard_rows, columns), *pieces])
-    table_all, qkv_sent, *rest_far = lax.optimization_barrier((table_all, qkv_sent, *rest_far))
+    qkv_sent, *rest_far = lax.optimization_barrier((qkv_sent, *rest_far))
     with jax.named_scope("rest_near"):
         rest_near = near_shards(rest_far)
     with jax.named_scope("qkv_far"):
@@ -934,6 +948,7 @@
         (*given, *mixed, us, act_pre, normed_one, dqkv, *[rows_held[r] for r in range(n_head)]),
         (),
         (2 * n_head,),
+        early=(2 * n_head + 2, 2 * n_head + 3),
     )
     if not stacked:
         weight_grads = weight_grads.reshape(6, n_dp, shard_rows, columns).transpose(1, 0, 2, 3)
@@ -959,7 +974,7 @@
         "table_scatter",
         40,
         (small_rows, *small_ints, big_rows, *big_ints, us, vector_rows),
-        [pltpu.VMEM((LANES, all_chunks * heads), F32)],
+        [pltpu.VMEM((LOOKUPS, SPLIT, SUB * max(HIGHS)), F32)],
         (8,),
     )
     with jax.named_scope("table_inner"):
@@ -971,24 +986,21 @@
         1,
         tuple(arrived),
     )
-    weights_arrived, *outer_sent = lax.optimization_barrier((weights_arrived, *outer_sent))
     with jax.named_scope("table_outer"):
         parts = [outer_sent[0]] + [
             lax.ppermute(outer_sent[k], "dp", dp_pairs(k * inner)) for k in range(1, outer)
         ]
-    shards, squares = kernel_call(
-        shard_body,
-        [struct((6, shard_rows, columns), F32), struct((1, LANES), F32)],
+    weights_arrived, *parts = lax.optimization_barrier((weights_arrived, *parts))
+    shards, table_shard, told = kernel_call(
+        told_body,
+        [
+            struct((6, shard_rows, columns), F32),
+            struct((table_rows, LANES), F32),
+            struct((n_dp * n_head, MESSAGE_ROWS, LANES), F32),
+        ],
         "shard_sums",
-        3,
-        (weights_arrived,),
-    )
-    table_shard, told = kernel_call(
-        told_body,
-        [struct((table_rows, LANES), F32), struct((n_dp * n_head, MESSAGE_ROWS, LANES), F32)],
-        "table_sums",
-        1,
-        (*parts, squares),
+        4,
+        (weights_arrived, *parts),
     )
     with jax.named_scope("squares"):
         told = exchange(told, everyone)

time: 208 us -> 205 us (0.986)
  starting transfers between devices: 46.7 us -> 56.2 us
  Pallas kernels: 114 us -> 106 us
  waiting for transfers between devices: 29.4 us -> 22.1 us
  local copies, waits for them, and re-layouts: 11.8 us -> 14.2 us
    all_to_all x4, waiting for transfers between devices: 16.3 us -> 7.78 us  [exchange(): return lax.all_to_all(value, axis, split_axis=0, concat_axis=0, tiled=True)]
    pallas_call x12 -> x11, Pallas kernels: 114 us -> 106 us  [kernel_call(): pl.pallas_call(wrapped, out_shape=tuple((shapes[i] for i, _ in flat)), in...]
    ppermute x3, starting transfers between devices: 4.39 us -> 10.1 us  [on_device(): lax.ppermute(outer_sent[k], 'dp', dp_pairs(k * inner))]
    ppermute x3, waiting for transfers between devices: 1.08 us -> 4.95 us  [on_device(): lax.ppermute(outer_sent[k], 'dp', dp_pairs(k * inner))]
    ppermute x1, waiting for transfers between devices: 5.46 us -> 2.63 us  [on_device(): lax.ppermute(inner_sent[k], 'dp', dp_pairs(k))]
  transfers between devices with their start and end apart: 36 -> 36, of which waited for: 11 -> 10; matrix products, arithmetic and copies ran while one was open for 3% -> 4% of each run, Pallas kernels for 49% -> 45%
where the time goes in v4:
time: 205 us; the launch traced here: 204 us
  Pallas kernels  106 us (52%)
  starting transfers between devices  56.2 us (27%)
  waiting for transfers between devices  22.1 us (11%)
  local copies, waits for them, and re-layouts  14.2 us (7%)
  other arithmetic  3.45 us (2%)
  between operations  2.26 us (1%)
    pallas_call x11, Pallas kernels, kernel_call(): pl.pallas_call(wrapped, out_shape=tuple((shapes[i] for i, _ in flat)), in...  106 us
    all_to_all x4, starting transfers between devices, exchange(): return lax.all_to_all(value, axis, split_axis=0, concat_axis=0, tiled=True)  18.5 us
    ppermute x6, starting transfers between devices, far_shards(): lax.ppermute(value, 'dp', dp_pairs(k))  10.2 us
    ppermute x3, starting transfers between devices, on_device(): lax.ppermute(outer_sent[k], 'dp', dp_pairs(k * inner))  10.1 us
    unnamed x89, local copies, waits for them, and re-layouts  9.7 us
    all_to_all x4, waiting for transfers between devices, exchange(): return lax.all_to_all(value, axis, split_axis=0, concat_axis=0, tiled=True)  7.78 us
    ppermute x9, starting transfers between devices, swap(): lax.ppermute(values[r], 'head', [(i, i ^ r) for i in range(n_head)])  5.83 us
    ppermute x9, waiting for transfers between devices, swap(): lax.ppermute(values[r], 'head', [(i, i ^ r) for i in range(n_head)])  5.36 us
  transfers between devices with their start and end apart: 36, of which 10 were waited for; matrix products, arithmetic and copies ran while one was open for 4% of the time, Pallas kernels for 45%

profile of v4, /device:TPU:0, one launch (start us, length us, event | category | flops | bytes accessed | tf_op | source)
XLA Modules:
  0.0 204.3 jit_solution(5340858971421026648)
XLA Ops:
  3.8 5.1 %collective-permute-start.5 = (bf16[3,96,192]{2,1,0:T(8,128)(2,1)S(1)}, bf16[3,96,192]{2,1,0:T(8,128)(2,1)S(1)}, u32[]{:S(2)}, u32[]{:S(2)}) collective-permute-start(bf16[3,96,192]{2,1,0:T(8,128)(2,1)S(1)} %pad_maximum_fusion.4), channel_id=1, source_target_pairs={{0,24},{4,28},{8,16},{12,20},{16,8},{20,12},{24,0},{28,4},{1,25},{... | collective-permute-start | bytes 331784 | tf_op jit(solution)/shard_map/rest_far/ppermute | solution.py:768
  12.8 5.8 %all-to-all-start = ((bf16[8,8,8,128]{3,2,1,0:T(8,128)(2,1)}), bf16[8,8,8,128]{3,2,1,0:T(8,128)(2,1)S(1)}, u32[]{:S(2)}, u32[]{:S(2)}) async-start(bf16[8,8,8,128]{3,2,1,0:T(8,128)(2,1)} %broadcast_in_dim.4), calls=%async_computation | async-start | bytes 262144 | tf_op jit(solution)/shard_map/table_all/all_to_all | solution.py:699
  22.2 3.9 %collective-permute-start.9 = (bf16[336,192]{1,0:T(8,128)(2,1)S(1)}, bf16[336,192]{1,0:T(8,128)(2,1)S(1)}, u32[]{:S(2)}, u32[]{:S(2)}) collective-permute-start(bf16[336,192]{1,0:T(8,128)(2,1)S(1)} %fusion.6), channel_id=1, source_target_pairs={{0,24},{4,28},{8,16},{12,20},{16,8},{20,12},{24,0},{28,4},{1,25},{... | collective-permute-start | bytes 387080 | tf_op jit(solution)/shard_map/qkv_far/ppermute | solution.py:768
  26.7 2.1 %collective-permute-start.6 = (bf16[4,3,96,192]{3,2,1,0:T(8,128)(2,1)S(1)}, bf16[4,3,96,192]{3,2,1,0:T(8,128)(2,1)S(1)}, u32[]{:S(2)}, u32[]{:S(2)}) collective-permute-start(bf16[4,3,96,192]{3,2,1,0:T(8,128)(2,1)S(1)} %pad_maximum_fusion.2), channel_id=1, source_target_pairs={{0,4},{4,0},{8,12},{12,8},{16,20},{20,16},{24,28},{28,24},{1,5},{5... | collective-permute-start | bytes 1327112 | tf_op jit(solution)/shard_map/rest_near/ppermute | solution.py:772
  29.5 13.2 %pair_bias.2 = (f32[8,2,64,128]{3,2,1,0:T(8,128)}, f32[8,2,64,128]{3,2,1,0:T(8,128)}) custom-call(bf16[512,128]{1,0:T(8,128)(2,1)} %bitcast.62, s32[4,64,64]{2,1,0:T(8,128)} %refs_1_.5, s32[5,4,64,64]{3,2,1,0:T(8,128)} %refs_2_.5, s32[4,64,64]{2,1,0:T(8,128)} %refs_3_.5, s32[1,256,256]{2,1,0:T(8,128)} %refs_5_.8, s32[5,1,256,256]{3,2,1,0:T(8,128)} %refs_6_.8, ...), custom_call_target="tpu_custom_call" | custom-call | flops 12000000000 | bytes 1048576 | tf_op jit(solution)/shard_map/pair_bias/pallas_call | solution.py:120
  47.8 18.5 %pair_bias.3.refs_10_ = f32[8,2,192,128]{3,2,1,0:T(8,128)} custom-call(bf16[512,128]{1,0:T(8,128)(2,1)} %bitcast.63, s32[1,256,256]{2,1,0:T(8,128)} %refs_5_.8, s32[5,1,256,256]{3,2,1,0:T(8,128)} %refs_6_.8, s32[1,256,256]{2,1,0:T(8,128)} %refs_7_.2), custom_call_target="tpu_custom_call" | custom-call | flops 20000000000 | bytes 1048576 | tf_op jit(solution)/shard_map/pair_bias/pallas_call | solution.py:120
  68.0 7.7 %attend_forward.1 = (bf16[512,768]{1,0:T(8,128)(2,1)}, bf16[3,512,192]{2,1,0:T(8,128)(2,1)}, f32[8,256,256]{2,1,0:T(8,128)}, f32[8,2,128,128]{3,2,1,0:T(8,128)},...) custom-call(bf16[2,128,768]{2,1,0:T(8,128)(2,1)} %copy-done.20, ...), custom_call_target="tpu_custom_call" | custom-call | flops 12000000000 | bytes 1048576 | tf_op jit(solution)/shard_map/attend_forward/pallas_call | solution.py:120
  79.0 2.3 %collective-permute-done.16.refs_2_ = bf16[128,192]{1,0:T(8,128)(2,1)S(1)} collective-permute-done((bf16[128,192]{1,0:T(8,128)(2,1)}, bf16[128,192]{1,0:T(8,128)(2,1)S(1)}, u32[]{:S(2)}, u32[]{:S(2)}) %collective-permute-start.16) | collective-permute-done | bytes 49184 | tf_op jit(solution)/shard_map/mixed_rows/ppermute | solution.py:709
  82.4 7.5 %feed_forward.1 = (bf16[128,768]{1,0:T(8,128)(2,1)}, f32[128,768]{1,0:T(8,128)}, f32[4,768]{1,0:T(4,128)}, f32[4,192]{1,0:T(4,128)}, bf16[2,128,768]{2,1,0:T(8,1...) custom-call(bf16[128,192]{1,0:T(8,128)(2,1)} %get-tuple-element.141., ...), custom_call_target="tpu_custom_call" | custom-call | flops 6000000000 | bytes 1048576 | tf_op jit(solution)/shard_map/feed_forward/pallas_call | solution.py:120
  93.5 3.6 %all-to-all-start.1 = ((bf16[4,128,512]{2,1,0:T(8,128)(2,1)}), bf16[4,128,512]{2,1,0:T(8,128)(2,1)S(1)}, u32[]{:S(2)}, u32[]{:S(2)}) async-start(bf16[4,128,512]{2,1,0:T(8,128)(2,1)} %get-tuple-element.151), calls=%async_computation.1 | async-start | bytes 1048576 | tf_op jit(solution)/shard_map/act_pre/all_to_all | solution.py:699
  97.8 9.2 %attend_backward.1 = (f32[1024,128]{1,0:T(8,128)}, f32[4096,128]{1,0:T(8,128)}, bf16[3,512,192]{2,1,0:T(8,128)(2,1)}, f32[2,4,192]{2,1,0:T(4,128)}, bf16[128,768...) custom-call(bf16[128,192]{1,0:T(8,128)(2,1)} %get-tuple-element.153.refs_0_, ...), custom_call_target="tpu_custom_call" | custom-call | flops 14000000000 | bytes 1048576 | tf_op jit(solution)/shard_map/attend_backward/pallas_call | solution.py:120
  111.3 5.7 %weight_grads.1 = bf16[8,6,96,192]{3,2,1,0:T(8,128)(2,1)} custom-call(bf16[2,128,768]{2,1,0:T(8,128)(2,1)} %copy-done.20, bf16[2,128,768]{2,1,0:T(8,128)(2,1)} %copy-done.25, bf16[2,128,768]{2,1,0:T(8,128)(2,1)} %collective-permute-done.refs_2_, bf16[2,128,768]{2,1,0:T(8,128)(2,1)} %copy-done.26, bf16[128,192]{1,0:T(8,128)(2,1)} %get-tuple-element.141.refs_0_.refs_4_, ...), custom_call_target="tpu_custom_call" | custom-call | flops 6000000000 | bytes 1048576 | tf_op jit(solution)/shard_map/weight_grads/pallas_call | solution.py:120
  119.6 5.4 %all-to-all-start.2 = ((bf16[8,6,96,192]{3,2,1,0:T(8,128)(2,1)}), bf16[8,6,96,192]{3,2,1,0:T(8,128)(2,1)S(1)}, u32[]{:S(2)}, u32[]{:S(2)}) async-start(bf16[8,6,96,192]{3,2,1,0:T(8,128)(2,1)} %weight_grads.1), calls=%async_computation.2 | async-start | bytes 4718592 | tf_op jit(solution)/shard_map/weight_grads/all_to_all | solution.py:699
  124.9 3.3 %input_grad.1 = (bf16[128,768]{1,0:T(8,128)(2,1)}, bf16[2,4,16,128]{3,2,1,0:T(8,128)(2,1)}) custom-call(bf16[128,768]{1,0:T(8,128)(2,1)} %get-tuple-element.169.refs_0_, bf16[128,768]{1,0:T(8,128)(2,1)} %copy-done.30, bf16[128,768]{1,0:T(8,128)(2,1)} %copy-done.31, bf16[128,768]{1,0:T(8,128)(2,1)} %copy-done.32, s32[2]{0:T(128)} %pad_add_fusion.refs_4_.refs_8_.refs_0_, ...), custom_call_target="tpu_custom_call" | custom-call | flops 3000000000 | bytes 1048576 | tf_op jit(solution)/shard_map/input_grad/pallas_call | solution.py:120
  128.2 33.6 %table_scatter.1 = (bf16[4,80,128]{2,1,0:T(8,128)(2,1)}, bf16[4,80,128]{2,1,0:T(8,128)(2,1)}) custom-call(f32[1024,128]{1,0:T(8,128)} %get-tuple-element.179.refs_0_, s32[4,64,64]{2,1,0:T(8,128)} %refs_1_.5, s32[5,4,64,64]{3,2,1,0:T(8,128)} %refs_2_.5, s32[4,64,64]{2,1,0:T(8,128)} %refs_3_.5, f32[4096,128]{1,0:T(8,128)} %get-tuple-element.180.refs_4_, ...), custom_call_target="tpu_custom_call" | custom-call | flops 40000000000 | bytes 1048576 | tf_op jit(solution)/shard_map/table_scatter/pallas_call | solution.py:120
  161.8 2.1 %collective-permute-start.28 = (bf16[4,80,128]{2,1,0:T(8,128)(2,1)}, bf16[4,80,128]{2,1,0:T(8,128)(2,1)S(1)}, u32[]{:S(2)}, u32[]{:S(2)}) collective-permute-start(bf16[4,80,128]{2,1,0:T(8,128)(2,1)} %get-tuple-element.183), channel_id=1, source_target_pairs={{0,4},{4,0},{8,12},{12,8},{16,20},{20,16},{24,28},{28,24},{1,5},{5... | collective-permute-start | bytes 245768 | tf_op jit(solution)/shard_map/table_inner/ppermute | solution.py:981
  163.9 2.6 %collective-permute-done.28.refs_1_ = bf16[4,80,128]{2,1,0:T(8,128)(2,1)S(1)} collective-permute-done((bf16[4,80,128]{2,1,0:T(8,128)(2,1)}, bf16[4,80,128]{2,1,0:T(8,128)(2,1)S(1)}, u32[]{:S(2)}, u32[]{:S(2)}) %collective-permute-start.28) | collective-permute-done | bytes 81952 | tf_op jit(solution)/shard_map/table_inner/ppermute | solution.py:981
  168.8 2.1 %collective-permute-start.29 = (bf16[80,128]{1,0:T(8,128)(2,1)}, bf16[80,128]{1,0:T(8,128)(2,1)S(1)}, u32[]{:S(2)}, u32[]{:S(2)}) collective-permute-start(bf16[80,128]{1,0:T(8,128)(2,1)} %get-tuple-element.185), channel_id=1, source_target_pairs={{0,8},{4,12},{8,0},{12,4},{16,24},{20,28},{24,16},{28,20},{1,9},{5... | collective-permute-start | bytes 61448 | tf_op jit(solution)/shard_map/table_outer/ppermute | solution.py:991
  170.9 7.2 %collective-permute-start.30 = (bf16[80,128]{1,0:T(8,128)(2,1)}, bf16[80,128]{1,0:T(8,128)(2,1)S(1)}, u32[]{:S(2)}, u32[]{:S(2)}) collective-permute-start(bf16[80,128]{1,0:T(8,128)(2,1)} %get-tuple-element.186), channel_id=1, source_target_pairs={{0,16},{4,20},{8,24},{12,28},{16,0},{20,4},{24,8},{28,12},{1,17},{... | collective-permute-start | bytes 61448 | tf_op jit(solution)/shard_map/table_outer/ppermute | solution.py:991
  180.4 3.5 %collective-permute-done.31.refs_4_ = bf16[80,128]{1,0:T(8,128)(2,1)S(1)} collective-permute-done((bf16[80,128]{1,0:T(8,128)(2,1)}, bf16[80,128]{1,0:T(8,128)(2,1)S(1)}, u32[]{:S(2)}, u32[]{:S(2)}) %collective-permute-start.31) | collective-permute-done | bytes 20512 | tf_op jit(solution)/shard_map/table_outer/ppermute | solution.py:991
  185.3 3.0 %shard_sums.1 = (f32[6,96,192]{2,1,0:T(8,128)}, f32[64,128]{1,0:T(8,128)}, f32[32,8,128]{2,1,0:T(8,128)}) custom-call(bf16[8,6,96,192]{3,2,1,0:T(8,128)(2,1)} %copy-done.18, bf16[80,128]{1,0:T(8,128)(2,1)} %get-tuple-element.189.refs_1_, bf16[80,128]{1,0:T(8,128)(2,1)} %copy-done.40, bf16[80,128]{1,0:T(8,128)(2,1)} %copy-done.41, bf16[80,128]{1,0:T(8,128)(2,1)} %copy-done.42), custom_call_target="tpu_custom_call" | custom-call | flops 4000000000 | bytes 1048576 | tf_op jit(solution)/shard_map/shard_sums/pallas_call | solution.py:120
  188.5 3.7 %all-to-all-start.3 = ((f32[32,8,128]{2,1,0:T(8,128)}), f32[32,8,128]{2,1,0:T(8,128)S(1)}, u32[]{:S(2)}, u32[]{:S(2)}) async-start(f32[32,8,128]{2,1,0:T(8,128)} %get-tuple-element.193), calls=%async_computation.3 | async-start | bytes 262144 | tf_op jit(solution)/shard_map/squares/all_to_all | solution.py:699
  193.5 6.9 %all-to-all-done.3.refs_1_ = f32[32,8,128]{2,1,0:T(8,128)S(1)} async-done(((f32[32,8,128]{2,1,0:T(8,128)}), f32[32,8,128]{2,1,0:T(8,128)S(1)}, u32[]{:S(2)}, u32[]{:S(2)}) %all-to-all-start.3) | async-done | bytes 131104 | tf_op jit(solution)/shard_map/squares/all_to_all | solution.py:699
  201.3 2.8 %update.1 = (f32[4,96,192]{2,1,0:T(8,128)}, f32[4,96,192]{2,1,0:T(8,128)}, f32[4,96,192]{2,1,0:T(8,128)}, f32[192,96]{1,0:T(8,128)}, f32[192,96]{1,0:T(8,128)}, ...) custom-call(s32[2]{0:T(128)S(1)} %copy-done.16, ...), custom_call_target="tpu_custom_call" | custom-call | flops 3000000000 | bytes 1048576 | tf_op jit(solution)/shard_map/update/pallas_call | solution.py:120
  (170 shorter events, 41.1 us)
Async XLA Ops:
  3.8 17.0 %collective-permute-start.5 = (bf16[3,96,192]{2,1,0:T(8,128)(2,1)S(1)}, bf16[3,96,192]{2,1,0:T(8,128)(2,1)S(1)}, u32[]{:S(2)}, u32[]{:S(2)}) collective-permute-start(bf16[3,96,192]{2,1,0:T(8,128)(2,1)S(1)} %pad_maximum_fusion.4), channel_id=1, source_target_pairs={{0,24},{4,28},{8,16},{12,20},{16,8},{20,12},{24,0},{28,4},{1,25},{... | collective-permute-start | bytes 331784 | tf_op jit(solution)/shard_map/rest_far/ppermute | solution.py:768
  8.9 13.2 %collective-permute-start.4 = (bf16[3,96,192]{2,1,0:T(8,128)(2,1)S(1)}, bf16[3,96,192]{2,1,0:T(8,128)(2,1)S(1)}, u32[]{:S(2)}, u32[]{:S(2)}) collective-permute-start(bf16[3,96,192]{2,1,0:T(8,128)(2,1)S(1)} %pad_maximum_fusion.4), channel_id=1, source_target_pairs={{0,16},{4,20},{8,24},{12,28},{16,0},{20,4},{24,8},{28,12},{1,17},{... | collective-permute-start | bytes 331784 | tf_op jit(solution)/shard_map/rest_far/ppermute | solution.py:768
  8.9 13.2 %collective-permute-start.3 = (bf16[3,96,192]{2,1,0:T(8,128)(2,1)S(1)}, bf16[3,96,192]{2,1,0:T(8,128)(2,1)S(1)}, u32[]{:S(2)}, u32[]{:S(2)}) collective-permute-start(bf16[3,96,192]{2,1,0:T(8,128)(2,1)S(1)} %pad_maximum_fusion.4), channel_id=1, source_target_pairs={{0,8},{4,12},{8,0},{12,4},{16,24},{20,28},{24,16},{28,20},{1,9},{5... | collective-permute-start | bytes 331784 | tf_op jit(solution)/shard_map/rest_far/ppermute | solution.py:768
  12.8 16.1 %all-to-all-start = ((bf16[8,8,8,128]{3,2,1,0:T(8,128)(2,1)}), bf16[8,8,8,128]{3,2,1,0:T(8,128)(2,1)S(1)}, u32[]{:S(2)}, u32[]{:S(2)}) async-start(bf16[8,8,8,128]{3,2,1,0:T(8,128)(2,1)} %broadcast_in_dim.4), calls=%async_computation | async-start | bytes 262144 | tf_op jit(solution)/shard_map/table_all/all_to_all | solution.py:699
  18.7 24.2 %collective-permute-start = (bf16[2,128,768]{2,1,0:T(8,128)(2,1)S(1)}, bf16[2,128,768]{2,1,0:T(8,128)(2,1)}, u32[]{:S(2)}, u32[]{:S(2)}) collective-permute-start(bf16[2,128,768]{2,1,0:T(8,128)(2,1)S(1)} %pad_maximum_fusion.3.refs_0_), channel_id=1, source_target_pairs={{0,2},{1,3},{2,0},{3,1},{4,6},{5,7},{6,4},{7,5},{8,10},{9,11},{10,... | collective-permute-start | bytes 1179656 | tf_op jit(solution)/shard_map/rows_far/ppermute | solution.py:775
  22.2 20.6 %collective-permute-start.9 = (bf16[336,192]{1,0:T(8,128)(2,1)S(1)}, bf16[336,192]{1,0:T(8,128)(2,1)S(1)}, u32[]{:S(2)}, u32[]{:S(2)}) collective-permute-start(bf16[336,192]{1,0:T(8,128)(2,1)S(1)} %fusion.6), channel_id=1, source_target_pairs={{0,24},{4,28},{8,16},{12,20},{16,8},{20,12},{24,0},{28,4},{1,25},{... | collective-permute-start | bytes 387080 | tf_op jit(solution)/shard_map/qkv_far/ppermute | solution.py:768
  26.0 16.8 %collective-permute-start.8 = (bf16[336,192]{1,0:T(8,128)(2,1)S(1)}, bf16[336,192]{1,0:T(8,128)(2,1)S(1)}, u32[]{:S(2)}, u32[]{:S(2)}) collective-permute-start(bf16[336,192]{1,0:T(8,128)(2,1)S(1)} %fusion.6), channel_id=1, source_target_pairs={{0,16},{4,20},{8,24},{12,28},{16,0},{20,4},{24,8},{28,12},{1,17},{... | collective-permute-start | bytes 387080 | tf_op jit(solution)/shard_map/qkv_far/ppermute | solution.py:768
  26.0 16.8 %collective-permute-start.7 = (bf16[336,192]{1,0:T(8,128)(2,1)S(1)}, bf16[336,192]{1,0:T(8,128)(2,1)S(1)}, u32[]{:S(2)}, u32[]{:S(2)}) collective-permute-start(bf16[336,192]{1,0:T(8,128)(2,1)S(1)} %fusion.6), channel_id=1, source_target_pairs={{0,8},{4,12},{8,0},{12,4},{16,24},{20,28},{24,16},{28,20},{1,9},{5... | collective-permute-start | bytes 387080 | tf_op jit(solution)/shard_map/qkv_far/ppermute | solution.py:768
  26.7 16.1 %collective-permute-start.6 = (bf16[4,3,96,192]{3,2,1,0:T(8,128)(2,1)S(1)}, bf16[4,3,96,192]{3,2,1,0:T(8,128)(2,1)S(1)}, u32[]{:S(2)}, u32[]{:S(2)}) collective-permute-start(bf16[4,3,96,192]{3,2,1,0:T(8,128)(2,1)S(1)} %pad_maximum_fusion.2), channel_id=1, source_target_pairs={{0,4},{4,0},{8,12},{12,8},{16,20},{20,16},{24,28},{28,24},{1,5},{5... | collective-permute-start | bytes 1327112 | tf_op jit(solution)/shard_map/rest_near/ppermute | solution.py:772
  42.8 23.5 %collective-permute-start.11 = (bf16[2,128,768]{2,1,0:T(8,128)(2,1)S(1)}, bf16[2,128,768]{2,1,0:T(8,128)(2,1)S(1)}, u32[]{:S(2)}, u32[]{:S(2)}) collective-permute-start(bf16[2,128,768]{2,1,0:T(8,128)(2,1)S(1)} %pad_maximum_fusion.3.refs_0_), channel_id=1, source_target_pairs={{0,1},{1,0},{2,3},{3,2},{4,5},{5,4},{6,7},{7,6},{8,9},{9,8},{10,11... | collective-permute-start | bytes 1179656 | tf_op jit(solution)/shard_map/rows_near/ppermute | solution.py:775
  44.6 31.1 %collective-permute-start.14 = (bf16[8,3,96,192]{3,2,1,0:T(8,128)(2,1)}, bf16[8,3,96,192]{3,2,1,0:T(8,128)(2,1)}, u32[]{:S(2)}, u32[]{:S(2)}) collective-permute-start(bf16[8,3,96,192]{3,2,1,0:T(8,128)(2,1)} %constant_dynamic-update-slice_fusion.refs_9_), channel_id=1, source_target_pairs={{0,2},{1,3},{2,0},{3,1},{4,6},{5,7},{6,4},{7,5},{8,10},{9,11},{10,... | collective-permute-start | bytes 2654216 | tf_op jit(solution)/shard_map/rest_far_head/ppermute | solution.py:775
  46.2 29.5 %collective-permute-start.13 = (bf16[8,3,96,192]{3,2,1,0:T(8,128)(2,1)}, bf16[8,3,96,192]{3,2,1,0:T(8,128)(2,1)}, u32[]{:S(2)}, u32[]{:S(2)}) collective-permute-start(bf16[8,3,96,192]{3,2,1,0:T(8,128)(2,1)} %constant_dynamic-update-slice_fusion.refs_9_), channel_id=1, source_target_pairs={{0,1},{1,0},{2,3},{3,2},{4,5},{5,4},{6,7},{7,6},{8,9},{9,8},{10,11... | collective-permute-start | bytes 2654216 | tf_op jit(solution)/shard_map/rest_near_head/ppermute | solution.py:775
  46.4 19.9 %collective-permute-start.12 = (bf16[2,128,768]{2,1,0:T(8,128)(2,1)}, bf16[2,128,768]{2,1,0:T(8,128)(2,1)S(1)}, u32[]{:S(2)}, u32[]{:S(2)}) collective-permute-start(bf16[2,128,768]{2,1,0:T(8,128)(2,1)} %collective-permute-done.refs_2_), channel_id=1, source_target_pairs={{0,1},{1,0},{2,3},{3,2},{4,5},{5,4},{6,7},{7,6},{8,9},{9,8},{10,11... | collective-permute-start | bytes 1179656 | tf_op jit(solution)/shard_map/rows_near/ppermute | solution.py:775
  47.2 19.1 %collective-permute-start.10 = (bf16[4,336,192]{1,2,0:T(8,128)(2,1)S(1)}, bf16[4,336,192]{1,2,0:T(8,128)(2,1)S(1)}, u32[]{:S(2)}, u32[]{:S(2)}) collective-permute-start(bf16[4,336,192]{1,2,0:T(8,128)(2,1)S(1)} %copy.49), channel_id=1, source_target_pairs={{0,4},{4,0},{8,12},{12,8},{16,20},{20,16},{24,28},{28,24},{1,5},{5... | collective-permute-start | bytes 1548296 | tf_op jit(solution)/shard_map/qkv_near/ppermute | solution.py:772
  91.9 15.2 %collective-permute-start.23 = (bf16[2,128,768]{2,1,0:T(8,128)(2,1)}, bf16[2,128,768]{2,1,0:T(8,128)(2,1)S(1)}, u32[]{:S(2)}, u32[]{:S(2)}) collective-permute-start(bf16[2,128,768]{2,1,0:T(8,128)(2,1)} %get-tuple-element.161.refs_12_), channel_id=1, source_target_pairs={{0,2},{1,3},{2,0},{3,1},{4,6},{5,7},{6,4},{7,5},{8,10},{9,11},{10,... | collective-permute-start | bytes 1179656 | tf_op jit(solution)/shard_map/normed_grad/ppermute | solution.py:914
  93.5 13.6 %collective-permute-start.22 = (bf16[2,128,768]{2,1,0:T(8,128)(2,1)}, bf16[2,128,768]{2,1,0:T(8,128)(2,1)S(1)}, u32[]{:S(2)}, u32[]{:S(2)}) collective-permute-start(bf16[2,128,768]{2,1,0:T(8,128)(2,1)} %get-tuple-element.161.refs_12_), channel_id=1, source_target_pairs={{0,1},{1,0},{2,3},{3,2},{4,5},{5,4},{6,7},{7,6},{8,9},{9,8},{10,11... | collective-permute-start | bytes 1179656 | tf_op jit(solution)/shard_map/normed_grad/ppermute | solution.py:914
  93.5 16.9 %all-to-all-start.1 = ((bf16[4,128,512]{2,1,0:T(8,128)(2,1)}), bf16[4,128,512]{2,1,0:T(8,128)(2,1)S(1)}, u32[]{:S(2)}, u32[]{:S(2)}) async-start(bf16[4,128,512]{2,1,0:T(8,128)(2,1)} %get-tuple-element.151), calls=%async_computation.1 | async-start | bytes 1048576 | tf_op jit(solution)/shard_map/act_pre/all_to_all | solution.py:699
  107.6 9.5 %collective-permute-start.25 = (bf16[128,768]{1,0:T(8,128)(2,1)}, bf16[128,768]{1,0:T(8,128)(2,1)S(1)}, u32[]{:S(2)}, u32[]{:S(2)}) collective-permute-start(bf16[128,768]{1,0:T(8,128)(2,1)} %get-tuple-element.166), channel_id=1, source_target_pairs={{0,1},{1,0},{2,3},{3,2},{4,5},{5,4},{6,7},{7,6},{8,9},{9,8},{10,11... | collective-permute-start | bytes 589832 | tf_op jit(solution)/shard_map/grad_normed_one/ppermute | solution.py:709
  107.7 9.4 %collective-permute-start.26 = (bf16[128,768]{1,0:T(8,128)(2,1)}, bf16[128,768]{1,0:T(8,128)(2,1)S(1)}, u32[]{:S(2)}, u32[]{:S(2)}) collective-permute-start(bf16[128,768]{1,0:T(8,128)(2,1)} %get-tuple-element.167), channel_id=1, source_target_pairs={{0,2},{1,3},{2,0},{3,1},{4,6},{5,7},{6,4},{7,5},{8,10},{9,11},{10,... | collective-permute-start | bytes 589832 | tf_op jit(solution)/shard_map/grad_normed_one/ppermute | solution.py:709
  109.5 9.4 %collective-permute-start.27 = (bf16[128,768]{1,0:T(8,128)(2,1)}, bf16[128,768]{1,0:T(8,128)(2,1)S(1)}, u32[]{:S(2)}, u32[]{:S(2)}) collective-permute-start(bf16[128,768]{1,0:T(8,128)(2,1)} %get-tuple-element.168), channel_id=1, source_target_pairs={{0,3},{1,2},{2,1},{3,0},{4,7},{5,6},{6,5},{7,4},{8,11},{9,10},{10,... | collective-permute-start | bytes 589832 | tf_op jit(solution)/shard_map/grad_normed_one/ppermute | solution.py:709
  119.6 64.3 %all-to-all-start.2 = ((bf16[8,6,96,192]{3,2,1,0:T(8,128)(2,1)}), bf16[8,6,96,192]{3,2,1,0:T(8,128)(2,1)S(1)}, u32[]{:S(2)}, u32[]{:S(2)}) async-start(bf16[8,6,96,192]{3,2,1,0:T(8,128)(2,1)} %weight_grads.1), calls=%async_computation.2 | async-start | bytes 4718592 | tf_op jit(solution)/shard_map/weight_grads/all_to_all | solution.py:699
  168.8 10.8 %collective-permute-start.29 = (bf16[80,128]{1,0:T(8,128)(2,1)}, bf16[80,128]{1,0:T(8,128)(2,1)S(1)}, u32[]{:S(2)}, u32[]{:S(2)}) collective-permute-start(bf16[80,128]{1,0:T(8,128)(2,1)} %get-tuple-element.185), channel_id=1, source_target_pairs={{0,8},{4,12},{8,0},{12,4},{16,24},{20,28},{24,16},{28,20},{1,9},{5... | collective-permute-start | bytes 61448 | tf_op jit(solution)/shard_map/table_outer/ppermute | solution.py:991
  170.9 9.5 %collective-permute-start.30 = (bf16[80,128]{1,0:T(8,128)(2,1)}, bf16[80,128]{1,0:T(8,128)(2,1)S(1)}, u32[]{:S(2)}, u32[]{:S(2)}) collective-permute-start(bf16[80,128]{1,0:T(8,128)(2,1)} %get-tuple-element.186), channel_id=1, source_target_pairs={{0,16},{4,20},{8,24},{12,28},{16,0},{20,4},{24,8},{28,12},{1,17},{... | collective-permute-start | bytes 61448 | tf_op jit(solution)/shard_map/table_outer/ppermute | solution.py:991
  188.5 11.9 %all-to-all-start.3 = ((f32[32,8,128]{2,1,0:T(8,128)}), f32[32,8,128]{2,1,0:T(8,128)S(1)}, u32[]{:S(2)}, u32[]{:S(2)}) async-start(f32[32,8,128]{2,1,0:T(8,128)} %get-tuple-element.193), calls=%async_computation.3 | async-start | bytes 262144 | tf_op jit(solution)/shard_map/squares/all_to_all | solution.py:699
  (55 other events, 381.4 us)

commit v5 on v4

--- a/solution.py
+++ b/solution.py
@@ -31,6 +31,7 @@
 BIG_QUARTERS = (1, 3)
 BIG_PARTS = len(BIG_QUARTERS)
 MESSAGE_ROWS = 8
+PRODUCTS = (STEPS - 1, STEPS)
 PIECES = 3
 PIECE_ROWS = 16
 FIXED = 8192.0
@@ -62,6 +63,9 @@
 
 
 def kernel_call(body, outs, name, micros, args, scratch=(), smem_in=(), placed=(), us_at=None, ready=(), limit=VMEM_BYTES, early=()):
+    groups = [arg if isinstance(arg, list) else [arg] for arg in args]
+    args = [struct((sum(a.shape[0] for a in g), *g[0].shape[1:]), g[0].dtype) if len(g) > 1 else g[0] for g in groups]
+    starts = [sum(len(g) for g in groups[:i]) for i in range(len(groups) + 1)]
     n_in, n_out = len(args), len(outs)
     moved = [i for i in range(n_in) if i not in smem_in and i not in ready]
     blocks = [out[0] if isinstance(out, tuple) else 0 for out in outs]
@@ -70,8 +74,9 @@
     n_sems = sum(args[i].shape[0] if i in placed else 1 for i in moved)
 
     def wrapped(*refs):
-        given, results = refs[:n_in], refs[n_in : n_in + len(flat)]
-        refs = refs[n_in + len(flat) :]
+        parts = [refs[starts[i] : starts[i + 1]] for i in range(n_in)]
+        given, results = [p[0] for p in parts], refs[starts[-1] : starts[-1] + len(flat)]
+        refs = refs[starts[-1] + len(flat) :]
         held = dict(zip(moved, refs))
         made, refs = refs[len(moved) : len(moved) + n_out], refs[len(moved) + n_out :]
         rest, (in_sems, out_sems) = refs[:-2], refs[-2:]
@@ -80,8 +85,10 @@
             pieces = [(given[i], held[i])]
             if i in placed:
                 size = args[i].shape[0]
+                each = size // len(parts[i])
                 pieces = [
-                    (given[i].at[k], held[i].at[given[us_at][1] ^ other]) for k, other in enumerate(xor_order(size))
+                    (parts[i][k // each].at[k % each], held[i].at[given[us_at][1] ^ other])
+                    for k, other in enumerate(xor_order(size))
                 ]
             arriving[i] = [pltpu.make_async_copy(a, b, in_sems.at[sem + n]) for n, (a, b) in enumerate(pieces)]
             sem += len(pieces)
@@ -120,7 +127,9 @@
     return pl.pallas_call(
         wrapped,
         out_shape=tuple(shapes[i] for i, _ in flat),
-        in_specs=[smem if i in smem_in else vmem if i in ready else anywhere for i in range(n_in)],
+        in_specs=[
+            smem if i in smem_in else vmem if i in ready else anywhere for i in range(n_in) for _ in groups[i]
+        ],
         out_specs=tuple([anywhere] * len(flat)),
         scratch_shapes=[pltpu.VMEM(args[i].shape, args[i].dtype) for i in moved]
         + [pltpu.VMEM((n, *o.shape) if n else o.shape, o.dtype) for n, o in zip(blocks, shapes)]
@@ -129,7 +138,7 @@
         name=name,
         compiler_params=pltpu.CompilerParams(vmem_limit_bytes=limit),
         cost_estimate=pl.CostEstimate(flops=int(micros * 1e9), bytes_accessed=1 << 20, transcendentals=0),
-    )(*args)
+    )(*[part for group in groups for part in group])
 
 
 def big_block(refs, block, half):
@@ -157,9 +166,21 @@
     lax.fori_loop(0, count // group, some, 0)
 
 
+def pick(items, high):
+    bit = 1
+    while len(items) > 1:
+        odd = (high & bit) != 0
+        items = [
+            jnp.where(odd, items[k + 1], items[k]) if k + 1 < len(items) else items[k]
+            for k in range(0, len(items), 2)
+        ]
+        bit *= 2
+    return items[0]
+
+
 def bias_body(part, need, done, table, *refs):
     small, refs = (refs[:3], refs[3:]) if part == 0 else (None, refs)
-    big, outs, words = refs[:3], refs[3:-1], refs[-1]
+    big, outs, (words, rows_of, found_rows) = refs[:3], refs[3:-3], refs[-3:]
     need(0)
     heads, count = words.shape[:2]
     for k in range(count):
@@ -169,12 +190,37 @@
         for h in range(heads):
             words[h, k] = jnp.broadcast_to(word[h : h + 1], (SUB, LANES))
 
+    for i, t in enumerate(PRODUCTS):
+        chunk = [table[SUB * c : SUB * (c + 1), :].astype(F32) for c in range(FIRST[t], FIRST[t] + CHUNKS[t])]
+        pairs_of = [jnp.concatenate(chunk[c : c + 2], axis=1) for c in range(0, CHUNKS[t], 2)]
+        rows_of[i] = jnp.concatenate(pairs_of, axis=0).astype(BF)
+    sub = lax.broadcasted_iota(jnp.int32, (2 * SUB, LANES), 0)
+    patterns = [(sub + 2 * SUB * k).astype(F32).astype(BF) for k in range(LANES // SUB)]
+    zero, one = jnp.zeros((2 * SUB, LANES), BF), jnp.ones((2 * SUB, LANES), BF)
+
+    def product(i, code):
+        spread = [jnp.broadcast_to(code[s : s + 1], (SUB, LANES)) for s in range(SUB)]
+        hot = []
+        for s in range(SUB):
+            low = (spread[s] & (2 * LANES - 1)).astype(F32)
+            low = jnp.concatenate([low, low], axis=0).astype(BF)
+            hot.append(jnp.concatenate([jnp.where(low == p, one, zero) for p in patterns], axis=0))
+        values = dot(rows_of[i], jnp.concatenate(hot, axis=1), NN)
+        for s in range(SUB):
+            lanes = slice(LANES * s, LANES * (s + 1))
+            items = [values[heads * c : heads * (c + 1), lanes] for c in range(values.shape[0] // heads)]
+            found_rows[i, pl.ds(s, heads, stride=SUB), :] = pick(items, spread[s] >> 8)
+
     def step(store):
         def run(parts):
             for index, lengths, block, side in parts:
-                share = (1.0 / FIXED) / lengths.astype(F32)
+                share = 1.0 / lengths.astype(F32)
                 first, edges = [None] * heads, [None] * heads
+                for i, t in enumerate(PRODUCTS):
+                    product(i, index[t])
                 for t in range(LOOKUPS):
+                    if t in PRODUCTS:
+                        continue
                     code = index[t]
                     lane = code & (LANES - 1)
                     odd = [(code & bit) != 0 for bit in (256, 512, 1024)]
@@ -199,8 +245,10 @@
                             value = jnp.where(live, value, 0)
                             edges[h] = value if edges[h] is None else edges[h] + value
                 for h in range(heads):
-                    value = first[h].astype(F32) * (1.0 / FIXED) + edges[h].astype(F32) * share
-                    store(h, side, block, value)
+                    edge = edges[h].astype(F32) * (1.0 / FIXED)
+                    for i, t in enumerate(PRODUCTS):
+                        edge = edge + jnp.where(lengths > t - 1, found_rows[i, SUB * h : SUB * (h + 1), :], 0.0)
+                    store(h, side, block, first[h].astype(F32) * (1.0 / FIXED) + edge * share)
 
         return run
 
@@ -817,7 +865,11 @@
             "pair_bias",
             12 if part == 0 else 20,
             (table, *ints),
-            [pltpu.VMEM((heads, all_chunks // 2, SUB, LANES), jnp.int32)],
+            [
+                pltpu.VMEM((heads, all_chunks // 2, SUB, LANES), jnp.int32),
+                pltpu.VMEM((len(PRODUCTS), max(CHUNKS) // 2 * heads, 2 * LANES), BF),
+                pltpu.VMEM((len(PRODUCTS), heads * SUB, LANES), F32),
+            ],
         )
 
     small_bias, *big_bias = pair_bias(0, table_all, (*small_ints, *big_ints))
@@ -843,10 +895,10 @@
     with jax.named_scope("rest_near_head"):
         for r in near_heads:
             weights_held[r] = to_head(weights_held[0], r)
-    weights_attend = jnp.concatenate(qkv_near)
+    weights_attend = list(qkv_near)
     vector_row, vector_pieces = 3 * shard_rows, ()
     if not stacked:
-        weights_attend = weights_attend[order]
+        weights_attend = jnp.concatenate(qkv_near)[order]
         vector_row, vector_pieces = 0, (weights_attend[:, 3 * shard_rows :],)
         weights_attend = weights_attend[:, : 3 * shard_rows].reshape(n_dp, 3, shard_rows, columns)
         weights_attend = weights_attend.transpose(1, 0, 2, 3).reshape(3, model, columns)
@@ -954,7 +1006,7 @@
         weight_grads = weight_grads.reshape(6, n_dp, shard_rows, columns).transpose(1, 0, 2, 3)
     with jax.named_scope("grad_normed_one"):
         rows_back = swap(rows_sent, n_head)
-    weight_grads, *rows_back = lax.optimization_barrier((weight_grads, *rows_back))
+    _, *rows_back = lax.optimization_barrier((weight_grads, *rows_back))
     with jax.named_scope("weight_grads"):
         weights_arrived = exchange(weight_grads, "dp")
     input_grad, vector_rows = kernel_call(

time: 205 us -> 198 us (0.966)
  starting transfers between devices: 56.2 us -> 50.1 us
  waiting for transfers between devices: 22.1 us -> 26.8 us
  Pallas kernels: 106 us -> 102 us
    ppermute x3, starting transfers between devices: 10.1 us -> 6.04 us  [on_device(): lax.ppermute(outer_sent[k], 'dp', dp_pairs(k * inner))]
    pallas_call x11, Pallas kernels: 106 us -> 102 us  [kernel_call(): pl.pallas_call(wrapped, out_shape=tuple((shapes[i] for i, _ in flat)), in...]
    ppermute x1, waiting for transfers between devices: 2.63 us -> 6.01 us  [on_device(): lax.ppermute(inner_sent[k], 'dp', dp_pairs(k))]
    unnamed x89 -> x91, local copies, waits for them, and re-layouts: 9.7 us -> 9.57 us
  transfers between devices with their start and end apart: 36 -> 36, of which waited for: 10 -> 11; matrix products, arithmetic and copies ran while one was open for 4% -> 3% of each run, Pallas kernels for 45% -> 45%
where the time goes in v5:
time: 198 us; the launch traced here: 197 us
  Pallas kernels  102 us (52%)
  starting transfers between devices  50.1 us (25%)
  waiting for transfers between devices  26.8 us (14%)
  local copies, waits for them, and re-layouts  13.4 us (7%)
  between operations  2.27 us (1%)
  other arithmetic  2.09 us (1%)
    pallas_call x11, Pallas kernels, kernel_call(): pl.pallas_call(wrapped, out_shape=tuple((shapes[i] for i, _ in flat)), in...  102 us
    all_to_all x4, starting transfers between devices, exchange(): return lax.all_to_all(value, axis, split_axis=0, concat_axis=0, tiled=True)  17.5 us
    ppermute x6, starting transfers between devices, far_shards(): lax.ppermute(value, 'dp', dp_pairs(k))  10.1 us
    unnamed x91, local copies, waits for them, and re-layouts  9.57 us
    all_to_all x4, waiting for transfers between devices, exchange(): return lax.all_to_all(value, axis, split_axis=0, concat_axis=0, tiled=True)  8.14 us
    ppermute x9, starting transfers between devices, swap(): lax.ppermute(values[r], 'head', [(i, i ^ r) for i in range(n_head)])  6.22 us
    ppermute x3, starting transfers between devices, on_device(): lax.ppermute(outer_sent[k], 'dp', dp_pairs(k * inner))  6.04 us
    ppermute x1, waiting for transfers between devices, on_device(): lax.ppermute(inner_sent[k], 'dp', dp_pairs(k))  6.01 us
  transfers between devices with their start and end apart: 36, of which 11 were waited for; matrix products, arithmetic and copies ran while one was open for 3% of the time, Pallas kernels for 45%

profile of v5, /device:TPU:0, one launch (start us, length us, event | category | flops | bytes accessed | tf_op | source)
XLA Modules:
  0.0 197.0 jit_solution(13167680457028250935)
XLA Ops:
  3.8 5.1 %collective-permute-start.5 = (bf16[3,96,192]{2,1,0:T(8,128)(2,1)S(1)}, bf16[3,96,192]{2,1,0:T(8,128)(2,1)S(1)}, u32[]{:S(2)}, u32[]{:S(2)}) collective-permute-start(bf16[3,96,192]{2,1,0:T(8,128)(2,1)S(1)} %pad_maximum_fusion.3), channel_id=1, source_target_pairs={{0,24},{4,28},{8,16},{12,20},{16,8},{20,12},{24,0},{28,4},{1,25},{... | collective-permute-start | bytes 331784 | tf_op jit(solution)/shard_map/rest_far/ppermute | solution.py:816
  12.1 5.8 %all-to-all-start = ((bf16[8,8,8,128]{3,2,1,0:T(8,128)(2,1)}), bf16[8,8,8,128]{3,2,1,0:T(8,128)(2,1)S(1)}, u32[]{:S(2)}, u32[]{:S(2)}) async-start(bf16[8,8,8,128]{3,2,1,0:T(8,128)(2,1)} %broadcast_in_dim.4), calls=%async_computation | async-start | bytes 262144 | tf_op jit(solution)/shard_map/table_all/all_to_all | solution.py:747
  20.3 2.6 %collective-permute-done.4 = bf16[3,96,192]{2,1,0:T(8,128)(2,1)S(1)} collective-permute-done((bf16[3,96,192]{2,1,0:T(8,128)(2,1)S(1)}, bf16[3,96,192]{2,1,0:T(8,128)(2,1)S(1)}, u32[]{:S(2)}, u32[]{:S(2)}) %collective-permute-start.4) | collective-permute-done | bytes 110624 | tf_op jit(solution)/shard_map/rest_far/ppermute | solution.py:816
  22.8 3.2 %collective-permute-start.9 = (bf16[336,192]{1,0:T(8,128)(2,1)S(1)}, bf16[336,192]{1,0:T(8,128)(2,1)S(1)}, u32[]{:S(2)}, u32[]{:S(2)}) collective-permute-start(bf16[336,192]{1,0:T(8,128)(2,1)S(1)} %fusion.6), channel_id=1, source_target_pairs={{0,24},{4,28},{8,16},{12,20},{16,8},{20,12},{24,0},{28,4},{1,25},{... | collective-permute-start | bytes 387080 | tf_op jit(solution)/shard_map/qkv_far/ppermute | solution.py:816
  29.6 11.6 %pair_bias.2 = (f32[8,2,64,128]{3,2,1,0:T(8,128)}, f32[8,2,64,128]{3,2,1,0:T(8,128)}) custom-call(bf16[512,128]{1,0:T(8,128)(2,1)} %bitcast.62, s32[4,64,64]{2,1,0:T(8,128)} %refs_1_.5, s32[5,4,64,64]{3,2,1,0:T(8,128)} %refs_2_.5, s32[4,64,64]{2,1,0:T(8,128)} %refs_3_.5, s32[1,256,256]{2,1,0:T(8,128)} %refs_5_.8, s32[5,1,256,256]{3,2,1,0:T(8,128)} %refs_6_.8, ...), custom_call_target="tpu_custom_call" | custom-call | flops 12000000000 | bytes 1048576 | tf_op jit(solution)/shard_map/pair_bias/pallas_call | solution.py:127
  45.2 16.2 %pair_bias.3.refs_11_ = f32[8,2,192,128]{3,2,1,0:T(8,128)} custom-call(bf16[512,128]{1,0:T(8,128)(2,1)} %bitcast.63, s32[1,256,256]{2,1,0:T(8,128)} %refs_5_.8, s32[5,1,256,256]{3,2,1,0:T(8,128)} %refs_6_.8, s32[1,256,256]{2,1,0:T(8,128)} %refs_7_.2), custom_call_target="tpu_custom_call" | custom-call | flops 20000000000 | bytes 1048576 | tf_op jit(solution)/shard_map/pair_bias/pallas_call | solution.py:127
  62.6 7.7 %attend_forward.1 = (bf16[512,768]{1,0:T(8,128)(2,1)}, bf16[3,512,192]{2,1,0:T(8,128)(2,1)}, f32[8,256,256]{2,1,0:T(8,128)}, f32[8,2,128,128]{3,2,1,0:T(8,128)},...) custom-call(bf16[2,128,768]{2,1,0:T(8,128)(2,1)} %copy-done.21, ...), custom_call_target="tpu_custom_call" | custom-call | flops 12000000000 | bytes 1048576 | tf_op jit(solution)/shard_map/attend_forward/pallas_call | solution.py:127
  78.5 7.5 %feed_forward.1 = (bf16[128,768]{1,0:T(8,128)(2,1)}, f32[128,768]{1,0:T(8,128)}, f32[4,768]{1,0:T(4,128)}, f32[4,192]{1,0:T(4,128)}, bf16[2,128,768]{2,1,0:T(8,1...) custom-call(bf16[128,192]{1,0:T(8,128)(2,1)} %get-tuple-element.140., ...), custom_call_target="tpu_custom_call" | custom-call | flops 6000000000 | bytes 1048576 | tf_op jit(solution)/shard_map/feed_forward/pallas_call | solution.py:127
  88.9 3.6 %all-to-all-start.1 = ((bf16[4,128,512]{2,1,0:T(8,128)(2,1)}), bf16[4,128,512]{2,1,0:T(8,128)(2,1)S(1)}, u32[]{:S(2)}, u32[]{:S(2)}) async-start(bf16[4,128,512]{2,1,0:T(8,128)(2,1)} %get-tuple-element.150), calls=%async_computation.1 | async-start | bytes 1048576 | tf_op jit(solution)/shard_map/act_pre/all_to_all | solution.py:747
  93.2 9.2 %attend_backward.1 = (f32[1024,128]{1,0:T(8,128)}, f32[4096,128]{1,0:T(8,128)}, bf16[3,512,192]{2,1,0:T(8,128)(2,1)}, f32[2,4,192]{2,1,0:T(4,128)}, bf16[128,768...) custom-call(bf16[128,192]{1,0:T(8,128)(2,1)} %get-tuple-element.152.refs_0_, ...), custom_call_target="tpu_custom_call" | custom-call | flops 14000000000 | bytes 1048576 | tf_op jit(solution)/shard_map/attend_backward/pallas_call | solution.py:127
  103.1 1.9 collective-permute-start.26
  107.2 5.7 %weight_grads.1 = bf16[8,6,96,192]{3,2,1,0:T(8,128)(2,1)} custom-call(bf16[2,128,768]{2,1,0:T(8,128)(2,1)} %copy-done.21, bf16[2,128,768]{2,1,0:T(8,128)(2,1)} %collective-permute-done.11.refs_1_, bf16[2,128,768]{2,1,0:T(8,128)(2,1)} %collective-permute-done.refs_2_, bf16[2,128,768]{2,1,0:T(8,128)(2,1)} %collective-permute-done.12.refs_3_, ...), custom_call_target="tpu_custom_call" | custom-call | flops 6000000000 | bytes 1048576 | tf_op jit(solution)/shard_map/weight_grads/pallas_call | solution.py:127
  113.0 4.4 %all-to-all-start.2 = ((bf16[8,6,96,192]{3,2,1,0:T(8,128)(2,1)}), bf16[8,6,96,192]{3,2,1,0:T(8,128)(2,1)S(1)}, u32[]{:S(2)}, u32[]{:S(2)}) async-start(bf16[8,6,96,192]{3,2,1,0:T(8,128)(2,1)} %weight_grads.1), calls=%async_computation.2 | async-start | bytes 4718592 | tf_op jit(solution)/shard_map/weight_grads/all_to_all | solution.py:747
  118.1 3.3 %input_grad.1 = (bf16[128,768]{1,0:T(8,128)(2,1)}, bf16[2,4,16,128]{3,2,1,0:T(8,128)(2,1)}) custom-call(bf16[128,768]{1,0:T(8,128)(2,1)} %get-tuple-element.168.refs_0_, bf16[128,768]{1,0:T(8,128)(2,1)} %copy-done.32, bf16[128,768]{1,0:T(8,128)(2,1)} %copy-done.33, bf16[128,768]{1,0:T(8,128)(2,1)} %collective-permute-done.27.refs_3_, ...), custom_call_target="tpu_custom_call" | custom-call | flops 3000000000 | bytes 1048576 | tf_op jit(solution)/shard_map/input_grad/pallas_call | solution.py:127
  121.4 33.6 %table_scatter.1 = (bf16[4,80,128]{2,1,0:T(8,128)(2,1)}, bf16[4,80,128]{2,1,0:T(8,128)(2,1)}) custom-call(f32[1024,128]{1,0:T(8,128)} %get-tuple-element.177.refs_0_, s32[4,64,64]{2,1,0:T(8,128)} %refs_1_.5, s32[5,4,64,64]{3,2,1,0:T(8,128)} %refs_2_.5, s32[4,64,64]{2,1,0:T(8,128)} %refs_3_.5, f32[4096,128]{1,0:T(8,128)} %get-tuple-element.178.refs_4_, ...), custom_call_target="tpu_custom_call" | custom-call | flops 40000000000 | bytes 1048576 | tf_op jit(solution)/shard_map/table_scatter/pallas_call | solution.py:127
  155.0 2.1 %collective-permute-start.28 = (bf16[4,80,128]{2,1,0:T(8,128)(2,1)}, bf16[4,80,128]{2,1,0:T(8,128)(2,1)S(1)}, u32[]{:S(2)}, u32[]{:S(2)}) collective-permute-start(bf16[4,80,128]{2,1,0:T(8,128)(2,1)} %get-tuple-element.181), channel_id=1, source_target_pairs={{0,4},{4,0},{8,12},{12,8},{16,20},{20,16},{24,28},{28,24},{1,5},{5... | collective-permute-start | bytes 245768 | tf_op jit(solution)/shard_map/table_inner/ppermute | solution.py:1033
  157.1 6.0 %collective-permute-done.28.refs_1_ = bf16[4,80,128]{2,1,0:T(8,128)(2,1)S(1)} collective-permute-done((bf16[4,80,128]{2,1,0:T(8,128)(2,1)}, bf16[4,80,128]{2,1,0:T(8,128)(2,1)S(1)}, u32[]{:S(2)}, u32[]{:S(2)}) %collective-permute-start.28) | collective-permute-done | bytes 81952 | tf_op jit(solution)/shard_map/table_inner/ppermute | solution.py:1033
  165.4 3.6 %collective-permute-start.29 = (bf16[80,128]{1,0:T(8,128)(2,1)}, bf16[80,128]{1,0:T(8,128)(2,1)S(1)}, u32[]{:S(2)}, u32[]{:S(2)}) collective-permute-start(bf16[80,128]{1,0:T(8,128)(2,1)} %get-tuple-element.183), channel_id=1, source_target_pairs={{0,8},{4,12},{8,0},{12,4},{16,24},{20,28},{24,16},{28,20},{1,9},{5... | collective-permute-start | bytes 61448 | tf_op jit(solution)/shard_map/table_outer/ppermute | solution.py:1043
  171.6 2.3 %collective-permute-done.30.refs_3_ = bf16[80,128]{1,0:T(8,128)(2,1)S(1)} collective-permute-done((bf16[80,128]{1,0:T(8,128)(2,1)}, bf16[80,128]{1,0:T(8,128)(2,1)S(1)}, u32[]{:S(2)}, u32[]{:S(2)}) %collective-permute-start.30) | collective-permute-done | bytes 20512 | tf_op jit(solution)/shard_map/table_outer/ppermute | solution.py:1043
  173.9 2.7 %collective-permute-done.31.refs_4_ = bf16[80,128]{1,0:T(8,128)(2,1)S(1)} collective-permute-done((bf16[80,128]{1,0:T(8,128)(2,1)}, bf16[80,128]{1,0:T(8,128)(2,1)S(1)}, u32[]{:S(2)}, u32[]{:S(2)}) %collective-permute-start.31) | collective-permute-done | bytes 20512 | tf_op jit(solution)/shard_map/table_outer/ppermute | solution.py:1043
  178.0 3.0 %shard_sums.1 = (f32[6,96,192]{2,1,0:T(8,128)}, f32[64,128]{1,0:T(8,128)}, f32[32,8,128]{2,1,0:T(8,128)}) custom-call(bf16[8,6,96,192]{3,2,1,0:T(8,128)(2,1)} %copy-done.19, bf16[80,128]{1,0:T(8,128)(2,1)} %get-tuple-element.187.refs_1_, bf16[80,128]{1,0:T(8,128)(2,1)} %copy-done.41, bf16[80,128]{1,0:T(8,128)(2,1)} %copy-done.42, bf16[80,128]{1,0:T(8,128)(2,1)} %copy-done.43), custom_call_target="tpu_custom_call" | custom-call | flops 4000000000 | bytes 1048576 | tf_op jit(solution)/shard_map/shard_sums/pallas_call | solution.py:127
  181.2 3.6 %all-to-all-start.3 = ((f32[32,8,128]{2,1,0:T(8,128)}), f32[32,8,128]{2,1,0:T(8,128)S(1)}, u32[]{:S(2)}, u32[]{:S(2)}) async-start(f32[32,8,128]{2,1,0:T(8,128)} %get-tuple-element.191), calls=%async_computation.3 | async-start | bytes 262144 | tf_op jit(solution)/shard_map/squares/all_to_all | solution.py:747
  186.2 6.9 %all-to-all-done.3.refs_1_ = f32[32,8,128]{2,1,0:T(8,128)S(1)} async-done(((f32[32,8,128]{2,1,0:T(8,128)}), f32[32,8,128]{2,1,0:T(8,128)S(1)}, u32[]{:S(2)}, u32[]{:S(2)}) %all-to-all-start.3) | async-done | bytes 131104 | tf_op jit(solution)/shard_map/squares/all_to_all | solution.py:747
  194.0 2.8 %update.1 = (f32[4,96,192]{2,1,0:T(8,128)}, f32[4,96,192]{2,1,0:T(8,128)}, f32[4,96,192]{2,1,0:T(8,128)}, f32[192,96]{1,0:T(8,128)}, f32[192,96]{1,0:T(8,128)}, ...) custom-call(s32[2]{0:T(128)S(1)} %copy-done.16, ...), custom_call_target="tpu_custom_call" | custom-call | flops 3000000000 | bytes 1048576 | tf_op jit(solution)/shard_map/update/pallas_call | solution.py:127
  (171 shorter events, 40.1 us)
Async XLA Ops:
  3.8 16.5 %collective-permute-start.5 = (bf16[3,96,192]{2,1,0:T(8,128)(2,1)S(1)}, bf16[3,96,192]{2,1,0:T(8,128)(2,1)S(1)}, u32[]{:S(2)}, u32[]{:S(2)}) collective-permute-start(bf16[3,96,192]{2,1,0:T(8,128)(2,1)S(1)} %pad_maximum_fusion.3), channel_id=1, source_target_pairs={{0,24},{4,28},{8,16},{12,20},{16,8},{20,12},{24,0},{28,4},{1,25},{... | collective-permute-start | bytes 331784 | tf_op jit(solution)/shard_map/rest_far/ppermute | solution.py:816
  8.9 13.9 %collective-permute-start.4 = (bf16[3,96,192]{2,1,0:T(8,128)(2,1)S(1)}, bf16[3,96,192]{2,1,0:T(8,128)(2,1)S(1)}, u32[]{:S(2)}, u32[]{:S(2)}) collective-permute-start(bf16[3,96,192]{2,1,0:T(8,128)(2,1)S(1)} %pad_maximum_fusion.3), channel_id=1, source_target_pairs={{0,16},{4,20},{8,24},{12,28},{16,0},{20,4},{24,8},{28,12},{1,17},{... | collective-permute-start | bytes 331784 | tf_op jit(solution)/shard_map/rest_far/ppermute | solution.py:816
  8.9 13.9 %collective-permute-start.3 = (bf16[3,96,192]{2,1,0:T(8,128)(2,1)S(1)}, bf16[3,96,192]{2,1,0:T(8,128)(2,1)S(1)}, u32[]{:S(2)}, u32[]{:S(2)}) collective-permute-start(bf16[3,96,192]{2,1,0:T(8,128)(2,1)S(1)} %pad_maximum_fusion.3), channel_id=1, source_target_pairs={{0,8},{4,12},{8,0},{12,4},{16,24},{20,28},{24,16},{28,20},{1,9},{5... | collective-permute-start | bytes 331784 | tf_op jit(solution)/shard_map/rest_far/ppermute | solution.py:816
  9.7 8.9 %collective-permute-start.1 = (f32[9,96]{1,0:T(8,128)S(1)}, f32[9,96]{1,0:T(8,128)S(1)}, u32[]{:S(2)}, u32[]{:S(2)}) collective-permute-start(f32[9,96]{1,0:T(8,128)S(1)} %dynamic_update_slice.5), channel_id=1, source_target_pairs={{0,2},{1,3},{2,0},{3,1},{4,6},{5,7},{6,4},{7,5},{8,10},{9,11},{10,... | collective-permute-start | bytes 10376 | tf_op jit(solution)/shard_map/vectors_head/ppermute | solution.py:823
  12.1 16.8 %all-to-all-start = ((bf16[8,8,8,128]{3,2,1,0:T(8,128)(2,1)}), bf16[8,8,8,128]{3,2,1,0:T(8,128)(2,1)S(1)}, u32[]{:S(2)}, u32[]{:S(2)}) async-start(bf16[8,8,8,128]{3,2,1,0:T(8,128)(2,1)} %broadcast_in_dim.4), calls=%async_computation | async-start | bytes 262144 | tf_op jit(solution)/shard_map/table_all/all_to_all | solution.py:747
  18.0 23.3 %collective-permute-start = (bf16[2,128,768]{2,1,0:T(8,128)(2,1)S(1)}, bf16[2,128,768]{2,1,0:T(8,128)(2,1)}, u32[]{:S(2)}, u32[]{:S(2)}) collective-permute-start(bf16[2,128,768]{2,1,0:T(8,128)(2,1)S(1)} %pad_maximum_fusion.2.refs_0_), channel_id=1, source_target_pairs={{0,2},{1,3},{2,0},{3,1},{4,6},{5,7},{6,4},{7,5},{8,10},{9,11},{10,... | collective-permute-start | bytes 1179656 | tf_op jit(solution)/shard_map/rows_far/ppermute | solution.py:823
  22.8 18.4 %collective-permute-start.9 = (bf16[336,192]{1,0:T(8,128)(2,1)S(1)}, bf16[336,192]{1,0:T(8,128)(2,1)S(1)}, u32[]{:S(2)}, u32[]{:S(2)}) collective-permute-start(bf16[336,192]{1,0:T(8,128)(2,1)S(1)} %fusion.6), channel_id=1, source_target_pairs={{0,24},{4,28},{8,16},{12,20},{16,8},{20,12},{24,0},{28,4},{1,25},{... | collective-permute-start | bytes 387080 | tf_op jit(solution)/shard_map/qkv_far/ppermute | solution.py:816
  26.0 15.3 %collective-permute-start.8 = (bf16[336,192]{1,0:T(8,128)(2,1)S(1)}, bf16[336,192]{1,0:T(8,128)(2,1)S(1)}, u32[]{:S(2)}, u32[]{:S(2)}) collective-permute-start(bf16[336,192]{1,0:T(8,128)(2,1)S(1)} %fusion.6), channel_id=1, source_target_pairs={{0,16},{4,20},{8,24},{12,28},{16,0},{20,4},{24,8},{28,12},{1,17},{... | collective-permute-start | bytes 387080 | tf_op jit(solution)/shard_map/qkv_far/ppermute | solution.py:816
  26.0 15.3 %collective-permute-start.7 = (bf16[336,192]{1,0:T(8,128)(2,1)S(1)}, bf16[336,192]{1,0:T(8,128)(2,1)S(1)}, u32[]{:S(2)}, u32[]{:S(2)}) collective-permute-start(bf16[336,192]{1,0:T(8,128)(2,1)S(1)} %fusion.6), channel_id=1, source_target_pairs={{0,8},{4,12},{8,0},{12,4},{16,24},{20,28},{24,16},{28,20},{1,9},{5... | collective-permute-start | bytes 387080 | tf_op jit(solution)/shard_map/qkv_far/ppermute | solution.py:816
  27.4 14.0 %collective-permute-start.6 = (bf16[4,3,96,192]{3,2,1,0:T(8,128)(2,1)S(1)}, bf16[4,3,96,192]{3,2,1,0:T(8,128)(2,1)S(1)}, u32[]{:S(2)}, u32[]{:S(2)}) collective-permute-start(bf16[4,3,96,192]{3,2,1,0:T(8,128)(2,1)S(1)} %pad_maximum_fusion.1), channel_id=1, source_target_pairs={{0,4},{4,0},{8,12},{12,8},{16,20},{20,16},{24,28},{28,24},{1,5},{5... | collective-permute-start | bytes 1327112 | tf_op jit(solution)/shard_map/rest_near/ppermute | solution.py:820
  41.2 20.2 %collective-permute-start.11 = (bf16[2,128,768]{2,1,0:T(8,128)(2,1)S(1)}, bf16[2,128,768]{2,1,0:T(8,128)(2,1)}, u32[]{:S(2)}, u32[]{:S(2)}) collective-permute-start(bf16[2,128,768]{2,1,0:T(8,128)(2,1)S(1)} %pad_maximum_fusion.2.refs_0_), channel_id=1, source_target_pairs={{0,1},{1,0},{2,3},{3,2},{4,5},{5,4},{6,7},{7,6},{8,9},{9,8},{10,11... | collective-permute-start | bytes 1179656 | tf_op jit(solution)/shard_map/rows_near/ppermute | solution.py:823
  42.1 28.6 %collective-permute-start.14 = (bf16[8,3,96,192]{3,2,1,0:T(8,128)(2,1)S(1)}, bf16[8,3,96,192]{3,2,1,0:T(8,128)(2,1)}, u32[]{:S(2)}, u32[]{:S(2)}) collective-permute-start(bf16[8,3,96,192]{3,2,1,0:T(8,128)(2,1)S(1)} %constant_dynamic-update-slice_fusion.refs_9_), channel_id=1, source_target_pairs={{0,2},{1,3},{2,0},{3,1},{4,6},{5,7},{6,4},{7,5},{8,10},{9,11},{10,... | collective-permute-start | bytes 2654216 | tf_op jit(solution)/shard_map/rest_far_head/ppermute | solution.py:823
  44.0 26.7 %collective-permute-start.13 = (bf16[8,3,96,192]{3,2,1,0:T(8,128)(2,1)S(1)}, bf16[8,3,96,192]{3,2,1,0:T(8,128)(2,1)}, u32[]{:S(2)}, u32[]{:S(2)}) collective-permute-start(bf16[8,3,96,192]{3,2,1,0:T(8,128)(2,1)S(1)} %constant_dynamic-update-slice_fusion.refs_9_), channel_id=1, source_target_pairs={{0,1},{1,0},{2,3},{3,2},{4,5},{5,4},{6,7},{7,6},{8,9},{9,8},{10,11... | collective-permute-start | bytes 2654216 | tf_op jit(solution)/shard_map/rest_near_head/ppermute | solution.py:823
  44.2 17.3 %collective-permute-start.12 = (bf16[2,128,768]{2,1,0:T(8,128)(2,1)}, bf16[2,128,768]{2,1,0:T(8,128)(2,1)}, u32[]{:S(2)}, u32[]{:S(2)}) collective-permute-start(bf16[2,128,768]{2,1,0:T(8,128)(2,1)} %collective-permute-done.refs_2_), channel_id=1, source_target_pairs={{0,1},{1,0},{2,3},{3,2},{4,5},{5,4},{6,7},{7,6},{8,9},{9,8},{10,11... | collective-permute-start | bytes 1179656 | tf_op jit(solution)/shard_map/rows_near/ppermute | solution.py:823
  45.0 16.5 %collective-permute-start.10 = (bf16[4,336,192]{1,2,0:T(8,128)(2,1)S(1)}, bf16[4,336,192]{1,2,0:T(8,128)(2,1)S(1)}, u32[]{:S(2)}, u32[]{:S(2)}) collective-permute-start(bf16[4,336,192]{1,2,0:T(8,128)(2,1)S(1)} %copy.49), channel_id=1, source_target_pairs={{0,4},{4,0},{8,12},{12,8},{16,20},{20,16},{24,28},{28,24},{1,5},{5... | collective-permute-start | bytes 1548296 | tf_op jit(solution)/shard_map/qkv_near/ppermute | solution.py:820
  88.0 14.5 %collective-permute-start.23 = (bf16[2,128,768]{2,1,0:T(8,128)(2,1)}, bf16[2,128,768]{2,1,0:T(8,128)(2,1)S(1)}, u32[]{:S(2)}, u32[]{:S(2)}) collective-permute-start(bf16[2,128,768]{2,1,0:T(8,128)(2,1)} %get-tuple-element.160.refs_12_), channel_id=1, source_target_pairs={{0,2},{1,3},{2,0},{3,1},{4,6},{5,7},{6,4},{7,5},{8,10},{9,11},{10,... | collective-permute-start | bytes 1179656 | tf_op jit(solution)/shard_map/normed_grad/ppermute | solution.py:966
  88.5 14.0 %collective-permute-start.22 = (bf16[2,128,768]{2,1,0:T(8,128)(2,1)}, bf16[2,128,768]{2,1,0:T(8,128)(2,1)S(1)}, u32[]{:S(2)}, u32[]{:S(2)}) collective-permute-start(bf16[2,128,768]{2,1,0:T(8,128)(2,1)} %get-tuple-element.160.refs_12_), channel_id=1, source_target_pairs={{0,1},{1,0},{2,3},{3,2},{4,5},{5,4},{6,7},{7,6},{8,9},{9,8},{10,11... | collective-permute-start | bytes 1179656 | tf_op jit(solution)/shard_map/normed_grad/ppermute | solution.py:966
  88.9 17.4 %all-to-all-start.1 = ((bf16[4,128,512]{2,1,0:T(8,128)(2,1)}), bf16[4,128,512]{2,1,0:T(8,128)(2,1)S(1)}, u32[]{:S(2)}, u32[]{:S(2)}) async-start(bf16[4,128,512]{2,1,0:T(8,128)(2,1)} %get-tuple-element.150), calls=%async_computation.1 | async-start | bytes 1048576 | tf_op jit(solution)/shard_map/act_pre/all_to_all | solution.py:747
  103.0 14.4 %collective-permute-start.25 = (bf16[128,768]{1,0:T(8,128)(2,1)}, bf16[128,768]{1,0:T(8,128)(2,1)S(1)}, u32[]{:S(2)}, u32[]{:S(2)}) collective-permute-start(bf16[128,768]{1,0:T(8,128)(2,1)} %get-tuple-element.165), channel_id=1, source_target_pairs={{0,1},{1,0},{2,3},{3,2},{4,5},{5,4},{6,7},{7,6},{8,9},{9,8},{10,11... | collective-permute-start | bytes 589832 | tf_op jit(solution)/shard_map/grad_normed_one/ppermute | solution.py:757
  103.1 14.3 %collective-permute-start.26 = (bf16[128,768]{1,0:T(8,128)(2,1)}, bf16[128,768]{1,0:T(8,128)(2,1)S(1)}, u32[]{:S(2)}, u32[]{:S(2)}) collective-permute-start(bf16[128,768]{1,0:T(8,128)(2,1)} %get-tuple-element.166), channel_id=1, source_target_pairs={{0,2},{1,3},{2,0},{3,1},{4,6},{5,7},{6,4},{7,5},{8,10},{9,11},{10,... | collective-permute-start | bytes 589832 | tf_op jit(solution)/shard_map/grad_normed_one/ppermute | solution.py:757
  105.0 12.4 %collective-permute-start.27 = (bf16[128,768]{1,0:T(8,128)(2,1)}, bf16[128,768]{1,0:T(8,128)(2,1)}, u32[]{:S(2)}, u32[]{:S(2)}) collective-permute-start(bf16[128,768]{1,0:T(8,128)(2,1)} %get-tuple-element.167), channel_id=1, source_target_pairs={{0,3},{1,2},{2,1},{3,0},{4,7},{5,6},{6,5},{7,4},{8,11},{9,10},{10,... | collective-permute-start | bytes 589832 | tf_op jit(solution)/shard_map/grad_normed_one/ppermute | solution.py:757
  113.0 63.6 %all-to-all-start.2 = ((bf16[8,6,96,192]{3,2,1,0:T(8,128)(2,1)}), bf16[8,6,96,192]{3,2,1,0:T(8,128)(2,1)S(1)}, u32[]{:S(2)}, u32[]{:S(2)}) async-start(bf16[8,6,96,192]{3,2,1,0:T(8,128)(2,1)} %weight_grads.1), calls=%async_computation.2 | async-start | bytes 4718592 | tf_op jit(solution)/shard_map/weight_grads/all_to_all | solution.py:747
  155.0 8.1 %collective-permute-start.28 = (bf16[4,80,128]{2,1,0:T(8,128)(2,1)}, bf16[4,80,128]{2,1,0:T(8,128)(2,1)S(1)}, u32[]{:S(2)}, u32[]{:S(2)}) collective-permute-start(bf16[4,80,128]{2,1,0:T(8,128)(2,1)} %get-tuple-element.181), channel_id=1, source_target_pairs={{0,4},{4,0},{8,12},{12,8},{16,20},{20,16},{24,28},{28,24},{1,5},{5... | collective-permute-start | bytes 245768 | tf_op jit(solution)/shard_map/table_inner/ppermute | solution.py:1033
  181.2 11.9 %all-to-all-start.3 = ((f32[32,8,128]{2,1,0:T(8,128)}), f32[32,8,128]{2,1,0:T(8,128)S(1)}, u32[]{:S(2)}, u32[]{:S(2)}) async-start(f32[32,8,128]{2,1,0:T(8,128)} %get-tuple-element.191), calls=%async_computation.3 | async-start | bytes 262144 | tf_op jit(solution)/shard_map/squares/all_to_all | solution.py:747
  (56 other events, 383.9 us)

commit v6 on v5

--- a/solution.py
+++ b/solution.py
@@ -191,25 +191,23 @@
             words[h, k] = jnp.broadcast_to(word[h : h + 1], (SUB, LANES))
 
     for i, t in enumerate(PRODUCTS):
-        chunk = [table[SUB * c : SUB * (c + 1), :].astype(F32) for c in range(FIRST[t], FIRST[t] + CHUNKS[t])]
-        pairs_of = [jnp.concatenate(chunk[c : c + 2], axis=1) for c in range(0, CHUNKS[t], 2)]
-        rows_of[i] = jnp.concatenate(pairs_of, axis=0).astype(BF)
+        rows_of[i] = table[SUB * FIRST[t] : SUB * (FIRST[t] + CHUNKS[t]), :]
     sub = lax.broadcasted_iota(jnp.int32, (2 * SUB, LANES), 0)
-    patterns = [(sub + 2 * SUB * k).astype(F32).astype(BF) for k in range(LANES // SUB)]
+    patterns = [(sub + 2 * SUB * k).astype(F32).astype(BF) for k in range(LANES // (2 * SUB))]
     zero, one = jnp.zeros((2 * SUB, LANES), BF), jnp.ones((2 * SUB, LANES), BF)
 
     def product(i, code):
         spread = [jnp.broadcast_to(code[s : s + 1], (SUB, LANES)) for s in range(SUB)]
         hot = []
         for s in range(SUB):
-            low = (spread[s] & (2 * LANES - 1)).astype(F32)
+            low = (spread[s] & (LANES - 1)).astype(F32)
             low = jnp.concatenate([low, low], axis=0).astype(BF)
             hot.append(jnp.concatenate([jnp.where(low == p, one, zero) for p in patterns], axis=0))
         values = dot(rows_of[i], jnp.concatenate(hot, axis=1), NN)
         for s in range(SUB):
             lanes = slice(LANES * s, LANES * (s + 1))
             items = [values[heads * c : heads * (c + 1), lanes] for c in range(values.shape[0] // heads)]
-            found_rows[i, pl.ds(s, heads, stride=SUB), :] = pick(items, spread[s] >> 8)
+            found_rows[i, pl.ds(s, heads, stride=SUB), :] = pick(items, spread[s] >> 7)
 
     def step(store):
         def run(parts):
@@ -471,9 +469,10 @@
     if len(ref.shape) == 3:
         ref[k] = value
         return
-    rows = ref.shape[2]
+    rows, columns = ref.shape[2], value.shape[1]
+    side = slice(k % 2 * columns, (k % 2 + 1) * columns)
     for d in range(ref.shape[0]):
-        ref[d, k] = value[d * rows : (d + 1) * rows]
+        ref[d, k // 2, :, side] = value[d * rows : (d + 1) * rows]
 
 
 def backward_body(n_head, need, done, *refs):
@@ -672,7 +671,9 @@
     rest = arrived[0].astype(F32)
     for d in range(1, arrived.shape[0]):
         rest = rest + arrived[d].astype(F32)
-    shards[...] = rest
+    columns = shards.shape[2]
+    for k in range(shards.shape[0]):
+        shards[k] = rest[k // 2, :, k % 2 * columns : (k % 2 + 1) * columns]
     done(0)
     need(*range(1, len(parts) + 1))
     value = parts[0][...].astype(F32)
@@ -867,7 +868,7 @@
             (table, *ints),
             [
                 pltpu.VMEM((heads, all_chunks // 2, SUB, LANES), jnp.int32),
-                pltpu.VMEM((len(PRODUCTS), max(CHUNKS) // 2 * heads, 2 * LANES), BF),
+                pltpu.VMEM((len(PRODUCTS), max(CHUNKS) * heads, LANES), BF),
                 pltpu.VMEM((len(PRODUCTS), heads * SUB, LANES), F32),
             ],
         )
@@ -994,7 +995,7 @@
             rows_held[far + r] = lax.ppermute(rows_held[far], "head", [(i, i ^ r) for i in range(n_head)])
     (weight_grads,) = kernel_call(
         lambda *refs: weight_grads_body(n_head, *refs),
-        [struct((n_dp, 6, shard_rows, columns) if stacked else (6, model, columns), BF)],
+        [struct((n_dp, 3, shard_rows, 2 * columns) if stacked else (6, model, columns), BF)],
         "weight_grads",
         6,
         (*given, *mixed, us, act_pre, normed_one, dqkv, *[rows_held[r] for r in range(n_head)]),
@@ -1003,7 +1004,8 @@
         early=(2 * n_head + 2, 2 * n_head + 3),
     )
     if not stacked:
-        weight_grads = weight_grads.reshape(6, n_dp, shard_rows, columns).transpose(1, 0, 2, 3)
+        weight_grads = weight_grads.reshape(3, 2, n_dp, shard_rows, columns).transpose(2, 0, 3, 1, 4)
+        weight_grads = weight_grads.reshape(n_dp, 3, shard_rows, 2 * columns)
     with jax.named_scope("grad_normed_one"):
         rows_back = swap(rows_sent, n_head)
     _, *rows_back = lax.optimization_barrier((weight_grads, *rows_back))

time: 198 us -> 191 us (0.965)
  waiting for transfers between devices: 26.8 us -> 24.1 us
  starting transfers between devices: 50.1 us -> 47.6 us
  Pallas kernels: 102 us -> 99.7 us
    ppermute x1, waiting for transfers between devices: 6.01 us -> 2.64 us  [on_device(): lax.ppermute(inner_sent[k], 'dp', dp_pairs(k))]
    pallas_call x11, Pallas kernels: 102 us -> 99.7 us  [kernel_call(): pl.pallas_call(wrapped, out_shape=tuple((shapes[i] for i, _ in flat)), in...]
    unnamed x91 -> x97, local copies, waits for them, and re-layouts: 9.57 us -> 9.46 us
  transfers between devices with their start and end apart: 36 -> 36, of which waited for: 11 -> 11; matrix products, arithmetic and copies ran while one was open for 3% -> 3% of each run, Pallas kernels for 45% -> 46%
where the time goes in v6:
time: 191 us; the launch traced here: 190 us
  Pallas kernels  99.7 us (52%)
  starting transfers between devices  47.6 us (25%)
  waiting for transfers between devices  24.1 us (13%)
  local copies, waits for them, and re-layouts  13.3 us (7%)
  other arithmetic  3.1 us (2%)
  between operations  2.29 us (1%)
    pallas_call x11, Pallas kernels, kernel_call(): pl.pallas_call(wrapped, out_shape=tuple((shapes[i] for i, _ in flat)), in...  99.7 us
    all_to_all x4, starting transfers between devices, exchange(): return lax.all_to_all(value, axis, split_axis=0, concat_axis=0, tiled=True)  16.4 us
    ppermute x6, starting transfers between devices, far_shards(): lax.ppermute(value, 'dp', dp_pairs(k))  10.1 us
    unnamed x97, local copies, waits for them, and re-layouts  9.46 us
    all_to_all x4, waiting for transfers between devices, exchange(): return lax.all_to_all(value, axis, split_axis=0, concat_axis=0, tiled=True)  8.16 us
    ppermute x9, starting transfers between devices, swap(): lax.ppermute(values[r], 'head', [(i, i ^ r) for i in range(n_head)])  6.23 us
    ppermute x3, waiting for transfers between devices, on_device(): lax.ppermute(outer_sent[k], 'dp', dp_pairs(k * inner))  5.71 us
    ppermute x8, starting transfers between devices, to_head(): return lax.ppermute(value, 'head', [(i, i ^ r) for i in range(n_head)])  4.82 us
  transfers between devices with their start and end apart: 36, of which 11 were waited for; matrix products, arithmetic and copies ran while one was open for 3% of the time, Pallas kernels for 46%

profile of v6, /device:TPU:0, one launch (start us, length us, event | category | flops | bytes accessed | tf_op | source)
XLA Modules:
  0.0 190.2 jit_solution(201362407052171245)
XLA Ops:
  3.8 5.1 %collective-permute-start.5 = (bf16[3,96,192]{2,1,0:T(8,128)(2,1)S(1)}, bf16[3,96,192]{2,1,0:T(8,128)(2,1)S(1)}, u32[]{:S(2)}, u32[]{:S(2)}) collective-permute-start(bf16[3,96,192]{2,1,0:T(8,128)(2,1)S(1)} %pad_maximum_fusion.3), channel_id=1, source_target_pairs={{0,24},{4,28},{8,16},{12,20},{16,8},{20,12},{24,0},{28,4},{1,25},{... | collective-permute-start | bytes 331784 | tf_op jit(solution)/shard_map/rest_far/ppermute | solution.py:817
  12.1 5.8 %all-to-all-start = ((bf16[8,8,8,128]{3,2,1,0:T(8,128)(2,1)}), bf16[8,8,8,128]{3,2,1,0:T(8,128)(2,1)S(1)}, u32[]{:S(2)}, u32[]{:S(2)}) async-start(bf16[8,8,8,128]{3,2,1,0:T(8,128)(2,1)} %broadcast_in_dim.4), calls=%async_computation | async-start | bytes 262144 | tf_op jit(solution)/shard_map/table_all/all_to_all | solution.py:748
  20.3 2.6 %collective-permute-done.4 = bf16[3,96,192]{2,1,0:T(8,128)(2,1)S(1)} collective-permute-done((bf16[3,96,192]{2,1,0:T(8,128)(2,1)S(1)}, bf16[3,96,192]{2,1,0:T(8,128)(2,1)S(1)}, u32[]{:S(2)}, u32[]{:S(2)}) %collective-permute-start.4) | collective-permute-done | bytes 110624 | tf_op jit(solution)/shard_map/rest_far/ppermute | solution.py:817
  22.8 3.2 %collective-permute-start.9 = (bf16[336,192]{1,0:T(8,128)(2,1)S(1)}, bf16[336,192]{1,0:T(8,128)(2,1)S(1)}, u32[]{:S(2)}, u32[]{:S(2)}) collective-permute-start(bf16[336,192]{1,0:T(8,128)(2,1)S(1)} %fusion.6), channel_id=1, source_target_pairs={{0,24},{4,28},{8,16},{12,20},{16,8},{20,12},{24,0},{28,4},{1,25},{... | collective-permute-start | bytes 387080 | tf_op jit(solution)/shard_map/qkv_far/ppermute | solution.py:817
  29.6 10.8 %pair_bias.2 = (f32[8,2,64,128]{3,2,1,0:T(8,128)}, f32[8,2,64,128]{3,2,1,0:T(8,128)}) custom-call(bf16[512,128]{1,0:T(8,128)(2,1)} %bitcast.62, s32[4,64,64]{2,1,0:T(8,128)} %refs_1_.5, s32[5,4,64,64]{3,2,1,0:T(8,128)} %refs_2_.5, s32[4,64,64]{2,1,0:T(8,128)} %refs_3_.5, s32[1,256,256]{2,1,0:T(8,128)} %refs_5_.8, s32[5,1,256,256]{3,2,1,0:T(8,128)} %refs_6_.8, ...), custom_call_target="tpu_custom_call" | custom-call | flops 12000000000 | bytes 1048576 | tf_op jit(solution)/shard_map/pair_bias/pallas_call | solution.py:127
  45.7 14.8 %pair_bias.3.refs_11_ = f32[8,2,192,128]{3,2,1,0:T(8,128)} custom-call(bf16[512,128]{1,0:T(8,128)(2,1)} %bitcast.63, s32[1,256,256]{2,1,0:T(8,128)} %refs_5_.8, s32[5,1,256,256]{3,2,1,0:T(8,128)} %refs_6_.8, s32[1,256,256]{2,1,0:T(8,128)} %refs_7_.2), custom_call_target="tpu_custom_call" | custom-call | flops 20000000000 | bytes 1048576 | tf_op jit(solution)/shard_map/pair_bias/pallas_call | solution.py:127
  61.9 7.7 %attend_forward.1 = (bf16[512,768]{1,0:T(8,128)(2,1)}, bf16[3,512,192]{2,1,0:T(8,128)(2,1)}, f32[8,256,256]{2,1,0:T(8,128)}, f32[8,2,128,128]{3,2,1,0:T(8,128)},...) custom-call(bf16[2,128,768]{2,1,0:T(8,128)(2,1)} %copy-done.21, ...), custom_call_target="tpu_custom_call" | custom-call | flops 12000000000 | bytes 1048576 | tf_op jit(solution)/shard_map/attend_forward/pallas_call | solution.py:127
  77.8 7.5 %feed_forward.1 = (bf16[128,768]{1,0:T(8,128)(2,1)}, f32[128,768]{1,0:T(8,128)}, f32[4,768]{1,0:T(4,128)}, f32[4,192]{1,0:T(4,128)}, bf16[2,128,768]{2,1,0:T(8,1...) custom-call(bf16[128,192]{1,0:T(8,128)(2,1)} %get-tuple-element.140., ...), custom_call_target="tpu_custom_call" | custom-call | flops 6000000000 | bytes 1048576 | tf_op jit(solution)/shard_map/feed_forward/pallas_call | solution.py:127
  88.2 3.6 %all-to-all-start.1 = ((bf16[4,128,512]{2,1,0:T(8,128)(2,1)}), bf16[4,128,512]{2,1,0:T(8,128)(2,1)S(1)}, u32[]{:S(2)}, u32[]{:S(2)}) async-start(bf16[4,128,512]{2,1,0:T(8,128)(2,1)} %get-tuple-element.150), calls=%async_computation.1 | async-start | bytes 1048576 | tf_op jit(solution)/shard_map/act_pre/all_to_all | solution.py:748
  92.5 9.2 %attend_backward.1 = (f32[1024,128]{1,0:T(8,128)}, f32[4096,128]{1,0:T(8,128)}, bf16[3,512,192]{2,1,0:T(8,128)(2,1)}, f32[2,4,192]{2,1,0:T(4,128)}, bf16[128,768...) custom-call(bf16[128,192]{1,0:T(8,128)(2,1)} %get-tuple-element.152.refs_0_, ...), custom_call_target="tpu_custom_call" | custom-call | flops 14000000000 | bytes 1048576 | tf_op jit(solution)/shard_map/attend_backward/pallas_call | solution.py:127
  106.5 5.6 %weight_grads.1 = bf16[8,3,96,384]{3,2,1,0:T(8,128)(2,1)} custom-call(bf16[2,128,768]{2,1,0:T(8,128)(2,1)} %copy-done.21, bf16[2,128,768]{2,1,0:T(8,128)(2,1)} %collective-permute-done.11.refs_1_, bf16[2,128,768]{2,1,0:T(8,128)(2,1)} %collective-permute-done.refs_2_, bf16[2,128,768]{2,1,0:T(8,128)(2,1)} %collective-permute-done.12.refs_3_, ...), custom_call_target="tpu_custom_call" | custom-call | flops 6000000000 | bytes 1048576 | tf_op jit(solution)/shard_map/weight_grads/pallas_call | solution.py:127
  112.1 4.2 %all-to-all-start.2 = ((bf16[8,3,96,384]{3,2,1,0:T(8,128)(2,1)}), bf16[8,3,96,384]{3,2,1,0:T(8,128)(2,1)S(1)}, u32[]{:S(2)}, u32[]{:S(2)}) async-start(bf16[8,3,96,384]{3,2,1,0:T(8,128)(2,1)} %weight_grads.1), calls=%async_computation.2 | async-start | bytes 3538944 | tf_op jit(solution)/shard_map/weight_grads/all_to_all | solution.py:748
  117.1 3.3 %input_grad.1 = (bf16[128,768]{1,0:T(8,128)(2,1)}, bf16[2,4,16,128]{3,2,1,0:T(8,128)(2,1)}) custom-call(bf16[128,768]{1,0:T(8,128)(2,1)} %get-tuple-element.168.refs_0_, bf16[128,768]{1,0:T(8,128)(2,1)} %copy-done.34, bf16[128,768]{1,0:T(8,128)(2,1)} %copy-done.35, bf16[128,768]{1,0:T(8,128)(2,1)} %copy-done.36, s32[2]{0:T(128)} %pad_add_fusion.refs_4_.refs_8_.refs_0_, ...), custom_call_target="tpu_custom_call" | custom-call | flops 3000000000 | bytes 1048576 | tf_op jit(solution)/shard_map/input_grad/pallas_call | solution.py:127
  120.3 33.6 %table_scatter.1 = (bf16[4,80,128]{2,1,0:T(8,128)(2,1)}, bf16[4,80,128]{2,1,0:T(8,128)(2,1)}) custom-call(f32[1024,128]{1,0:T(8,128)} %get-tuple-element.177.refs_0_, s32[4,64,64]{2,1,0:T(8,128)} %refs_1_.5, s32[5,4,64,64]{3,2,1,0:T(8,128)} %refs_2_.5, s32[4,64,64]{2,1,0:T(8,128)} %refs_3_.5, f32[4096,128]{1,0:T(8,128)} %get-tuple-element.178.refs_4_, ...), custom_call_target="tpu_custom_call" | custom-call | flops 40000000000 | bytes 1048576 | tf_op jit(solution)/shard_map/table_scatter/pallas_call | solution.py:127
  153.9 2.1 %collective-permute-start.28 = (bf16[4,80,128]{2,1,0:T(8,128)(2,1)}, bf16[4,80,128]{2,1,0:T(8,128)(2,1)S(1)}, u32[]{:S(2)}, u32[]{:S(2)}) collective-permute-start(bf16[4,80,128]{2,1,0:T(8,128)(2,1)} %get-tuple-element.181), channel_id=1, source_target_pairs={{0,4},{4,0},{8,12},{12,8},{16,20},{20,16},{24,28},{28,24},{1,5},{5... | collective-permute-start | bytes 245768 | tf_op jit(solution)/shard_map/table_inner/ppermute | solution.py:1035
  156.0 2.6 %collective-permute-done.28.refs_1_ = bf16[4,80,128]{2,1,0:T(8,128)(2,1)S(1)} collective-permute-done((bf16[4,80,128]{2,1,0:T(8,128)(2,1)}, bf16[4,80,128]{2,1,0:T(8,128)(2,1)S(1)}, u32[]{:S(2)}, u32[]{:S(2)}) %collective-permute-start.28) | collective-permute-done | bytes 81952 | tf_op jit(solution)/shard_map/table_inner/ppermute | solution.py:1035
  160.9 2.1 %collective-permute-start.29 = (bf16[80,128]{1,0:T(8,128)(2,1)}, bf16[80,128]{1,0:T(8,128)(2,1)S(1)}, u32[]{:S(2)}, u32[]{:S(2)}) collective-permute-start(bf16[80,128]{1,0:T(8,128)(2,1)} %get-tuple-element.183), channel_id=1, source_target_pairs={{0,8},{4,12},{8,0},{12,4},{16,24},{20,28},{24,16},{28,20},{1,9},{5... | collective-permute-start | bytes 61448 | tf_op jit(solution)/shard_map/table_outer/ppermute | solution.py:1045
  163.0 2.4 %collective-permute-start.30 = (bf16[80,128]{1,0:T(8,128)(2,1)}, bf16[80,128]{1,0:T(8,128)(2,1)S(1)}, u32[]{:S(2)}, u32[]{:S(2)}) collective-permute-start(bf16[80,128]{1,0:T(8,128)(2,1)} %get-tuple-element.184), channel_id=1, source_target_pairs={{0,16},{4,20},{8,24},{12,28},{16,0},{20,4},{24,8},{28,12},{1,17},{... | collective-permute-start | bytes 61448 | tf_op jit(solution)/shard_map/table_outer/ppermute | solution.py:1045
  165.5 2.5 %collective-permute-done.30.refs_3_ = bf16[80,128]{1,0:T(8,128)(2,1)S(1)} collective-permute-done((bf16[80,128]{1,0:T(8,128)(2,1)}, bf16[80,128]{1,0:T(8,128)(2,1)S(1)}, u32[]{:S(2)}, u32[]{:S(2)}) %collective-permute-start.30) | collective-permute-done | bytes 20512 | tf_op jit(solution)/shard_map/table_outer/ppermute | solution.py:1045
  168.0 3.2 %collective-permute-done.31.refs_4_ = bf16[80,128]{1,0:T(8,128)(2,1)S(1)} collective-permute-done((bf16[80,128]{1,0:T(8,128)(2,1)}, bf16[80,128]{1,0:T(8,128)(2,1)S(1)}, u32[]{:S(2)}, u32[]{:S(2)}) %collective-permute-start.31) | collective-permute-done | bytes 20512 | tf_op jit(solution)/shard_map/table_outer/ppermute | solution.py:1045
  172.4 2.8 %shard_sums.1 = (f32[6,96,192]{2,1,0:T(8,128)}, f32[64,128]{1,0:T(8,128)}, f32[32,8,128]{2,1,0:T(8,128)}) custom-call(bf16[8,3,96,384]{3,2,1,0:T(8,128)(2,1)} %copy-done.19, bf16[80,128]{1,0:T(8,128)(2,1)} %get-tuple-element.187.refs_1_, bf16[80,128]{1,0:T(8,128)(2,1)} %copy-done.44, bf16[80,128]{1,0:T(8,128)(2,1)} %copy-done.45, bf16[80,128]{1,0:T(8,128)(2,1)} %copy-done.46), custom_call_target="tpu_custom_call" | custom-call | flops 4000000000 | bytes 1048576 | tf_op jit(solution)/shard_map/shard_sums/pallas_call | solution.py:127
  175.3 2.7 %all-to-all-start.3 = ((f32[32,8,128]{2,1,0:T(8,128)}), f32[32,8,128]{2,1,0:T(8,128)S(1)}, u32[]{:S(2)}, u32[]{:S(2)}) async-start(f32[32,8,128]{2,1,0:T(8,128)} %get-tuple-element.191), calls=%async_computation.3 | async-start | bytes 262144 | tf_op jit(solution)/shard_map/squares/all_to_all | solution.py:748
  179.4 6.9 %all-to-all-done.3.refs_1_ = f32[32,8,128]{2,1,0:T(8,128)S(1)} async-done(((f32[32,8,128]{2,1,0:T(8,128)}), f32[32,8,128]{2,1,0:T(8,128)S(1)}, u32[]{:S(2)}, u32[]{:S(2)}) %all-to-all-start.3) | async-done | bytes 131104 | tf_op jit(solution)/shard_map/squares/all_to_all | solution.py:748
  187.2 2.8 %update.1 = (f32[4,96,192]{2,1,0:T(8,128)}, f32[4,96,192]{2,1,0:T(8,128)}, f32[4,96,192]{2,1,0:T(8,128)}, f32[192,96]{1,0:T(8,128)}, f32[192,96]{1,0:T(8,128)}, ...) custom-call(s32[2]{0:T(128)S(1)} %copy-done.16, ...), custom_call_target="tpu_custom_call" | custom-call | flops 3000000000 | bytes 1048576 | tf_op jit(solution)/shard_map/update/pallas_call | solution.py:127
  (177 shorter events, 40.8 us)
Async XLA Ops:
  3.8 16.5 %collective-permute-start.5 = (bf16[3,96,192]{2,1,0:T(8,128)(2,1)S(1)}, bf16[3,96,192]{2,1,0:T(8,128)(2,1)S(1)}, u32[]{:S(2)}, u32[]{:S(2)}) collective-permute-start(bf16[3,96,192]{2,1,0:T(8,128)(2,1)S(1)} %pad_maximum_fusion.3), channel_id=1, source_target_pairs={{0,24},{4,28},{8,16},{12,20},{16,8},{20,12},{24,0},{28,4},{1,25},{... | collective-permute-start | bytes 331784 | tf_op jit(solution)/shard_map/rest_far/ppermute | solution.py:817
  8.9 13.9 %collective-permute-start.4 = (bf16[3,96,192]{2,1,0:T(8,128)(2,1)S(1)}, bf16[3,96,192]{2,1,0:T(8,128)(2,1)S(1)}, u32[]{:S(2)}, u32[]{:S(2)}) collective-permute-start(bf16[3,96,192]{2,1,0:T(8,128)(2,1)S(1)} %pad_maximum_fusion.3), channel_id=1, source_target_pairs={{0,16},{4,20},{8,24},{12,28},{16,0},{20,4},{24,8},{28,12},{1,17},{... | collective-permute-start | bytes 331784 | tf_op jit(solution)/shard_map/rest_far/ppermute | solution.py:817
  8.9 13.9 %collective-permute-start.3 = (bf16[3,96,192]{2,1,0:T(8,128)(2,1)S(1)}, bf16[3,96,192]{2,1,0:T(8,128)(2,1)S(1)}, u32[]{:S(2)}, u32[]{:S(2)}) collective-permute-start(bf16[3,96,192]{2,1,0:T(8,128)(2,1)S(1)} %pad_maximum_fusion.3), channel_id=1, source_target_pairs={{0,8},{4,12},{8,0},{12,4},{16,24},{20,28},{24,16},{28,20},{1,9},{5... | collective-permute-start | bytes 331784 | tf_op jit(solution)/shard_map/rest_far/ppermute | solution.py:817
  9.7 8.9 %collective-permute-start.1 = (f32[9,96]{1,0:T(8,128)S(1)}, f32[9,96]{1,0:T(8,128)S(1)}, u32[]{:S(2)}, u32[]{:S(2)}) collective-permute-start(f32[9,96]{1,0:T(8,128)S(1)} %dynamic_update_slice.5), channel_id=1, source_target_pairs={{0,2},{1,3},{2,0},{3,1},{4,6},{5,7},{6,4},{7,5},{8,10},{9,11},{10,... | collective-permute-start | bytes 10376 | tf_op jit(solution)/shard_map/vectors_head/ppermute | solution.py:824
  12.1 16.8 %all-to-all-start = ((bf16[8,8,8,128]{3,2,1,0:T(8,128)(2,1)}), bf16[8,8,8,128]{3,2,1,0:T(8,128)(2,1)S(1)}, u32[]{:S(2)}, u32[]{:S(2)}) async-start(bf16[8,8,8,128]{3,2,1,0:T(8,128)(2,1)} %broadcast_in_dim.4), calls=%async_computation | async-start | bytes 262144 | tf_op jit(solution)/shard_map/table_all/all_to_all | solution.py:748
  18.0 22.5 %collective-permute-start = (bf16[2,128,768]{2,1,0:T(8,128)(2,1)S(1)}, bf16[2,128,768]{2,1,0:T(8,128)(2,1)}, u32[]{:S(2)}, u32[]{:S(2)}) collective-permute-start(bf16[2,128,768]{2,1,0:T(8,128)(2,1)S(1)} %pad_maximum_fusion.2.refs_0_), channel_id=1, source_target_pairs={{0,2},{1,3},{2,0},{3,1},{4,6},{5,7},{6,4},{7,5},{8,10},{9,11},{10,... | collective-permute-start | bytes 1179656 | tf_op jit(solution)/shard_map/rows_far/ppermute | solution.py:824
  22.8 17.6 %collective-permute-start.9 = (bf16[336,192]{1,0:T(8,128)(2,1)S(1)}, bf16[336,192]{1,0:T(8,128)(2,1)S(1)}, u32[]{:S(2)}, u32[]{:S(2)}) collective-permute-start(bf16[336,192]{1,0:T(8,128)(2,1)S(1)} %fusion.6), channel_id=1, source_target_pairs={{0,24},{4,28},{8,16},{12,20},{16,8},{20,12},{24,0},{28,4},{1,25},{... | collective-permute-start | bytes 387080 | tf_op jit(solution)/shard_map/qkv_far/ppermute | solution.py:817
  26.0 14.5 %collective-permute-start.8 = (bf16[336,192]{1,0:T(8,128)(2,1)S(1)}, bf16[336,192]{1,0:T(8,128)(2,1)S(1)}, u32[]{:S(2)}, u32[]{:S(2)}) collective-permute-start(bf16[336,192]{1,0:T(8,128)(2,1)S(1)} %fusion.6), channel_id=1, source_target_pairs={{0,16},{4,20},{8,24},{12,28},{16,0},{20,4},{24,8},{28,12},{1,17},{... | collective-permute-start | bytes 387080 | tf_op jit(solution)/shard_map/qkv_far/ppermute | solution.py:817
  26.0 14.5 %collective-permute-start.7 = (bf16[336,192]{1,0:T(8,128)(2,1)S(1)}, bf16[336,192]{1,0:T(8,128)(2,1)S(1)}, u32[]{:S(2)}, u32[]{:S(2)}) collective-permute-start(bf16[336,192]{1,0:T(8,128)(2,1)S(1)} %fusion.6), channel_id=1, source_target_pairs={{0,8},{4,12},{8,0},{12,4},{16,24},{20,28},{24,16},{28,20},{1,9},{5... | collective-permute-start | bytes 387080 | tf_op jit(solution)/shard_map/qkv_far/ppermute | solution.py:817
  27.4 13.2 %collective-permute-start.6 = (bf16[4,3,96,192]{3,2,1,0:T(8,128)(2,1)S(1)}, bf16[4,3,96,192]{3,2,1,0:T(8,128)(2,1)S(1)}, u32[]{:S(2)}, u32[]{:S(2)}) collective-permute-start(bf16[4,3,96,192]{3,2,1,0:T(8,128)(2,1)S(1)} %pad_maximum_fusion.1), channel_id=1, source_target_pairs={{0,4},{4,0},{8,12},{12,8},{16,20},{20,16},{24,28},{28,24},{1,5},{5... | collective-permute-start | bytes 1327112 | tf_op jit(solution)/shard_map/rest_near/ppermute | solution.py:821
  40.4 20.1 %collective-permute-start.11 = (bf16[2,128,768]{2,1,0:T(8,128)(2,1)S(1)}, bf16[2,128,768]{2,1,0:T(8,128)(2,1)}, u32[]{:S(2)}, u32[]{:S(2)}) collective-permute-start(bf16[2,128,768]{2,1,0:T(8,128)(2,1)S(1)} %pad_maximum_fusion.2.refs_0_), channel_id=1, source_target_pairs={{0,1},{1,0},{2,3},{3,2},{4,5},{5,4},{6,7},{7,6},{8,9},{9,8},{10,11... | collective-permute-start | bytes 1179656 | tf_op jit(solution)/shard_map/rows_near/ppermute | solution.py:824
  41.4 28.6 %collective-permute-start.14 = (bf16[8,3,96,192]{3,2,1,0:T(8,128)(2,1)S(1)}, bf16[8,3,96,192]{3,2,1,0:T(8,128)(2,1)}, u32[]{:S(2)}, u32[]{:S(2)}) collective-permute-start(bf16[8,3,96,192]{3,2,1,0:T(8,128)(2,1)S(1)} %constant_dynamic-update-slice_fusion.refs_9_), channel_id=1, source_target_pairs={{0,2},{1,3},{2,0},{3,1},{4,6},{5,7},{6,4},{7,5},{8,10},{9,11},{10,... | collective-permute-start | bytes 2654216 | tf_op jit(solution)/shard_map/rest_far_head/ppermute | solution.py:824
  43.2 26.7 %collective-permute-start.13 = (bf16[8,3,96,192]{3,2,1,0:T(8,128)(2,1)S(1)}, bf16[8,3,96,192]{3,2,1,0:T(8,128)(2,1)}, u32[]{:S(2)}, u32[]{:S(2)}) collective-permute-start(bf16[8,3,96,192]{3,2,1,0:T(8,128)(2,1)S(1)} %constant_dynamic-update-slice_fusion.refs_9_), channel_id=1, source_target_pairs={{0,1},{1,0},{2,3},{3,2},{4,5},{5,4},{6,7},{7,6},{8,9},{9,8},{10,11... | collective-permute-start | bytes 2654216 | tf_op jit(solution)/shard_map/rest_near_head/ppermute | solution.py:824
  43.4 17.1 %collective-permute-start.12 = (bf16[2,128,768]{2,1,0:T(8,128)(2,1)}, bf16[2,128,768]{2,1,0:T(8,128)(2,1)}, u32[]{:S(2)}, u32[]{:S(2)}) collective-permute-start(bf16[2,128,768]{2,1,0:T(8,128)(2,1)} %collective-permute-done.refs_2_), channel_id=1, source_target_pairs={{0,1},{1,0},{2,3},{3,2},{4,5},{5,4},{6,7},{7,6},{8,9},{9,8},{10,11... | collective-permute-start | bytes 1179656 | tf_op jit(solution)/shard_map/rows_near/ppermute | solution.py:824
  45.3 15.5 %collective-permute-start.10 = (bf16[4,336,192]{1,2,0:T(8,128)(2,1)S(1)}, bf16[4,336,192]{1,2,0:T(8,128)(2,1)S(1)}, u32[]{:S(2)}, u32[]{:S(2)}) collective-permute-start(bf16[4,336,192]{1,2,0:T(8,128)(2,1)S(1)} %copy.49), channel_id=1, source_target_pairs={{0,4},{4,0},{8,12},{12,8},{16,20},{20,16},{24,28},{28,24},{1,5},{5... | collective-permute-start | bytes 1548296 | tf_op jit(solution)/shard_map/qkv_near/ppermute | solution.py:821
  69.9 6.8 %collective-permute-start.18 = (bf16[8,3,96,192]{3,2,1,0:T(8,128)(2,1)}, bf16[8,3,96,192]{3,2,1,0:T(8,128)(2,1)S(1)}, u32[]{:S(2)}, u32[]{:S(2)}) collective-permute-start(bf16[8,3,96,192]{3,2,1,0:T(8,128)(2,1)} %collective-permute-done.14.refs_11_), channel_id=1, source_target_pairs={{0,1},{1,0},{2,3},{3,2},{4,5},{5,4},{6,7},{7,6},{8,9},{9,8},{10,11... | collective-permute-start | bytes 2654216 | tf_op jit(solution)/shard_map/rest_near_head/ppermute | solution.py:824
  87.2 14.4 %collective-permute-start.23 = (bf16[2,128,768]{2,1,0:T(8,128)(2,1)}, bf16[2,128,768]{2,1,0:T(8,128)(2,1)S(1)}, u32[]{:S(2)}, u32[]{:S(2)}) collective-permute-start(bf16[2,128,768]{2,1,0:T(8,128)(2,1)} %get-tuple-element.160.refs_12_), channel_id=1, source_target_pairs={{0,2},{1,3},{2,0},{3,1},{4,6},{5,7},{6,4},{7,5},{8,10},{9,11},{10,... | collective-permute-start | bytes 1179656 | tf_op jit(solution)/shard_map/normed_grad/ppermute | solution.py:967
  87.7 14.0 %collective-permute-start.22 = (bf16[2,128,768]{2,1,0:T(8,128)(2,1)}, bf16[2,128,768]{2,1,0:T(8,128)(2,1)S(1)}, u32[]{:S(2)}, u32[]{:S(2)}) collective-permute-start(bf16[2,128,768]{2,1,0:T(8,128)(2,1)} %get-tuple-element.160.refs_12_), channel_id=1, source_target_pairs={{0,1},{1,0},{2,3},{3,2},{4,5},{5,4},{6,7},{7,6},{8,9},{9,8},{10,11... | collective-permute-start | bytes 1179656 | tf_op jit(solution)/shard_map/normed_grad/ppermute | solution.py:967
  88.2 17.4 %all-to-all-start.1 = ((bf16[4,128,512]{2,1,0:T(8,128)(2,1)}), bf16[4,128,512]{2,1,0:T(8,128)(2,1)S(1)}, u32[]{:S(2)}, u32[]{:S(2)}) async-start(bf16[4,128,512]{2,1,0:T(8,128)(2,1)} %get-tuple-element.150), calls=%async_computation.1 | async-start | bytes 1048576 | tf_op jit(solution)/shard_map/act_pre/all_to_all | solution.py:748
  102.2 14.0 %collective-permute-start.25 = (bf16[128,768]{1,0:T(8,128)(2,1)}, bf16[128,768]{1,0:T(8,128)(2,1)S(1)}, u32[]{:S(2)}, u32[]{:S(2)}) collective-permute-start(bf16[128,768]{1,0:T(8,128)(2,1)} %get-tuple-element.165), channel_id=1, source_target_pairs={{0,1},{1,0},{2,3},{3,2},{4,5},{5,4},{6,7},{7,6},{8,9},{9,8},{10,11... | collective-permute-start | bytes 589832 | tf_op jit(solution)/shard_map/grad_normed_one/ppermute | solution.py:758
  102.3 13.9 %collective-permute-start.26 = (bf16[128,768]{1,0:T(8,128)(2,1)}, bf16[128,768]{1,0:T(8,128)(2,1)S(1)}, u32[]{:S(2)}, u32[]{:S(2)}) collective-permute-start(bf16[128,768]{1,0:T(8,128)(2,1)} %get-tuple-element.166), channel_id=1, source_target_pairs={{0,2},{1,3},{2,0},{3,1},{4,6},{5,7},{6,4},{7,5},{8,10},{9,11},{10,... | collective-permute-start | bytes 589832 | tf_op jit(solution)/shard_map/grad_normed_one/ppermute | solution.py:758
  104.3 12.0 %collective-permute-start.27 = (bf16[128,768]{1,0:T(8,128)(2,1)}, bf16[128,768]{1,0:T(8,128)(2,1)S(1)}, u32[]{:S(2)}, u32[]{:S(2)}) collective-permute-start(bf16[128,768]{1,0:T(8,128)(2,1)} %get-tuple-element.167), channel_id=1, source_target_pairs={{0,3},{1,2},{2,1},{3,0},{4,7},{5,6},{6,5},{7,4},{8,11},{9,10},{10,... | collective-permute-start | bytes 589832 | tf_op jit(solution)/shard_map/grad_normed_one/ppermute | solution.py:758
  112.1 59.1 %all-to-all-start.2 = ((bf16[8,3,96,384]{3,2,1,0:T(8,128)(2,1)}), bf16[8,3,96,384]{3,2,1,0:T(8,128)(2,1)S(1)}, u32[]{:S(2)}, u32[]{:S(2)}) async-start(bf16[8,3,96,384]{3,2,1,0:T(8,128)(2,1)} %weight_grads.1), calls=%async_computation.2 | async-start | bytes 3538944 | tf_op jit(solution)/shard_map/weight_grads/all_to_all | solution.py:748
  175.3 11.0 %all-to-all-start.3 = ((f32[32,8,128]{2,1,0:T(8,128)}), f32[32,8,128]{2,1,0:T(8,128)S(1)}, u32[]{:S(2)}, u32[]{:S(2)}) async-start(f32[32,8,128]{2,1,0:T(8,128)} %get-tuple-element.191), calls=%async_computation.3 | async-start | bytes 262144 | tf_op jit(solution)/shard_map/squares/all_to_all | solution.py:748
  (59 other events, 373.0 us)

commit v7 on v6

--- a/solution.py
+++ b/solution.py
@@ -314,9 +314,9 @@
 
     need(0, 1, 2, 3)
     narrow, width = sd.shape[1], bd.shape[1]
-    each_block(small_block, (sd, sp, sl), 0, narrow // SUB, sd.shape[0] // 2, 4, step(small_grads, narrow))
+    each_block(small_block, (sd, sp, sl), 0, narrow // SUB, sd.shape[0] // 2, 8, step(small_grads, narrow))
     need(4, 5, 6, 7)
-    each_block(big_block, (bd, bp, bl), 0, width // SUB, width // LANES, 4, step(big_grads, width))
+    each_block(big_block, (bd, bp, bl), 0, width // SUB, width // LANES, 8, step(big_grads, width))
     need(9)
     inner, outer, height, _ = parcel.shape
     height -= VECTOR_ROWS
@@ -372,6 +372,17 @@
 
 def peer_block(me, r, rows):
     return pl.ds(pl.multiple_of((me[0] ^ r) * rows, rows), rows)
+
+
+def pack_rows(ref, value):
+    half, columns = ref.shape[0], value.shape[1]
+    ref[:, 0:columns] = value[:half]
+    ref[:, columns:] = value[half:]
+
+
+def unpack_rows(ref):
+    columns = ref.shape[1] // 2
+    return jnp.concatenate([ref[:, 0:columns], ref[:, columns:]], axis=0)
 
 
 def forward_body(n_head, vector_row, need, done, *refs):
@@ -462,7 +473,7 @@
         attend(span, small_extra, small_live[pair], store_small)
     done(3)
     for r in range(n_head):
-        mixed_out[r][...] = mixed[peer_block(me, r, block), :]
+        pack_rows(mixed_out[r], mixed[peer_block(me, r, block), :])
 
 
 def put_matrix(ref, k, value):
@@ -485,9 +496,9 @@
     narrow = wide // 2
     columns = qkv.shape[2]
     halves = width // LANES
-    block = grads_in[0].shape[0]
+    block = 2 * grads_in[0].shape[0]
     for r in range(n_head):
-        grad_heads[peer_block(me, r, block), :] = grads_in[r][...]
+        grad_heads[peer_block(me, r, block), :] = unpack_rows(grads_in[r])
 
     need(n_head + 3)
 
@@ -550,12 +561,11 @@
     layer_out, grad_hidden, sums, pre_sums, normed_grad, act_pre = refs[:6]
     grad_heads = refs[6:]
     need(*range(n_head + 5))
-    columns = mixed[0].shape[1]
-    slot = parcel_slot(columns)
+    columns = mixed[0].shape[1] // 2
     hidden = rows[...].astype(F32) + vectors[6:7, :]
     for r in range(n_head):
         need(n_head + 5 + r)
-        hidden = hidden + dot(mixed[r][...], whole_matrix(weights[r], 0), NT)
+        hidden = hidden + dot(unpack_rows(mixed[r]), whole_matrix(weights[r], 0), NT)
     xhat, spread = norm_parts(hidden)
     low = (xhat * vectors[2:3, :] + vectors[3:4, :]).astype(BF)
     normed_grad[0] = low
@@ -574,7 +584,7 @@
         pre_sums[pl.ds(peer, 1), :] = jnp.sum(low_grad.astype(F32), axis=0, keepdims=True)
         grad_normed = grad_normed + dot(low_grad, into, NT)
         act_pre[peer, :, 0:columns] = active
-        act_pre[peer, :, slot : slot + columns] = low_grad
+        act_pre[peer, :, columns : 2 * columns] = low_grad
     layer_out[...] = final.astype(BF)
     wide = cotangent.astype(F32)
     grad = wide + norm_back(grad_normed * vectors[2:3, :], xhat, spread)
@@ -582,23 +592,18 @@
     grad_small = grad.astype(BF)
     normed_grad[1] = grad_small
     for r in range(n_head):
-        grad_heads[r][...] = dot(grad_small, whole_matrix(weights[r], 0), NN).astype(BF)
+        pack_rows(grad_heads[r], dot(grad_small, whole_matrix(weights[r], 0), NN).astype(BF))
     sums[0:1, :] = jnp.sum(grad_normed * xhat, axis=0, keepdims=True)
     sums[1:2, :] = jnp.sum(grad_normed, axis=0, keepdims=True)
     sums[2:3, :] = jnp.sum(grad, axis=0, keepdims=True)
     sums[3:4, :] = jnp.sum(wide, axis=0, keepdims=True)
 
 
-def parcel_slot(columns):
-    return (columns + LANES - 1) // LANES * LANES
-
-
 def weight_grads_body(n_head, need, done, *refs):
     given, mixed, refs = refs[:n_head], refs[n_head : 2 * n_head], refs[2 * n_head :]
     me, act_pre, normed_one, dqkv = refs[:4]
     normed_grad, out = refs[4 : 4 + n_head], refs[-1]
-    columns = mixed[0].shape[1]
-    slot = parcel_slot(columns)
+    columns = mixed[0].shape[1] // 2
 
     def all_rows(pick):
         return jnp.concatenate([pick(me[0] ^ r) for r in range(n_head)], axis=0)
@@ -607,9 +612,9 @@
     for k in range(3):
         put_matrix(out, k, dot(normed_one[...], dqkv[k], TN).astype(BF))
     need(*range(2 * n_head), 2 * n_head + 1, *range(2 * n_head + 4, 3 * n_head + 4))
-    heads_out = jnp.concatenate([m[...] for m in mixed], axis=0)
+    heads_out = jnp.concatenate([unpack_rows(m) for m in mixed], axis=0)
     put_matrix(out, 3, dot(jnp.concatenate([n[1] for n in normed_grad], axis=0), heads_out, TN).astype(BF))
-    grad_pre = all_rows(lambda p: act_pre[p, :, slot : slot + columns])
+    grad_pre = all_rows(lambda p: act_pre[p, :, columns : 2 * columns])
     put_matrix(out, 4, dot(jnp.concatenate([n[0] for n in normed_grad], axis=0), grad_pre, TN).astype(BF))
     cotangent = jnp.concatenate([g[1] for g in given], axis=0)
     put_matrix(out, 5, dot(cotangent, all_rows(lambda p: act_pre[p, :, 0:columns]), TN).astype(BF))
@@ -904,7 +909,7 @@
         weights_attend = weights_attend[:, : 3 * shard_rows].reshape(n_dp, 3, shard_rows, columns)
         weights_attend = weights_attend.transpose(1, 0, 2, 3).reshape(3, model, columns)
 
-    block = struct((my_rows, columns), BF)
+    block = struct((my_rows // 2, 2 * columns), BF)
     rows_block = struct((my_rows, model), BF)
     normed_one, qkv, big_probs, small_probs, all_vectors, hidden_bias, *mixed = kernel_call(
         lambda *refs: forward_body(n_head, vector_row, *refs),
@@ -946,7 +951,7 @@
             struct((4, model), F32),
             struct((n_head, columns), F32),
             struct((2, my_rows, model), BF),
-            struct((n_head, my_rows, 2 * parcel_slot(columns)), BF),
+            struct((n_head, my_rows, 2 * columns), BF),
             *[block] * n_head,
         ],
         "feed_forward",
@@ -988,7 +993,9 @@
         (n_head + 4,) if stacked else (),
         n_head,
     )
-    small_rows, *arrived = lax.optimization_barrier((small_rows, *[rows_held[r] for r in range(1, far + 1)]))
+    small_rows, act_pre, *arrived = lax.optimization_barrier(
+        (small_rows, act_pre, *[rows_held[r] for r in range(1, far + 1)])
+    )
     rows_held.update(zip(range(1, far + 1), arrived))
     with jax.named_scope("normed_grad"):
         for r in range(1, far):

time: 191 us -> 190 us (level)
  transfers between devices with their start and end apart: 36 -> 36, of which waited for: 11 -> 11; matrix products, arithmetic and copies ran while one was open for 3% -> 3% of each run, Pallas kernels for 46% -> 45%
where the time goes in v7:
time: 190 us; the launch traced here: 189 us
  Pallas kernels  99.2 us (52%)
  starting transfers between devices  46.8 us (25%)
  waiting for transfers between devices  24.7 us (13%)
  local copies, waits for them, and re-layouts  13.2 us (7%)
  other arithmetic  3.1 us (2%)
  between operations  2.3 us (1%)
    pallas_call x11, Pallas kernels, kernel_call(): pl.pallas_call(wrapped, out_shape=tuple((shapes[i] for i, _ in flat)), in...  99.2 us
    all_to_all x4, starting transfers between devices, exchange(): return lax.all_to_all(value, axis, split_axis=0, concat_axis=0, tiled=True)  16.4 us
    ppermute x6, starting transfers between devices, far_shards(): lax.ppermute(value, 'dp', dp_pairs(k))  10.1 us
    unnamed x97, local copies, waits for them, and re-layouts  9.32 us
    all_to_all x4, waiting for transfers between devices, exchange(): return lax.all_to_all(value, axis, split_axis=0, concat_axis=0, tiled=True)  8.91 us
    ppermute x9, starting transfers between devices, swap(): lax.ppermute(values[r], 'head', [(i, i ^ r) for i in range(n_head)])  6.12 us
    ppermute x3, waiting for transfers between devices, on_device(): lax.ppermute(outer_sent[k], 'dp', dp_pairs(k * inner))  5.5 us
    ppermute x8, starting transfers between devices, to_head(): return lax.ppermute(value, 'head', [(i, i ^ r) for i in range(n_head)])  4.82 us
  transfers between devices with their start and end apart: 36, of which 11 were waited for; matrix products, arithmetic and copies ran while one was open for 3% of the time, Pallas kernels for 45%

profile of v7, /device:TPU:0, one launch (start us, length us, event | category | flops | bytes accessed | tf_op | source)
XLA Modules:
  0.0 189.2 jit_solution(5786094856722004656)
XLA Ops:
  3.8 5.1 %collective-permute-start.5 = (bf16[3,96,192]{2,1,0:T(8,128)(2,1)S(1)}, bf16[3,96,192]{2,1,0:T(8,128)(2,1)S(1)}, u32[]{:S(2)}, u32[]{:S(2)}) collective-permute-start(bf16[3,96,192]{2,1,0:T(8,128)(2,1)S(1)} %pad_maximum_fusion.3), channel_id=1, source_target_pairs={{0,24},{4,28},{8,16},{12,20},{16,8},{20,12},{24,0},{28,4},{1,25},{... | collective-permute-start | bytes 331784 | tf_op jit(solution)/shard_map/rest_far/ppermute | solution.py:822
  12.1 5.8 %all-to-all-start = ((bf16[8,8,8,128]{3,2,1,0:T(8,128)(2,1)}), bf16[8,8,8,128]{3,2,1,0:T(8,128)(2,1)S(1)}, u32[]{:S(2)}, u32[]{:S(2)}) async-start(bf16[8,8,8,128]{3,2,1,0:T(8,128)(2,1)} %broadcast_in_dim.4), calls=%async_computation | async-start | bytes 262144 | tf_op jit(solution)/shard_map/table_all/all_to_all | solution.py:753
  20.3 2.6 %collective-permute-done.4 = bf16[3,96,192]{2,1,0:T(8,128)(2,1)S(1)} collective-permute-done((bf16[3,96,192]{2,1,0:T(8,128)(2,1)S(1)}, bf16[3,96,192]{2,1,0:T(8,128)(2,1)S(1)}, u32[]{:S(2)}, u32[]{:S(2)}) %collective-permute-start.4) | collective-permute-done | bytes 110624 | tf_op jit(solution)/shard_map/rest_far/ppermute | solution.py:822
  22.8 3.2 %collective-permute-start.9 = (bf16[336,192]{1,0:T(8,128)(2,1)S(1)}, bf16[336,192]{1,0:T(8,128)(2,1)S(1)}, u32[]{:S(2)}, u32[]{:S(2)}) collective-permute-start(bf16[336,192]{1,0:T(8,128)(2,1)S(1)} %fusion.6), channel_id=1, source_target_pairs={{0,24},{4,28},{8,16},{12,20},{16,8},{20,12},{24,0},{28,4},{1,25},{... | collective-permute-start | bytes 387080 | tf_op jit(solution)/shard_map/qkv_far/ppermute | solution.py:822
  29.6 10.8 %pair_bias.2 = (f32[8,2,64,128]{3,2,1,0:T(8,128)}, f32[8,2,64,128]{3,2,1,0:T(8,128)}) custom-call(bf16[512,128]{1,0:T(8,128)(2,1)} %bitcast.62, s32[4,64,64]{2,1,0:T(8,128)} %refs_1_.5, s32[5,4,64,64]{3,2,1,0:T(8,128)} %refs_2_.5, s32[4,64,64]{2,1,0:T(8,128)} %refs_3_.5, s32[1,256,256]{2,1,0:T(8,128)} %refs_5_.8, s32[5,1,256,256]{3,2,1,0:T(8,128)} %refs_6_.8, ...), custom_call_target="tpu_custom_call" | custom-call | flops 12000000000 | bytes 1048576 | tf_op jit(solution)/shard_map/pair_bias/pallas_call | solution.py:127
  45.7 14.8 %pair_bias.3.refs_11_ = f32[8,2,192,128]{3,2,1,0:T(8,128)} custom-call(bf16[512,128]{1,0:T(8,128)(2,1)} %bitcast.63, s32[1,256,256]{2,1,0:T(8,128)} %refs_5_.8, s32[5,1,256,256]{3,2,1,0:T(8,128)} %refs_6_.8, s32[1,256,256]{2,1,0:T(8,128)} %refs_7_.2), custom_call_target="tpu_custom_call" | custom-call | flops 20000000000 | bytes 1048576 | tf_op jit(solution)/shard_map/pair_bias/pallas_call | solution.py:127
  61.9 7.7 %attend_forward.1 = (bf16[512,768]{1,0:T(8,128)(2,1)}, bf16[3,512,192]{2,1,0:T(8,128)(2,1)}, f32[8,256,256]{2,1,0:T(8,128)}, f32[8,2,128,128]{3,2,1,0:T(8,128)},...) custom-call(bf16[2,128,768]{2,1,0:T(8,128)(2,1)} %copy-done.20, ...), custom_call_target="tpu_custom_call" | custom-call | flops 12000000000 | bytes 1048576 | tf_op jit(solution)/shard_map/attend_forward/pallas_call | solution.py:127
  77.4 7.6 %feed_forward.1 = (bf16[128,768]{1,0:T(8,128)(2,1)}, f32[128,768]{1,0:T(8,128)}, f32[4,768]{1,0:T(4,128)}, f32[4,192]{1,0:T(4,128)}, bf16[2,128,768]{2,1,0:T(8,1...) custom-call(bf16[64,384]{1,0:T(8,128)(2,1)} %get-tuple-element.141.r, ...), custom_call_target="tpu_custom_call" | custom-call | flops 6000000000 | bytes 1048576 | tf_op jit(solution)/shard_map/feed_forward/pallas_call | solution.py:127
  87.7 3.6 %all-to-all-start.1 = ((bf16[4,128,384]{2,1,0:T(8,128)(2,1)}), bf16[4,128,384]{2,1,0:T(8,128)(2,1)S(1)}, u32[]{:S(2)}, u32[]{:S(2)}) async-start(bf16[4,128,384]{2,1,0:T(8,128)(2,1)} %get-tuple-element.159), calls=%async_computation.1 | async-start | bytes 786432 | tf_op jit(solution)/shard_map/act_pre/all_to_all | solution.py:753
  92.0 9.1 %attend_backward.1 = (f32[1024,128]{1,0:T(8,128)}, f32[4096,128]{1,0:T(8,128)}, bf16[3,512,192]{2,1,0:T(8,128)(2,1)}, f32[2,4,192]{2,1,0:T(4,128)}, bf16[128,768...) custom-call(bf16[64,384]{1,0:T(8,128)(2,1)} %get-tuple-element.151.refs_0_, ...), custom_call_target="tpu_custom_call" | custom-call | flops 14000000000 | bytes 1048576 | tf_op jit(solution)/shard_map/attend_backward/pallas_call | solution.py:127
  101.1 2.0 %all-to-all-done.1.refs_9_ = bf16[4,128,384]{2,1,0:T(8,128)(2,1)S(1)} async-done(((bf16[4,128,384]{2,1,0:T(8,128)(2,1)}), bf16[4,128,384]{2,1,0:T(8,128)(2,1)S(1)}, u32[]{:S(2)}, u32[]{:S(2)}) %all-to-all-start.1) | async-done | bytes 393248 | tf_op jit(solution)/shard_map/act_pre/all_to_all | solution.py:753
  106.0 5.7 %weight_grads.1 = bf16[8,3,96,384]{3,2,1,0:T(8,128)(2,1)} custom-call(bf16[2,128,768]{2,1,0:T(8,128)(2,1)} %copy-done.20, bf16[2,128,768]{2,1,0:T(8,128)(2,1)} %collective-permute-done.11.refs_1_, bf16[2,128,768]{2,1,0:T(8,128)(2,1)} %collective-permute-done.refs_2_, bf16[2,128,768]{2,1,0:T(8,128)(2,1)} %collective-permute-done.12.refs_3_, ...), custom_call_target="tpu_custom_call" | custom-call | flops 6000000000 | bytes 1048576 | tf_op jit(solution)/shard_map/weight_grads/pallas_call | solution.py:127
  111.7 4.2 %all-to-all-start.2 = ((bf16[8,3,96,384]{3,2,1,0:T(8,128)(2,1)}), bf16[8,3,96,384]{3,2,1,0:T(8,128)(2,1)S(1)}, u32[]{:S(2)}, u32[]{:S(2)}) async-start(bf16[8,3,96,384]{3,2,1,0:T(8,128)(2,1)} %weight_grads.1), calls=%async_computation.2 | async-start | bytes 3538944 | tf_op jit(solution)/shard_map/weight_grads/all_to_all | solution.py:753
  116.7 3.3 %input_grad.1 = (bf16[128,768]{1,0:T(8,128)(2,1)}, bf16[2,4,16,128]{3,2,1,0:T(8,128)(2,1)}) custom-call(bf16[128,768]{1,0:T(8,128)(2,1)} %get-tuple-element.170.refs_0_, bf16[128,768]{1,0:T(8,128)(2,1)} %copy-done.34, bf16[128,768]{1,0:T(8,128)(2,1)} %copy-done.35, bf16[128,768]{1,0:T(8,128)(2,1)} %copy-done.36, s32[2]{0:T(128)} %pad_add_fusion.refs_4_.refs_8_.refs_0_, ...), custom_call_target="tpu_custom_call" | custom-call | flops 3000000000 | bytes 1048576 | tf_op jit(solution)/shard_map/input_grad/pallas_call | solution.py:127
  120.0 32.9 %table_scatter.1 = (bf16[4,80,128]{2,1,0:T(8,128)(2,1)}, bf16[4,80,128]{2,1,0:T(8,128)(2,1)}) custom-call(f32[1024,128]{1,0:T(8,128)} %get-tuple-element.179.refs_0_, s32[4,64,64]{2,1,0:T(8,128)} %refs_1_.5, s32[5,4,64,64]{3,2,1,0:T(8,128)} %refs_2_.5, s32[4,64,64]{2,1,0:T(8,128)} %refs_3_.5, f32[4096,128]{1,0:T(8,128)} %get-tuple-element.180.refs_4_, ...), custom_call_target="tpu_custom_call" | custom-call | flops 40000000000 | bytes 1048576 | tf_op jit(solution)/shard_map/table_scatter/pallas_call | solution.py:127
  152.9 2.1 %collective-permute-start.28 = (bf16[4,80,128]{2,1,0:T(8,128)(2,1)}, bf16[4,80,128]{2,1,0:T(8,128)(2,1)S(1)}, u32[]{:S(2)}, u32[]{:S(2)}) collective-permute-start(bf16[4,80,128]{2,1,0:T(8,128)(2,1)} %get-tuple-element.183), channel_id=1, source_target_pairs={{0,4},{4,0},{8,12},{12,8},{16,20},{20,16},{24,28},{28,24},{1,5},{5... | collective-permute-start | bytes 245768 | tf_op jit(solution)/shard_map/table_inner/ppermute | solution.py:1042
  154.9 3.0 %collective-permute-done.28.refs_1_ = bf16[4,80,128]{2,1,0:T(8,128)(2,1)S(1)} collective-permute-done((bf16[4,80,128]{2,1,0:T(8,128)(2,1)}, bf16[4,80,128]{2,1,0:T(8,128)(2,1)S(1)}, u32[]{:S(2)}, u32[]{:S(2)}) %collective-permute-start.28) | collective-permute-done | bytes 81952 | tf_op jit(solution)/shard_map/table_inner/ppermute | solution.py:1042
  162.0 2.4 %collective-permute-start.30 = (bf16[80,128]{1,0:T(8,128)(2,1)}, bf16[80,128]{1,0:T(8,128)(2,1)S(1)}, u32[]{:S(2)}, u32[]{:S(2)}) collective-permute-start(bf16[80,128]{1,0:T(8,128)(2,1)} %get-tuple-element.186), channel_id=1, source_target_pairs={{0,16},{4,20},{8,24},{12,28},{16,0},{20,4},{24,8},{28,12},{1,17},{... | collective-permute-start | bytes 61448 | tf_op jit(solution)/shard_map/table_outer/ppermute | solution.py:1052
  164.7 2.2 %collective-permute-done.30.refs_3_ = bf16[80,128]{1,0:T(8,128)(2,1)S(1)} collective-permute-done((bf16[80,128]{1,0:T(8,128)(2,1)}, bf16[80,128]{1,0:T(8,128)(2,1)S(1)}, u32[]{:S(2)}, u32[]{:S(2)}) %collective-permute-start.30) | collective-permute-done | bytes 20512 | tf_op jit(solution)/shard_map/table_outer/ppermute | solution.py:1052
  166.9 3.3 %collective-permute-done.31.refs_4_ = bf16[80,128]{1,0:T(8,128)(2,1)S(1)} collective-permute-done((bf16[80,128]{1,0:T(8,128)(2,1)}, bf16[80,128]{1,0:T(8,128)(2,1)S(1)}, u32[]{:S(2)}, u32[]{:S(2)}) %collective-permute-start.31) | collective-permute-done | bytes 20512 | tf_op jit(solution)/shard_map/table_outer/ppermute | solution.py:1052
  171.4 2.8 %shard_sums.1 = (f32[6,96,192]{2,1,0:T(8,128)}, f32[64,128]{1,0:T(8,128)}, f32[32,8,128]{2,1,0:T(8,128)}) custom-call(bf16[8,3,96,384]{3,2,1,0:T(8,128)(2,1)} %copy-done.19, bf16[80,128]{1,0:T(8,128)(2,1)} %get-tuple-element.189.refs_1_, bf16[80,128]{1,0:T(8,128)(2,1)} %copy-done.44, bf16[80,128]{1,0:T(8,128)(2,1)} %copy-done.45, bf16[80,128]{1,0:T(8,128)(2,1)} %copy-done.46), custom_call_target="tpu_custom_call" | custom-call | flops 4000000000 | bytes 1048576 | tf_op jit(solution)/shard_map/shard_sums/pallas_call | solution.py:127
  174.3 2.7 %all-to-all-start.3 = ((f32[32,8,128]{2,1,0:T(8,128)}), f32[32,8,128]{2,1,0:T(8,128)S(1)}, u32[]{:S(2)}, u32[]{:S(2)}) async-start(f32[32,8,128]{2,1,0:T(8,128)} %get-tuple-element.193), calls=%async_computation.3 | async-start | bytes 262144 | tf_op jit(solution)/shard_map/squares/all_to_all | solution.py:753
  178.4 6.9 %all-to-all-done.3.refs_1_ = f32[32,8,128]{2,1,0:T(8,128)S(1)} async-done(((f32[32,8,128]{2,1,0:T(8,128)}), f32[32,8,128]{2,1,0:T(8,128)S(1)}, u32[]{:S(2)}, u32[]{:S(2)}) %all-to-all-start.3) | async-done | bytes 131104 | tf_op jit(solution)/shard_map/squares/all_to_all | solution.py:753
  186.2 2.8 %update.1 = (f32[4,96,192]{2,1,0:T(8,128)}, f32[4,96,192]{2,1,0:T(8,128)}, f32[4,96,192]{2,1,0:T(8,128)}, f32[192,96]{1,0:T(8,128)}, f32[192,96]{1,0:T(8,128)}, ...) custom-call(s32[2]{0:T(128)S(1)} %copy-done.16, ...), custom_call_target="tpu_custom_call" | custom-call | flops 3000000000 | bytes 1048576 | tf_op jit(solution)/shard_map/update/pallas_call | solution.py:127
  (177 shorter events, 40.3 us)
Async XLA Ops:
  3.8 16.5 %collective-permute-start.5 = (bf16[3,96,192]{2,1,0:T(8,128)(2,1)S(1)}, bf16[3,96,192]{2,1,0:T(8,128)(2,1)S(1)}, u32[]{:S(2)}, u32[]{:S(2)}) collective-permute-start(bf16[3,96,192]{2,1,0:T(8,128)(2,1)S(1)} %pad_maximum_fusion.3), channel_id=1, source_target_pairs={{0,24},{4,28},{8,16},{12,20},{16,8},{20,12},{24,0},{28,4},{1,25},{... | collective-permute-start | bytes 331784 | tf_op jit(solution)/shard_map/rest_far/ppermute | solution.py:822
  8.9 13.9 %collective-permute-start.4 = (bf16[3,96,192]{2,1,0:T(8,128)(2,1)S(1)}, bf16[3,96,192]{2,1,0:T(8,128)(2,1)S(1)}, u32[]{:S(2)}, u32[]{:S(2)}) collective-permute-start(bf16[3,96,192]{2,1,0:T(8,128)(2,1)S(1)} %pad_maximum_fusion.3), channel_id=1, source_target_pairs={{0,16},{4,20},{8,24},{12,28},{16,0},{20,4},{24,8},{28,12},{1,17},{... | collective-permute-start | bytes 331784 | tf_op jit(solution)/shard_map/rest_far/ppermute | solution.py:822
  8.9 13.9 %collective-permute-start.3 = (bf16[3,96,192]{2,1,0:T(8,128)(2,1)S(1)}, bf16[3,96,192]{2,1,0:T(8,128)(2,1)S(1)}, u32[]{:S(2)}, u32[]{:S(2)}) collective-permute-start(bf16[3,96,192]{2,1,0:T(8,128)(2,1)S(1)} %pad_maximum_fusion.3), channel_id=1, source_target_pairs={{0,8},{4,12},{8,0},{12,4},{16,24},{20,28},{24,16},{28,20},{1,9},{5... | collective-permute-start | bytes 331784 | tf_op jit(solution)/shard_map/rest_far/ppermute | solution.py:822
  9.7 8.9 %collective-permute-start.1 = (f32[9,96]{1,0:T(8,128)S(1)}, f32[9,96]{1,0:T(8,128)S(1)}, u32[]{:S(2)}, u32[]{:S(2)}) collective-permute-start(f32[9,96]{1,0:T(8,128)S(1)} %dynamic_update_slice.5), channel_id=1, source_target_pairs={{0,2},{1,3},{2,0},{3,1},{4,6},{5,7},{6,4},{7,5},{8,10},{9,11},{10,... | collective-permute-start | bytes 10376 | tf_op jit(solution)/shard_map/vectors_head/ppermute | solution.py:829
  12.1 16.8 %all-to-all-start = ((bf16[8,8,8,128]{3,2,1,0:T(8,128)(2,1)}), bf16[8,8,8,128]{3,2,1,0:T(8,128)(2,1)S(1)}, u32[]{:S(2)}, u32[]{:S(2)}) async-start(bf16[8,8,8,128]{3,2,1,0:T(8,128)(2,1)} %broadcast_in_dim.4), calls=%async_computation | async-start | bytes 262144 | tf_op jit(solution)/shard_map/table_all/all_to_all | solution.py:753
  18.0 22.5 %collective-permute-start = (bf16[2,128,768]{2,1,0:T(8,128)(2,1)S(1)}, bf16[2,128,768]{2,1,0:T(8,128)(2,1)}, u32[]{:S(2)}, u32[]{:S(2)}) collective-permute-start(bf16[2,128,768]{2,1,0:T(8,128)(2,1)S(1)} %pad_maximum_fusion.2.refs_0_), channel_id=1, source_target_pairs={{0,2},{1,3},{2,0},{3,1},{4,6},{5,7},{6,4},{7,5},{8,10},{9,11},{10,... | collective-permute-start | bytes 1179656 | tf_op jit(solution)/shard_map/rows_far/ppermute | solution.py:829
  22.8 17.6 %collective-permute-start.9 = (bf16[336,192]{1,0:T(8,128)(2,1)S(1)}, bf16[336,192]{1,0:T(8,128)(2,1)S(1)}, u32[]{:S(2)}, u32[]{:S(2)}) collective-permute-start(bf16[336,192]{1,0:T(8,128)(2,1)S(1)} %fusion.6), channel_id=1, source_target_pairs={{0,24},{4,28},{8,16},{12,20},{16,8},{20,12},{24,0},{28,4},{1,25},{... | collective-permute-start | bytes 387080 | tf_op jit(solution)/shard_map/qkv_far/ppermute | solution.py:822
  26.0 14.5 %collective-permute-start.8 = (bf16[336,192]{1,0:T(8,128)(2,1)S(1)}, bf16[336,192]{1,0:T(8,128)(2,1)S(1)}, u32[]{:S(2)}, u32[]{:S(2)}) collective-permute-start(bf16[336,192]{1,0:T(8,128)(2,1)S(1)} %fusion.6), channel_id=1, source_target_pairs={{0,16},{4,20},{8,24},{12,28},{16,0},{20,4},{24,8},{28,12},{1,17},{... | collective-permute-start | bytes 387080 | tf_op jit(solution)/shard_map/qkv_far/ppermute | solution.py:822
  26.0 14.5 %collective-permute-start.7 = (bf16[336,192]{1,0:T(8,128)(2,1)S(1)}, bf16[336,192]{1,0:T(8,128)(2,1)S(1)}, u32[]{:S(2)}, u32[]{:S(2)}) collective-permute-start(bf16[336,192]{1,0:T(8,128)(2,1)S(1)} %fusion.6), channel_id=1, source_target_pairs={{0,8},{4,12},{8,0},{12,4},{16,24},{20,28},{24,16},{28,20},{1,9},{5... | collective-permute-start | bytes 387080 | tf_op jit(solution)/shard_map/qkv_far/ppermute | solution.py:822
  27.4 13.2 %collective-permute-start.6 = (bf16[4,3,96,192]{3,2,1,0:T(8,128)(2,1)S(1)}, bf16[4,3,96,192]{3,2,1,0:T(8,128)(2,1)S(1)}, u32[]{:S(2)}, u32[]{:S(2)}) collective-permute-start(bf16[4,3,96,192]{3,2,1,0:T(8,128)(2,1)S(1)} %pad_maximum_fusion.1), channel_id=1, source_target_pairs={{0,4},{4,0},{8,12},{12,8},{16,20},{20,16},{24,28},{28,24},{1,5},{5... | collective-permute-start | bytes 1327112 | tf_op jit(solution)/shard_map/rest_near/ppermute | solution.py:826
  40.4 20.1 %collective-permute-start.11 = (bf16[2,128,768]{2,1,0:T(8,128)(2,1)S(1)}, bf16[2,128,768]{2,1,0:T(8,128)(2,1)}, u32[]{:S(2)}, u32[]{:S(2)}) collective-permute-start(bf16[2,128,768]{2,1,0:T(8,128)(2,1)S(1)} %pad_maximum_fusion.2.refs_0_), channel_id=1, source_target_pairs={{0,1},{1,0},{2,3},{3,2},{4,5},{5,4},{6,7},{7,6},{8,9},{9,8},{10,11... | collective-permute-start | bytes 1179656 | tf_op jit(solution)/shard_map/rows_near/ppermute | solution.py:829
  41.4 28.6 %collective-permute-start.14 = (bf16[8,3,96,192]{3,2,1,0:T(8,128)(2,1)S(1)}, bf16[8,3,96,192]{3,2,1,0:T(8,128)(2,1)}, u32[]{:S(2)}, u32[]{:S(2)}) collective-permute-start(bf16[8,3,96,192]{3,2,1,0:T(8,128)(2,1)S(1)} %constant_dynamic-update-slice_fusion.refs_9_), channel_id=1, source_target_pairs={{0,2},{1,3},{2,0},{3,1},{4,6},{5,7},{6,4},{7,5},{8,10},{9,11},{10,... | collective-permute-start | bytes 2654216 | tf_op jit(solution)/shard_map/rest_far_head/ppermute | solution.py:829
  43.2 26.7 %collective-permute-start.13 = (bf16[8,3,96,192]{3,2,1,0:T(8,128)(2,1)S(1)}, bf16[8,3,96,192]{3,2,1,0:T(8,128)(2,1)}, u32[]{:S(2)}, u32[]{:S(2)}) collective-permute-start(bf16[8,3,96,192]{3,2,1,0:T(8,128)(2,1)S(1)} %constant_dynamic-update-slice_fusion.refs_9_), channel_id=1, source_target_pairs={{0,1},{1,0},{2,3},{3,2},{4,5},{5,4},{6,7},{7,6},{8,9},{9,8},{10,11... | collective-permute-start | bytes 2654216 | tf_op jit(solution)/shard_map/rest_near_head/ppermute | solution.py:829
  43.4 17.1 %collective-permute-start.12 = (bf16[2,128,768]{2,1,0:T(8,128)(2,1)}, bf16[2,128,768]{2,1,0:T(8,128)(2,1)}, u32[]{:S(2)}, u32[]{:S(2)}) collective-permute-start(bf16[2,128,768]{2,1,0:T(8,128)(2,1)} %collective-permute-done.refs_2_), channel_id=1, source_target_pairs={{0,1},{1,0},{2,3},{3,2},{4,5},{5,4},{6,7},{7,6},{8,9},{9,8},{10,11... | collective-permute-start | bytes 1179656 | tf_op jit(solution)/shard_map/rows_near/ppermute | solution.py:829
  45.3 15.5 %collective-permute-start.10 = (bf16[4,336,192]{1,2,0:T(8,128)(2,1)S(1)}, bf16[4,336,192]{1,2,0:T(8,128)(2,1)S(1)}, u32[]{:S(2)}, u32[]{:S(2)}) collective-permute-start(bf16[4,336,192]{1,2,0:T(8,128)(2,1)S(1)} %copy.49), channel_id=1, source_target_pairs={{0,4},{4,0},{8,12},{12,8},{16,20},{20,16},{24,28},{28,24},{1,5},{5... | collective-permute-start | bytes 1548296 | tf_op jit(solution)/shard_map/qkv_near/ppermute | solution.py:826
  69.9 6.4 %collective-permute-start.18 = (bf16[8,3,96,192]{3,2,1,0:T(8,128)(2,1)}, bf16[8,3,96,192]{3,2,1,0:T(8,128)(2,1)S(1)}, u32[]{:S(2)}, u32[]{:S(2)}) collective-permute-start(bf16[8,3,96,192]{3,2,1,0:T(8,128)(2,1)} %collective-permute-done.14.refs_11_), channel_id=1, source_target_pairs={{0,1},{1,0},{2,3},{3,2},{4,5},{5,4},{6,7},{7,6},{8,9},{9,8},{10,11... | collective-permute-start | bytes 2654216 | tf_op jit(solution)/shard_map/rest_near_head/ppermute | solution.py:829
  86.9 16.2 %collective-permute-start.23 = (bf16[2,128,768]{2,1,0:T(8,128)(2,1)}, bf16[2,128,768]{2,1,0:T(8,128)(2,1)S(1)}, u32[]{:S(2)}, u32[]{:S(2)}) collective-permute-start(bf16[2,128,768]{2,1,0:T(8,128)(2,1)} %get-tuple-element.160.refs_12_), channel_id=1, source_target_pairs={{0,2},{1,3},{2,0},{3,1},{4,6},{5,7},{6,4},{7,5},{8,10},{9,11},{10,... | collective-permute-start | bytes 1179656 | tf_op jit(solution)/shard_map/normed_grad/ppermute | solution.py:972
  87.3 15.8 %collective-permute-start.22 = (bf16[2,128,768]{2,1,0:T(8,128)(2,1)}, bf16[2,128,768]{2,1,0:T(8,128)(2,1)S(1)}, u32[]{:S(2)}, u32[]{:S(2)}) collective-permute-start(bf16[2,128,768]{2,1,0:T(8,128)(2,1)} %get-tuple-element.160.refs_12_), channel_id=1, source_target_pairs={{0,1},{1,0},{2,3},{3,2},{4,5},{5,4},{6,7},{7,6},{8,9},{9,8},{10,11... | collective-permute-start | bytes 1179656 | tf_op jit(solution)/shard_map/normed_grad/ppermute | solution.py:972
  87.7 15.5 %all-to-all-start.1 = ((bf16[4,128,384]{2,1,0:T(8,128)(2,1)}), bf16[4,128,384]{2,1,0:T(8,128)(2,1)S(1)}, u32[]{:S(2)}, u32[]{:S(2)}) async-start(bf16[4,128,384]{2,1,0:T(8,128)(2,1)} %get-tuple-element.159), calls=%async_computation.1 | async-start | bytes 786432 | tf_op jit(solution)/shard_map/act_pre/all_to_all | solution.py:753
  103.2 12.7 %collective-permute-start.25 = (bf16[128,768]{1,0:T(8,128)(2,1)}, bf16[128,768]{1,0:T(8,128)(2,1)S(1)}, u32[]{:S(2)}, u32[]{:S(2)}) collective-permute-start(bf16[128,768]{1,0:T(8,128)(2,1)} %get-tuple-element.167), channel_id=1, source_target_pairs={{0,1},{1,0},{2,3},{3,2},{4,5},{5,4},{6,7},{7,6},{8,9},{9,8},{10,11... | collective-permute-start | bytes 589832 | tf_op jit(solution)/shard_map/grad_normed_one/ppermute | solution.py:763
  103.7 12.2 %collective-permute-start.26 = (bf16[128,768]{1,0:T(8,128)(2,1)}, bf16[128,768]{1,0:T(8,128)(2,1)S(1)}, u32[]{:S(2)}, u32[]{:S(2)}) collective-permute-start(bf16[128,768]{1,0:T(8,128)(2,1)} %get-tuple-element.168), channel_id=1, source_target_pairs={{0,2},{1,3},{2,0},{3,1},{4,6},{5,7},{6,4},{7,5},{8,10},{9,11},{10,... | collective-permute-start | bytes 589832 | tf_op jit(solution)/shard_map/grad_normed_one/ppermute | solution.py:763
  104.7 11.3 %collective-permute-start.27 = (bf16[128,768]{1,0:T(8,128)(2,1)}, bf16[128,768]{1,0:T(8,128)(2,1)S(1)}, u32[]{:S(2)}, u32[]{:S(2)}) collective-permute-start(bf16[128,768]{1,0:T(8,128)(2,1)} %get-tuple-element.169), channel_id=1, source_target_pairs={{0,3},{1,2},{2,1},{3,0},{4,7},{5,6},{6,5},{7,4},{8,11},{9,10},{10,... | collective-permute-start | bytes 589832 | tf_op jit(solution)/shard_map/grad_normed_one/ppermute | solution.py:763
  111.7 58.5 %all-to-all-start.2 = ((bf16[8,3,96,384]{3,2,1,0:T(8,128)(2,1)}), bf16[8,3,96,384]{3,2,1,0:T(8,128)(2,1)S(1)}, u32[]{:S(2)}, u32[]{:S(2)}) async-start(bf16[8,3,96,384]{3,2,1,0:T(8,128)(2,1)} %weight_grads.1), calls=%async_computation.2 | async-start | bytes 3538944 | tf_op jit(solution)/shard_map/weight_grads/all_to_all | solution.py:753
  174.3 11.0 %all-to-all-start.3 = ((f32[32,8,128]{2,1,0:T(8,128)}), f32[32,8,128]{2,1,0:T(8,128)S(1)}, u32[]{:S(2)}, u32[]{:S(2)}) async-start(f32[32,8,128]{2,1,0:T(8,128)} %get-tuple-element.193), calls=%async_computation.3 | async-start | bytes 262144 | tf_op jit(solution)/shard_map/squares/all_to_all | solution.py:753
  (59 other events, 367.2 us)
